TPU v7x, 256 devices: a whole 4x4x8 slice. The times are simulated.
256 devices in a mesh: lon: 16 (over y_hi, z), lat: 16 (over y_lo, x, core).
Axes of the slice: x: 4, y: 4 (y_hi: 2, y_lo: 2; y = y_hi * 2 + y_lo), z: 8, core: 2. Of those that a mesh axis runs over, the one named last changes fastest.
Arguments:
- ocean_state: bfloat16 [200, 128, 2048], P(None, 'lat', 'lon'), may hold values from -6 to 6
- land_sea: int32 [128, 2048], P('lat', 'lon'), may hold values 0 or 1
- depth_kernel: bfloat16 [49, 200], replicated, may hold values from -0.875 to 0.875
- norm_gain: float32 [200], replicated, may hold values from 0.1 to 1.9
- w_expand: bfloat16 [800, 200], replicated, may hold values from -0.4375 to 0.4375
- b_expand: float32 [800], replicated, may hold values from -3 to 3
- w_project: bfloat16 [800, 200], replicated, may hold values from -0.21875 to 0.21875
- cotangent: bfloat16 [200, 128, 2048], P(None, 'lat', 'lon'), may hold values from -6 to 6
Outputs:
- next_state: bfloat16 [200, 128, 2048], P(None, 'lat', 'lon')
- grad_state: bfloat16 [200, 128, 2048], P(None, 'lat', 'lon')
- grad_kernel: float32 [49, 200], replicated
- grad_gain: float32 [200], replicated
- grad_expand: float32 [800, 200], P('lon')
- grad_project: float32 [800, 200], P('lon')
- grad_bias: float32 [800], P('lon')
All inputs are finite; a program needn't handle non-finite values. No bound on the sum of `land_sea` on one device may be relied on, other than what follows from the above.
Results may differ from a plain program's by a relative error of at most 0.014.
Values may be sent and summed in bfloat16 or wider, within the bound.
No kernel may reach another device: no remote copies, remote signals or barrier semaphores. Data moves between devices by JAX's collectives and lax.ppermute only.
A program may use at most 64 MiB of HBM per device.

v0:
```python
import jax
import jax.numpy as jnp
from jax import lax
from jax.sharding import PartitionSpec as P

EPS = 1e-06


def with_halo(value, sides, width, wrap):
    for axis, dim in sides:
        size, length = (lax.axis_size(axis), value.shape[dim])
        up = [(i, (i + 1) % size) for i in range(size if wrap else size - 1)]
        down = [(j, i) for i, j in up]
        last = lax.slice_in_dim(value, length - width, length, axis=dim)
        initial = lax.slice_in_dim(value, 0, width, axis=dim)
        before = lax.ppermute(last, axis, up)
        after = lax.ppermute(initial, axis, down)
        value = jnp.concatenate([before, value, after], axis=dim)
    return value


def gelu_pair(inner):
    normal_cdf = 0.5 * (1.0 + lax.erf(inner * 0.7071067811865476))
    density = jnp.exp(-0.5 * inner * inner) * 0.3989422804014327
    return (inner * normal_cdf, normal_cdf + inner * density)


def extend(field):
    wide = with_halo(field, (("lon", 2),), 3, True)
    return with_halo(wide, (("lat", 1),), 3, False)


def depthwise(padded, kernel, row_count, col_count, flipped):
    total = jnp.zeros((padded.shape[0], row_count, col_count), jnp.float32)
    for row_tap in range(7):
        for col_tap in range(7):
            weight = kernel[row_tap * 7 + col_tap].astype(jnp.float32)[:, None, None]
            row_start = 6 - row_tap if flipped else row_tap
            col_start = 6 - col_tap if flipped else col_tap
            window = padded[:, row_start : row_start + row_count, col_start : col_start + col_count]
            total = total + weight * window.astype(jnp.float32)
    return total


def kernel_grad(padded, upstream, row_count, col_count):
    rows_out = []
    for row_tap in range(7):
        for col_tap in range(7):
            window = padded[:, row_tap : row_tap + row_count, col_tap : col_tap + col_count]
            rows_out.append(jnp.sum(upstream * window.astype(jnp.float32), axis=(1, 2)))
    return jnp.stack(rows_out, axis=0)


def cell_part(
    state_cells, mixed_cells, mask_cells, cot_cells, norm_gain, w_expand, b_expand, w_project
):
    center = jnp.mean(mixed_cells, axis=0, keepdims=True)
    centered = mixed_cells - center
    inv_spread = lax.rsqrt(jnp.mean(centered * centered, axis=0, keepdims=True) + EPS)
    whitened = centered * inv_spread
    normed = (whitened * norm_gain[:, None]).astype(jnp.bfloat16)
    hidden_in = jnp.dot(w_expand, normed, preferred_element_type=jnp.float32) + b_expand[:, None]
    gelu_value, gelu_slope = gelu_pair(hidden_in)
    activ = gelu_value.astype(jnp.bfloat16)
    branch = lax.dot_general(
        w_project, activ, (((0,), (0,)), ((), ())), preferred_element_type=jnp.float32
    )
    mask_float = mask_cells.astype(jnp.float32)[None]
    next_cells = (mask_float * (state_cells.astype(jnp.float32) + branch)).astype(jnp.bfloat16)
    gated = (cot_cells.astype(jnp.float32) * mask_float).astype(jnp.bfloat16)
    back_act = jnp.dot(w_project, gated, preferred_element_type=jnp.float32)
    back_in = (back_act * gelu_slope).astype(jnp.bfloat16)
    bias_term = jnp.sum(back_in.astype(jnp.float32), axis=1)
    back_norm = lax.dot_general(
        w_expand, back_in, (((0,), (0,)), ((), ())), preferred_element_type=jnp.float32
    )
    gain_term = jnp.sum(back_norm * whitened, axis=1)
    scaled = back_norm * norm_gain[:, None]
    back_mixed = inv_spread * (
        scaled
        - jnp.mean(scaled, axis=0, keepdims=True)
        - whitened * jnp.mean(scaled * whitened, axis=0, keepdims=True)
    )
    return (
        next_cells,
        back_mixed.astype(jnp.bfloat16),
        activ,
        gated,
        back_in,
        normed,
        bias_term,
        gain_term,
    )


def shards(
    ocean_state, land_sea, depth_kernel, norm_gain, w_expand, b_expand, w_project, cotangent
):
    channels, row_count, col_count = ocean_state.shape
    cell_count = row_count * col_count
    hidden_units = w_expand.shape[0]
    masked = ocean_state * land_sea.astype(jnp.bfloat16)[None]
    padded = extend(masked)
    mixed_field = depthwise(padded, depth_kernel, row_count, col_count, False)
    outs = cell_part(
        ocean_state.reshape(channels, cell_count),
        mixed_field.reshape(channels, cell_count),
        land_sea.reshape(cell_count),
        cotangent.reshape(channels, cell_count),
        norm_gain,
        w_expand,
        b_expand,
        w_project,
    )
    next_cells, back_cells, activ, gated, back_in, normed, bias_term, gain_term = outs
    next_state = next_cells.reshape(channels, row_count, col_count)
    back_mixed = back_cells.reshape(channels, row_count, col_count)
    kernel_term = kernel_grad(padded, back_mixed.astype(jnp.float32), row_count, col_count)
    back_masked = depthwise(extend(back_mixed), depth_kernel, row_count, col_count, True)
    mask_float = land_sea.astype(jnp.float32)[None]
    grad_state = (mask_float * (cotangent.astype(jnp.float32) + back_masked)).astype(jnp.bfloat16)
    share = hidden_units // lax.axis_size("lon")
    first_row = lax.axis_index("lon") * share
    proj_term = lax.dot_general(
        activ, gated, (((1,), (1,)), ((), ())), preferred_element_type=jnp.float32
    )
    expand_term = lax.dot_general(
        back_in, normed, (((1,), (1,)), ((), ())), preferred_element_type=jnp.float32
    )
    expand_all, project_all, bias_all, grad_gain, grad_kernel = lax.psum(
        (expand_term, proj_term, bias_term, gain_term, kernel_term), ("lon", "lat")
    )
    grad_expand = lax.dynamic_slice_in_dim(expand_all, first_row, share, 0)
    grad_project = lax.dynamic_slice_in_dim(project_all, first_row, share, 0)
    grad_bias = lax.dynamic_slice_in_dim(bias_all, first_row, share, 0)
    return (next_state, grad_state, grad_kernel, grad_gain, grad_expand, grad_project, grad_bias)


def solution(mesh):
    placed = (
        P(None, "lat", "lon"),
        P("lat", "lon"),
        P(),
        P(),
        P(),
        P(),
        P(),
        P(None, "lat", "lon"),
    )
    return jax.shard_map(
        shards,
        mesh=mesh,
        in_specs=placed,
        out_specs=(
            P(None, "lat", "lon"),
            P(None, "lat", "lon"),
            P(),
            P(),
            P("lon", None),
            P("lon", None),
            P("lon"),
        ),
        check_vma=False,
    )
```

profile of v0, /device:TPU:1, one launch (start us, length us, event | category | flops | bytes accessed | tf_op | source)
XLA Modules:
  0.0 334.8 jit_solution(4527853498532908957)
XLA Ops:
  8.0 1.3 copy.15
  9.5 2.5 collective-permute-start
  12.1 6.7 %collective-permute-start.1 = (bf16[200,8,3]{0,2,1:T(4,128)(2,1)S(1)}, bf16[200,8,3]{0,2,1:T(4,128)(2,1)S(1)}, u32[]{:S(2)}, u32[]{:S(2)}) collective-permute-start(bf16[200,8,3]{0,2,1:T(4,128)(2,1)S(1)} %get-tuple-element.90), channel_id=1, source_target_pairs={{16,0},{32,16},{48,32},{64,48},{80,64},{96,80},{112,96},{128,112},... | collective-permute-start | bytes 28808 | tf_op jit(solution)/shard_map/ppermute | solution.py:17
  19.4 1.1 copy.27
  20.5 1.0 convert.51
  21.6 4.0 %collective-permute-start.2 = (bf16[200,3,134]{0,2,1:T(8,128)(2,1)S(1)}, bf16[200,3,134]{0,2,1:T(8,128)(2,1)S(1)}, u32[]{:S(2)}, u32[]{:S(2)}) collective-permute-start(bf16[200,3,134]{0,2,1:T(8,128)(2,1)S(1)} %get-tuple-element.85), channel_id=1, source_target_pairs={{0,1},{1,2},{2,3},{3,4},{4,5},{5,6},{6,7},{7,8},{8,9},{9,10},{10,1... | collective-permute-start | bytes 482408 | tf_op jit(solution)/shard_map/ppermute | solution.py:16
  25.5 2.1 collective-permute-start.3
  28.3 4.4 %collective-permute-done.3 = bf16[200,3,134]{0,2,1:T(8,128)(2,1)S(1)} collective-permute-done((bf16[200,3,134]{0,2,1:T(8,128)(2,1)S(1)}, bf16[200,3,134]{0,2,1:T(8,128)(2,1)S(1)}, u32[]{:S(2)}, u32[]{:S(2)}) %collective-permute-start.3) | collective-permute-done | bytes 160832 | tf_op jit(solution)/shard_map/ppermute | solution.py:17
  33.2 8.3 %fusion.148 = (f32[8,128]{1,0:T(8,128)S(1)}, f32[200,8,128]{0,2,1:T(8,128)S(1)}) fusion(bf16[200,11,134]{0,2,1:T(8,128)(2,1)S(1)} %get-tuple-element.84, f32[200]{0:T(256)S(1)} %bitcast.304, f32[200]{0:T(256)S(1)} %bitcast.306, f32[200]{0:T(256)S(1)} %bitcast.212, f32[200]{0:T(256)S(1)} %bitcast.214, f32[200]{0:T(256)S(1)} %bitcast.216, ...), kind=kLoop, calls=%fused_computation.341 | loop fusion | flops 33790976 | bytes 18494496 | tf_op jit(solution)/shard_map/reduce_sum | solution.py:57
  42.5 1.5 copy.26
  44.1 2.3 fusion.9
  46.4 2.2 convert_reduce_fusion
  48.7 1.6 fusion.146
  50.3 1.3 multiply_reduce_fusion.1
  51.6 1.0 multiply_convert_fusion.1
  52.6 1.2 copy.28
  53.8 3.8 %fusion.135 = (f32[200]{0:T(256)S(1)}, f32[200]{0:T(256)S(1)}, f32[200]{0:T(256)S(1)}, f32[200]{0:T(256)S(1)}, f32[200]{0:T(256)S(1)}, /*index=5*/f32[200]{0:T(2...) fusion(bf16[200,11,134]{0,2,1:T(8,128)(2,1)S(1)} %get-tuple-ele, ...), kind=kLoop, calls=%fused_computation.240 | loop fusion | flops 11260400 | bytes 7796800 | tf_op jit(solution)/shard_map/reduce_sum | solution.py:50
  57.6 3.8 %fusion.107 = (f32[200]{0:T(256)}, f32[200]{0:T(256)}, f32[200]{0:T(256)}, f32[200]{0:T(256)}, f32[200]{0:T(256)}, /*index=5*/f32[200]{0:T(256)}, f32[200]{0:T(2...) fusion(bf16[200,11,134]{0,2,1:T(8,128)(2,1)S(1)} %get-tuple-ele, ...), kind=kLoop, calls=%fused_computation.212 | loop fusion | flops 11260400 | bytes 7796800 | tf_op jit(solution)/shard_map/reduce_sum | solution.py:50
  61.4 1.5 fusion.144
  63.0 5.1 %collective-permute-start.5 = (bf16[200,8,3]{0,2,1:T(4,128)(2,1)S(1)}, bf16[200,8,3]{0,2,1:T(4,128)(2,1)S(1)}, u32[]{:S(2)}, u32[]{:S(2)}) collective-permute-start(bf16[200,8,3]{0,2,1:T(4,128)(2,1)S(1)} %get-tuple-element.87), channel_id=1, source_target_pairs={{16,0},{32,16},{48,32},{64,48},{80,64},{96,80},{112,96},{128,112},... | collective-permute-start | bytes 28808 | tf_op jit(solution)/shard_map/ppermute | solution.py:17
  68.1 2.4 fusion.13
  71.3 1.5 fusion.114
  72.9 0.9 pad_maximum_fusion.8
  73.7 1.9 collective-permute-start.6
  75.7 3.6 %collective-permute-start.7 = (bf16[200,3,134]{0,2,1:T(8,128)(2,1)}, bf16[200,3,134]{0,2,1:T(8,128)(2,1)S(1)}, u32[]{:S(2)}, u32[]{:S(2)}) collective-permute-start(bf16[200,3,134]{0,2,1:T(8,128)(2,1)} %get-tuple-element.82), channel_id=1, source_target_pairs={{0,1},{1,2},{2,3},{3,4},{4,5},{5,6},{6,7},{7,8},{8,9},{9,10},{10,1... | collective-permute-start | bytes 482408 | tf_op jit(solution)/shard_map/ppermute | solution.py:16
  79.3 0.9 fusion.117
  80.2 3.6 %stack.199 = f32[49,200]{1,0:T(8,128)S(1)} concatenate(f32[1,200]{1,0:T(1,128)S(1)} %bitcast.318, f32[1,200]{1,0:T(1,128)S(1)} %bitcast.319, f32[1,200]{1,0:T(1,128)S(1)} %bitcast.320, f32[1,200]{1,0:T(1,128)} %bitcast.356, f32[1,200]{1,0:T(1,128)} %bitcast.355, f32[1,200]{1,0:T(1,128)} %bitcast.354, f32[1,200]{1,0:T(1,128)} %bitcast.353, f32[1,200]{1,0:T(1,128)} %bitcast.352, ...), dimensions={0} | concatenate | bytes 78400 | tf_op jit(solution)/shard_map/stack | solution.py:51
  83.9 77.7 %all-reduce = (f32[49,200]{1,0:T(8,128)}, f32[200]{0:T(256)}, f32[800]{0:T(1024)S(1)}) all-reduce(f32[49,200]{1,0:T(8,128)S(1)} %stack.199, f32[200]{0:T(256)} %get-tuple-element.14, f32[800]{0:T(1024)S(1)} %get-tuple-element.148), channel_id=1, replica_groups=mesh['lon'=16,'lat'=16] {'lon','lat'}, use_global_device_ids=true, to_apply=%region_53.0 | all-reduce | flops 10800 | bytes 86400 | tf_op jit(solution)/shard_map/psum | solution.py:130
  162.5 8.5 %multiply_convert_fusion = bf16[200,8,128]{0,2,1:T(8,128)(2,1)S(1)} fusion(bf16[200,8,128]{0,2,1:T(8,128)(2,1)S(1)} %bitcast.205, bf16[200,8,3]{0,2,1:T(4,128)(2,1)S(1)} %collective-permute-done.4, bf16[200,8,3]{0,2,1:T(4,128)(2,1)S(1)} %collective-permute-done.5, bf16[200,11,134]{0,2,1:T(8,128)(2,1)S(1)} %get-tuple-element.80, ...), kind=kLoop, calls=%fused_computation.241 | loop fusion | flops 34406400 | bytes 18494496 | tf_op jit(solution)/shard_map/convert_element_type | solution.py:121
  171.0 1.0 copy.25
  172.0 154.5 %all-reduce.4.cloned.1.call-done = (f32[800,200]{1,0:T(8,128)}, f32[800,200]{1,0:T(8,128)}) async-done(((f32[800,200]{1,0:T(8,128)}, f32[800,200]{1,0:T(8,128)}), (f32[800,200]{1,0:T(8,128)}, f32[800,200]{1,0:T(8,128)})) %all-reduce.4.cloned.1.call-update) | async-done | bytes 1280016 | tf_op jit(solution)/shard_map/psum | solution.py:130
  326.5 1.5 constant_dynamic-slice_fusion
  (125 shorter events, 5.2 us)
Async XLA Ops:
  7.2 36.9 %copy-start = (bf16[800,200]{0,1:T(8,128)(2,1)S(1)}, bf16[800,200]{0,1:T(8,128)(2,1)}, u32[]{:S(2)}) copy-start(bf16[800,200]{0,1:T(8,128)(2,1)} %param.12) | copy-start | bytes 960004
  7.2 319.2 %all-reduce.4.cloned.1.call-start = ((), (), s32[]{:S(2)}) async-start(), calls=%async_computation | async-start | bytes 3276800 | tf_op jit(solution)/shard_map/psum | solution.py:130
  9.5 11.9 %collective-permute-start = (bf16[200,8,3]{0,2,1:T(4,128)(2,1)S(1)}, bf16[200,8,3]{0,2,1:T(4,128)(2,1)S(1)}, u32[]{:S(2)}, u32[]{:S(2)}) collective-permute-start(bf16[200,8,3]{0,2,1:T(4,128)(2,1)S(1)} %get-tuple-element.89), channel_id=1, source_target_pairs={{0,16},{16,32},{32,48},{48,64},{64,80},{80,96},{96,112},{112,128},... | collective-permute-start | bytes 28808 | tf_op jit(solution)/shard_map/ppermute | solution.py:16
  12.1 9.3 %collective-permute-start.1 = (bf16[200,8,3]{0,2,1:T(4,128)(2,1)S(1)}, bf16[200,8,3]{0,2,1:T(4,128)(2,1)S(1)}, u32[]{:S(2)}, u32[]{:S(2)}) collective-permute-start(bf16[200,8,3]{0,2,1:T(4,128)(2,1)S(1)} %get-tuple-element.90), channel_id=1, source_target_pairs={{16,0},{32,16},{48,32},{64,48},{80,64},{96,80},{112,96},{128,112},... | collective-permute-start | bytes 28808 | tf_op jit(solution)/shard_map/ppermute | solution.py:17
  18.8 14.1 %copy-start.11 = (f32[1,200]{1,0:T(1,128)}, f32[1,200]{1,0:T(1,128)S(1)}, u32[]{:S(2)}) copy-start(f32[1,200]{1,0:T(1,128)S(1)} %get-tuple-element.104) | copy-start | bytes 2404
  18.8 14.1 %copy-start.12 = (f32[1,200]{1,0:T(1,128)}, f32[1,200]{1,0:T(1,128)S(1)}, u32[]{:S(2)}) copy-start(f32[1,200]{1,0:T(1,128)S(1)} %get-tuple-element.105) | copy-start | bytes 2404
  18.8 14.1 %copy-start.13 = (f32[1,200]{1,0:T(1,128)}, f32[1,200]{1,0:T(1,128)S(1)}, u32[]{:S(2)}) copy-start(f32[1,200]{1,0:T(1,128)S(1)} %get-tuple-element.106) | copy-start | bytes 2404
  18.8 14.1 %copy-start.14 = (f32[1,200]{1,0:T(1,128)}, f32[1,200]{1,0:T(1,128)S(1)}, u32[]{:S(2)}) copy-start(f32[1,200]{1,0:T(1,128)S(1)} %get-tuple-element.107) | copy-start | bytes 2404
  18.8 14.1 %copy-start.15 = (f32[1,200]{1,0:T(1,128)}, f32[1,200]{1,0:T(1,128)S(1)}, u32[]{:S(2)}) copy-start(f32[1,200]{1,0:T(1,128)S(1)} %get-tuple-element.108) | copy-start | bytes 2404
  18.8 14.1 %copy-start.16 = (f32[1,200]{1,0:T(1,128)}, f32[1,200]{1,0:T(1,128)S(1)}, u32[]{:S(2)}) copy-start(f32[1,200]{1,0:T(1,128)S(1)} %get-tuple-element.109) | copy-start | bytes 2404
  18.9 14.1 %copy-start.17 = (f32[1,200]{1,0:T(1,128)}, f32[1,200]{1,0:T(1,128)S(1)}, u32[]{:S(2)}) copy-start(f32[1,200]{1,0:T(1,128)S(1)} %get-tuple-element.110) | copy-start | bytes 2404
  18.9 14.1 %copy-start.18 = (f32[1,200]{1,0:T(1,128)}, f32[1,200]{1,0:T(1,128)S(1)}, u32[]{:S(2)}) copy-start(f32[1,200]{1,0:T(1,128)S(1)} %get-tuple-element.111) | copy-start | bytes 2404
  18.9 14.1 %copy-start.19 = (f32[1,200]{1,0:T(1,128)}, f32[1,200]{1,0:T(1,128)S(1)}, u32[]{:S(2)}) copy-start(f32[1,200]{1,0:T(1,128)S(1)} %get-tuple-element.112) | copy-start | bytes 2404
  18.9 14.1 %copy-start.20 = (f32[1,200]{1,0:T(1,128)}, f32[1,200]{1,0:T(1,128)S(1)}, u32[]{:S(2)}) copy-start(f32[1,200]{1,0:T(1,128)S(1)} %get-tuple-element.113) | copy-start | bytes 2404
  18.9 14.1 %copy-start.21 = (f32[1,200]{1,0:T(1,128)}, f32[1,200]{1,0:T(1,128)S(1)}, u32[]{:S(2)}) copy-start(f32[1,200]{1,0:T(1,128)S(1)} %get-tuple-element.114) | copy-start | bytes 2404
  18.9 14.1 %copy-start.22 = (f32[1,200]{1,0:T(1,128)}, f32[1,200]{1,0:T(1,128)S(1)}, u32[]{:S(2)}) copy-start(f32[1,200]{1,0:T(1,128)S(1)} %get-tuple-element.115) | copy-start | bytes 2404
  18.9 14.1 %copy-start.23 = (f32[1,200]{1,0:T(1,128)}, f32[1,200]{1,0:T(1,128)S(1)}, u32[]{:S(2)}) copy-start(f32[1,200]{1,0:T(1,128)S(1)} %get-tuple-element.116) | copy-start | bytes 2404
  18.9 14.1 %copy-start.24 = (f32[1,200]{1,0:T(1,128)}, f32[1,200]{1,0:T(1,128)S(1)}, u32[]{:S(2)}) copy-start(f32[1,200]{1,0:T(1,128)S(1)} %get-tuple-element.117) | copy-start | bytes 2404
  18.9 14.1 %copy-start.25 = (f32[1,200]{1,0:T(1,128)}, f32[1,200]{1,0:T(1,128)S(1)}, u32[]{:S(2)}) copy-start(f32[1,200]{1,0:T(1,128)S(1)} %get-tuple-element.118) | copy-start | bytes 2404
  18.9 14.1 %copy-start.26 = (f32[1,200]{1,0:T(1,128)}, f32[1,200]{1,0:T(1,128)S(1)}, u32[]{:S(2)}) copy-start(f32[1,200]{1,0:T(1,128)S(1)} %get-tuple-element.119) | copy-start | bytes 2404
  19.0 14.1 %copy-start.27 = (f32[1,200]{1,0:T(1,128)}, f32[1,200]{1,0:T(1,128)S(1)}, u32[]{:S(2)}) copy-start(f32[1,200]{1,0:T(1,128)S(1)} %get-tuple-element.120) | copy-start | bytes 2404
  19.0 14.1 %copy-start.28 = (f32[1,200]{1,0:T(1,128)}, f32[1,200]{1,0:T(1,128)S(1)}, u32[]{:S(2)}) copy-start(f32[1,200]{1,0:T(1,128)S(1)} %get-tuple-element.121) | copy-start | bytes 2404
  19.0 14.1 %copy-start.29 = (f32[1,200]{1,0:T(1,128)}, f32[1,200]{1,0:T(1,128)S(1)}, u32[]{:S(2)}) copy-start(f32[1,200]{1,0:T(1,128)S(1)} %get-tuple-element.122) | copy-start | bytes 2404
  19.0 14.1 %copy-start.30 = (f32[1,200]{1,0:T(1,128)}, f32[1,200]{1,0:T(1,128)S(1)}, u32[]{:S(2)}) copy-start(f32[1,200]{1,0:T(1,128)S(1)} %get-tuple-element.123) | copy-start | bytes 2404
  19.0 14.1 %copy-start.31 = (f32[1,200]{1,0:T(1,128)}, f32[1,200]{1,0:T(1,128)S(1)}, u32[]{:S(2)}) copy-start(f32[1,200]{1,0:T(1,128)S(1)} %get-tuple-element.124) | copy-start | bytes 2404
  21.6 6.7 %collective-permute-start.2 = (bf16[200,3,134]{0,2,1:T(8,128)(2,1)S(1)}, bf16[200,3,134]{0,2,1:T(8,128)(2,1)S(1)}, u32[]{:S(2)}, u32[]{:S(2)}) collective-permute-start(bf16[200,3,134]{0,2,1:T(8,128)(2,1)S(1)} %get-tuple-element.85), channel_id=1, source_target_pairs={{0,1},{1,2},{2,3},{3,4},{4,5},{5,6},{6,7},{7,8},{8,9},{9,10},{10,1... | collective-permute-start | bytes 482408 | tf_op jit(solution)/shard_map/ppermute | solution.py:16
  25.5 7.1 %collective-permute-start.3 = (bf16[200,3,134]{0,2,1:T(8,128)(2,1)S(1)}, bf16[200,3,134]{0,2,1:T(8,128)(2,1)S(1)}, u32[]{:S(2)}, u32[]{:S(2)}) collective-permute-start(bf16[200,3,134]{0,2,1:T(8,128)(2,1)S(1)} %get-tuple-element.86), channel_id=1, source_target_pairs={{1,0},{2,1},{3,2},{4,3},{5,4},{6,5},{7,6},{8,7},{9,8},{10,9},{11,1... | collective-permute-start | bytes 482408 | tf_op jit(solution)/shard_map/ppermute | solution.py:17
  62.9 9.9 %collective-permute-start.4 = (bf16[200,8,3]{0,2,1:T(4,128)(2,1)S(1)}, bf16[200,8,3]{0,2,1:T(4,128)(2,1)S(1)}, u32[]{:S(2)}, u32[]{:S(2)}) collective-permute-start(bf16[200,8,3]{0,2,1:T(4,128)(2,1)S(1)} %get-tuple-element.88), channel_id=1, source_target_pairs={{0,16},{16,32},{32,48},{48,64},{64,80},{80,96},{96,112},{112,128},... | collective-permute-start | bytes 28808 | tf_op jit(solution)/shard_map/ppermute | solution.py:16
  63.0 9.8 %collective-permute-start.5 = (bf16[200,8,3]{0,2,1:T(4,128)(2,1)S(1)}, bf16[200,8,3]{0,2,1:T(4,128)(2,1)S(1)}, u32[]{:S(2)}, u32[]{:S(2)}) collective-permute-start(bf16[200,8,3]{0,2,1:T(4,128)(2,1)S(1)} %get-tuple-element.87), channel_id=1, source_target_pairs={{16,0},{32,16},{48,32},{64,48},{80,64},{96,80},{112,96},{128,112},... | collective-permute-start | bytes 28808 | tf_op jit(solution)/shard_map/ppermute | solution.py:17
  73.7 88.4 %collective-permute-start.6 = (bf16[200,3,134]{0,2,1:T(8,128)(2,1)}, bf16[200,3,134]{0,2,1:T(8,128)(2,1)S(1)}, u32[]{:S(2)}, u32[]{:S(2)}) collective-permute-start(bf16[200,3,134]{0,2,1:T(8,128)(2,1)} %get-tuple-element.81), channel_id=1, source_target_pairs={{1,0},{2,1},{3,2},{4,3},{5,4},{6,5},{7,6},{8,7},{9,8},{10,9},{11,1... | collective-permute-start | bytes 482408 | tf_op jit(solution)/shard_map/ppermute | solution.py:17
  75.7 86.5 %collective-permute-start.7 = (bf16[200,3,134]{0,2,1:T(8,128)(2,1)}, bf16[200,3,134]{0,2,1:T(8,128)(2,1)S(1)}, u32[]{:S(2)}, u32[]{:S(2)}) collective-permute-start(bf16[200,3,134]{0,2,1:T(8,128)(2,1)} %get-tuple-element.82), channel_id=1, source_target_pairs={{0,1},{1,2},{2,3},{3,4},{4,5},{5,6},{6,7},{7,8},{8,9},{9,10},{10,1... | collective-permute-start | bytes 482408 | tf_op jit(solution)/shard_map/ppermute | solution.py:16
  80.2 82.2 %copy-start.4 = (bf16[200,8,128]{0,2,1:T(8,128)(2,1)S(1)}, bf16[200,8,128]{0,2,1:T(8,128)(2,1)}, u32[]{:S(2)}) copy-start(bf16[200,8,128]{0,2,1:T(8,128)(2,1)} %copy-done.3) | copy-start | bytes 1228804
  (26 other events, 262.8 us)
Sparse Core Ops, SparseCore 0:
  71.5 254.9 all-reduce.3
where the time goes:
time: 337 us; the launch traced here: 335 us
  waiting for transfers between devices  159 us (47%)
  blocking collectives  77.7 us (23%)
  other arithmetic  31.7 us (9%)
  starting transfers between devices  26 us (8%)
  between operations  14.9 us (4%)
  local copies, waits for them, and re-layouts  13.7 us (4%)
  matrix products  11.4 us (3%)
    psum x1, waiting for transfers between devices, shards(): lax.psum((expand_term, proj_term, bias_term, gain_term, kernel_term), ('l...  154 us
    psum x1, blocking collectives, shards(): lax.psum((expand_term, proj_term, bias_term, gain_term, kernel_term), ('l...  77.7 us
    ppermute x4, starting transfers between devices, with_halo(): after = lax.ppermute(initial, axis, down)  15.7 us
    ppermute x4, starting transfers between devices, with_halo(): before = lax.ppermute(last, axis, up)  10.2 us
    reduce_sum x4, other arithmetic, kernel_grad(): rows_out.append(jnp.sum(upstream * window.astype(jnp.float32), axis=(1, 2)))  10 us
    convert_element_type x1, other arithmetic, shards(): (mask_float * (cotangent.astype(jnp.float32) + back_masked)).astype(jnp.b...  8.52 us
    reduce_sum x1, other arithmetic, cell_part(): center = jnp.mean(mixed_cells, axis=0, keepdims=True)  8.26 us
  transfers between devices with their start and end apart: 9, of which 3 were waited for; matrix products, arithmetic and copies ran while one was open for 7% of the time, Pallas kernels for 0%

commit v1 on v0

--- a/solution.py
+++ b/solution.py
@@ -90,6 +90,49 @@
         normed,
         bias_term,
         gain_term,
+    )
+
+
+def reduce_grads(expand, project, bias, gain, taps):
+    hidden, channels = expand.shape
+    n_lon, n_lat = lax.axis_size("lon"), lax.axis_size("lat")
+    share = hidden // n_lon
+    first_core = lax.axis_index("lat") % 2 == 0
+    swap = [(i, i ^ 1) for i in range(n_lat)]
+    tap_rows = jnp.concatenate([taps, gain[None]], axis=0)
+    half_rows = tap_rows.shape[0] // 2
+    pad = jnp.zeros((hidden, 1), jnp.float32)
+    full_a = jnp.concatenate([expand, bias[:, None]], axis=1)
+    full_b = jnp.concatenate([project, pad], axis=1)
+    taps_a = jnp.pad(tap_rows[:half_rows], ((0, 0), (0, 1)))
+    taps_b = jnp.pad(tap_rows[half_rows:], ((0, 0), (0, 1)))
+
+    def halve(one, two):
+        own = jnp.where(first_core, one, two)
+        other = jnp.where(first_core, two, one).astype(jnp.bfloat16)
+        return own + lax.ppermute(other, "lat", swap).astype(jnp.float32)
+
+    weights = halve(full_a, full_b).astype(jnp.bfloat16).reshape(n_lon, share, channels + 1)
+    taps_own = halve(taps_a, taps_b).astype(jnp.bfloat16)
+    parts = jnp.concatenate(
+        [weights, jnp.broadcast_to(taps_own, (n_lon, *taps_own.shape))], axis=1
+    )
+    parts = lax.all_to_all(parts, "lon", 0, 0)
+    own = jnp.sum(parts.astype(jnp.float32), axis=0).astype(jnp.bfloat16)
+    groups = [list(range(core, n_lat, 2)) for core in range(2)]
+    spread = jnp.broadcast_to(own, (n_lat // 2, *own.shape))
+    spread = lax.all_to_all(spread, "lat", 0, 0, axis_index_groups=groups)
+    own = jnp.sum(spread.astype(jnp.float32), axis=0).astype(jnp.bfloat16)
+    other = lax.ppermute(own, "lat", swap)
+    part_a = jnp.where(first_core, own, other).astype(jnp.float32)
+    part_b = jnp.where(first_core, other, own).astype(jnp.float32)
+    tap_sums = jnp.concatenate([part_a[share:], part_b[share:]], axis=0)[:, :channels]
+    return (
+        part_a[:share, :channels],
+        part_b[:share, :channels],
+        part_a[:share, channels],
+        tap_sums[-1],
+        tap_sums[:-1],
     )
 
 
@@ -119,20 +162,15 @@
     back_masked = depthwise(extend(back_mixed), depth_kernel, row_count, col_count, True)
     mask_float = land_sea.astype(jnp.float32)[None]
     grad_state = (mask_float * (cotangent.astype(jnp.float32) + back_masked)).astype(jnp.bfloat16)
-    share = hidden_units // lax.axis_size("lon")
-    first_row = lax.axis_index("lon") * share
     proj_term = lax.dot_general(
         activ, gated, (((1,), (1,)), ((), ())), preferred_element_type=jnp.float32
     )
     expand_term = lax.dot_general(
         back_in, normed, (((1,), (1,)), ((), ())), preferred_element_type=jnp.float32
     )
-    expand_all, project_all, bias_all, grad_gain, grad_kernel = lax.psum(
-        (expand_term, proj_term, bias_term, gain_term, kernel_term), ("lon", "lat")
-    )
-    grad_expand = lax.dynamic_slice_in_dim(expand_all, first_row, share, 0)
-    grad_project = lax.dynamic_slice_in_dim(project_all, first_row, share, 0)
-    grad_bias = lax.dynamic_slice_in_dim(bias_all, first_row, share, 0)
+    grad_expand, grad_project, grad_bias, grad_gain, grad_kernel = reduce_grads(
+        expand_term, proj_term, bias_term, gain_term, kernel_term
+    )
     return (next_state, grad_state, grad_kernel, grad_gain, grad_expand, grad_project, grad_bias)
 
 

time: 337 us -> 128 us (0.38)
  waiting for transfers between devices: 159 us -> 21.6 us
  blocking collectives: 77.7 us -> 0 us
  starting transfers between devices: 26 us -> 42.1 us
  between operations: 14.9 us -> 1.67 us
  other arithmetic: 31.7 us -> 37.5 us
    psum x1 -> x0, waiting for transfers between devices: 154 us -> none  [shards(): lax.psum((expand_term, proj_term, bias_term, gain_term, kernel_term), ('l...]
    psum x1 -> x0, blocking collectives: 77.7 us -> none  [shards(): lax.psum((expand_term, proj_term, bias_term, gain_term, kernel_term), ('l...]
    all_to_all x0 -> x2, starting transfers between devices: none -> 12.2 us  [the longest x1 6.67 us: reduce_grads(): parts = lax.all_to_all(parts, 'lon', 0, 0)]
    ppermute x4, waiting for transfers between devices: 0.49 us -> 12 us  [with_halo(): before = lax.ppermute(last, axis, up)]
    all_to_all x0 -> x2, waiting for transfers between devices: none -> 4.4 us  [the longest x1 4.4 us: reduce_grads(): spread = lax.all_to_all(spread, 'lat', 0, 0, axis_index_groups=groups)]
    another operation x1, local copies, waits for them, and re-layouts: 3.63 us -> 0.1 us  [kernel_grad(): return jnp.stack(rows_out, axis=0)]
  transfers between devices with their start and end apart: 9 -> 13, of which waited for: 3 -> 4; matrix products, arithmetic and copies ran while one was open for 7% -> 17% of each run, Pallas kernels for 0% -> 0%
where the time goes in v1:
time: 128 us
  starting transfers between devices  42.1 us (33%)
  other arithmetic  37.5 us (29%)
  waiting for transfers between devices  21.6 us (17%)
  local copies, waits for them, and re-layouts  13.9 us (11%)
  matrix products  10.9 us (9%)
  between operations  1.67 us (1%)
    ppermute x4, starting transfers between devices, with_halo(): after = lax.ppermute(initial, axis, down)  17.5 us
    ppermute x4, waiting for transfers between devices, with_halo(): before = lax.ppermute(last, axis, up)  12 us
    ppermute x4, starting transfers between devices, with_halo(): before = lax.ppermute(last, axis, up)  10.9 us
    reduce_sum x1, other arithmetic, cell_part(): center = jnp.mean(mixed_cells, axis=0, keepdims=True)  9.09 us
    reduce_sum x4, other arithmetic, kernel_grad(): rows_out.append(jnp.sum(upstream * window.astype(jnp.float32), axis=(1, 2)))  8.91 us
    convert_element_type x1, other arithmetic, shards(): (mask_float * (cotangent.astype(jnp.float32) + back_masked)).astype(jnp.b...  8.49 us
    all_to_all x1, starting transfers between devices, reduce_grads(): parts = lax.all_to_all(parts, 'lon', 0, 0)  6.67 us
    unnamed x114, local copies, waits for them, and re-layouts  6.3 us
  transfers between devices with their start and end apart: 13, of which 4 were waited for; matrix products, arithmetic and copies ran while one was open for 17% of the time, Pallas kernels for 0%

profile of v1, /device:TPU:1, one launch (start us, length us, event | category | flops | bytes accessed | tf_op | source)
XLA Modules:
  0.0 127.7 jit_solution(8117618750503570084)
XLA Ops:
  1.4 1.3 copy.40
  2.9 2.5 %collective-permute-start = (bf16[200,8,3]{0,2,1:T(4,128)(2,1)S(1)}, bf16[200,8,3]{0,2,1:T(4,128)(2,1)S(1)}, u32[]{:S(2)}, u32[]{:S(2)}) collective-permute-start(bf16[200,8,3]{0,2,1:T(4,128)(2,1)S(1)} %get-tuple-element.99), channel_id=1, source_target_pairs={{0,16},{16,32},{32,48},{48,64},{64,80},{80,96},{96,112},{112,128},... | collective-permute-start | bytes 28808 | tf_op jit(solution)/shard_map/ppermute | solution.py:16
  5.5 6.7 %collective-permute-start.1 = (bf16[200,8,3]{0,2,1:T(4,128)(2,1)S(1)}, bf16[200,8,3]{0,2,1:T(4,128)(2,1)S(1)}, u32[]{:S(2)}, u32[]{:S(2)}) collective-permute-start(bf16[200,8,3]{0,2,1:T(4,128)(2,1)S(1)} %get-tuple-element.100), channel_id=1, source_target_pairs={{16,0},{32,16},{48,32},{64,48},{80,64},{96,80},{112,96},{128,112},... | collective-permute-start | bytes 28808 | tf_op jit(solution)/shard_map/ppermute | solution.py:17
  12.9 1.1 copy.54
  14.1 4.0 %collective-permute-start.2 = (bf16[200,3,134]{0,2,1:T(8,128)(2,1)S(1)}, bf16[200,3,134]{0,2,1:T(8,128)(2,1)S(1)}, u32[]{:S(2)}, u32[]{:S(2)}) collective-permute-start(bf16[200,3,134]{0,2,1:T(8,128)(2,1)S(1)} %get-tuple-element.95), channel_id=1, source_target_pairs={{0,1},{1,2},{2,3},{3,4},{4,5},{5,6},{6,7},{7,8},{8,9},{9,10},{10,1... | collective-permute-start | bytes 482408 | tf_op jit(solution)/shard_map/ppermute | solution.py:16
  18.1 2.1 %collective-permute-start.3 = (bf16[200,3,134]{0,2,1:T(8,128)(2,1)S(1)}, bf16[200,3,134]{0,2,1:T(8,128)(2,1)S(1)}, u32[]{:S(2)}, u32[]{:S(2)}) collective-permute-start(bf16[200,3,134]{0,2,1:T(8,128)(2,1)S(1)} %get-tuple-element.96), channel_id=1, source_target_pairs={{1,0},{2,1},{3,2},{4,3},{5,4},{6,5},{7,6},{8,7},{9,8},{10,9},{11,1... | collective-permute-start | bytes 482408 | tf_op jit(solution)/shard_map/ppermute | solution.py:17
  20.8 4.4 %collective-permute-done.3 = bf16[200,3,134]{0,2,1:T(8,128)(2,1)S(1)} collective-permute-done((bf16[200,3,134]{0,2,1:T(8,128)(2,1)S(1)}, bf16[200,3,134]{0,2,1:T(8,128)(2,1)S(1)}, u32[]{:S(2)}, u32[]{:S(2)}) %collective-permute-start.3) | collective-permute-done | bytes 160832 | tf_op jit(solution)/shard_map/ppermute | solution.py:17
  25.8 9.1 %fusion.148 = (f32[8,128]{1,0:T(8,128)S(1)}, f32[200,8,128]{0,2,1:T(8,128)S(1)}) fusion(bf16[200,11,134]{0,2,1:T(8,128)(2,1)S(1)} %get-tuple-element.94, f32[200]{0:T(256)} %bitcast.49, f32[200]{0:T(256)} %bitcast.48, f32[200]{0:T(256)S(1)} %bitcast.214, f32[200]{0:T(256)S(1)} %bitcast.216, f32[200]{0:T(256)S(1)} %bitcast.218, f32[200]{0:T(256)S(1)} %bitcast.220, ...), kind=kLoop, calls=%fused_computation.349 | loop fusion | flops 33790976 | bytes 18494496 | tf_op jit(solution)/shard_map/reduce_sum | solution.py:57
  35.0 0.9 copy-done.2
  36.3 2.4 %copy.53 = f32[200,1024]{1,0:T(8,128)} copy(f32[200,1024]{0,1:T(8,128)} %bitcast.208) | data formatting | bytes 1638400 | tf_op jit(solution)/shard_map/reshape | solution.py:150
  38.8 3.5 %fusion.9 = (bf16[800,1024]{1,0:T(8,128)(2,1)}, f32[1024,800]{0,1:T(8,128)S(1)}) fusion(f32[800]{0:T(1024)S(1)} %copy-done.52, bf16[800,200]{0,1:T(8,128)(2,1)S(1)} %copy-done, f32[200,1024]{1,0:T(8,128)} %copy.53, f32[200]{0:T(256)S(1)} %copy-done.14, f32[1024]{0:T(1024)S(1)} %rsqrt_bitcast_fusion, f32[1024]{0:T(1024)S(1)} %get-tuple-element.155), kind=kOutput, calls=%fused_computation.62 | convolution fusion | flops 333414400 | bytes 6066592 | tf_op jit(solution)/shard_map/dot_general | solution.py:62
  42.3 2.3 %convert_reduce_fusion = (f32[800]{0:T(1024)S(1)}, bf16[800,1024]{1,0:T(8,128)(2,1)S(1)}) fusion(f32[1024,800]{0,1:T(8,128)S(1)} %get-tuple-element.158, f32[800]{0:T(1024)S(1)} %copy-done.52, bf16[800,200]{0,1:T(8,128)(2,1)S(1)} %copy-done.53, f32[200,1024]{1,0:T(8,128)S(1)} %copy-done.9, f32[1024]{0:T(1024)S(1)} %get-tuple-element.153), kind=kOutput, calls=%fused_computation.63 | convolution fusion | flops 338738400 | bytes 6064896 | tf_op jit(solution)/shard_map/dot_general | solution.py:71
  44.6 1.7 %fusion.146 = f32[800,200]{0,1:T(8,128)} fusion(bf16[800,1024]{1,0:T(8,128)(2,1)S(1)} %get-tuple-element.161, f32[200,1024]{1,0:T(8,128)S(1)} %copy-done.1, f32[200]{0:T(256)S(1)} %copy-done.14, f32[1024]{0:T(1024)S(1)} %rsqrt_bitcast_fusion, f32[1024]{0:T(1024)S(1)} %get-tuple-element.155), kind=kOutput, calls=%fused_computation.347 | convolution fusion | flops 328499200 | bytes 3106592 | tf_op jit(solution)/shard_map/dot_general | solution.py:168
  47.6 3.2 %fusion.107 = (f32[200]{0:T(256)S(1)}, f32[200]{0:T(256)S(1)}, f32[200]{0:T(256)S(1)}, f32[200]{0:T(256)S(1)}, f32[200]{0:T(256)S(1)}, /*index=5*/f32[200]{0:T(2...) fusion(bf16[200,11,134]{0,2,1:T(8,128)(2,1)S(1)} %get-tuple-ele, ...), kind=kLoop, calls=%fused_computation.212 | loop fusion | flops 11260400 | bytes 7796800 | tf_op jit(solution)/shard_map/reduce_sum | solution.py:50
  50.8 3.2 %fusion.135 = (f32[200]{0:T(256)S(1)}, f32[200]{0:T(256)S(1)}, f32[200]{0:T(256)S(1)}, f32[200]{0:T(256)S(1)}, f32[200]{0:T(256)S(1)}, /*index=5*/f32[200]{0:T(2...) fusion(bf16[200,11,134]{0,2,1:T(8,128)(2,1)S(1)} %get-tuple-ele, ...), kind=kLoop, calls=%fused_computation.240 | loop fusion | flops 11260400 | bytes 7796800 | tf_op jit(solution)/shard_map/reduce_sum | solution.py:50
  57.5 2.0 %fusion.110 = (f32[200]{0:T(256)S(1)}, f32[200]{0:T(256)S(1)}, f32[200]{0:T(256)S(1)}, f32[200]{0:T(256)S(1)}, f32[200]{0:T(256)S(1)}, /*index=5*/f32[200]{0:T(2...) fusion(bf16[200,8,128]{0,2,1:T(8,128)(2,1)S(1)} %broadcast_multiply_fusion, ...), kind=kLoop, calls=%fused_computation.215 | loop fusion | flops 10033200 | bytes 2075200 | tf_op jit(solution)/shard_map/reduce_sum | solution.py:50
  61.2 1.4 %add_convert_fusion = bf16[800,201]{0,1:T(8,128)(2,1)S(1)} fusion(bf16[800,201]{0,1:T(8,128)(2,1)} %collective-permute-done.8, f32[800,200]{0,1:T(8,128)} %copy-done.6, f32[800,1]{0,1:T(1,128)S(1)} %broadcast_in_dim.8, f32[800,200]{0,1:T(8,128)S(1)} %copy-done.5, pred[]{:T(512)S(6)} %eq.5), kind=kLoop, calls=%fused_computation.262 | loop fusion | flops 804000 | bytes 1926401 | tf_op jit(solution)/shard_map/convert_element_type | solution.py:115
  62.9 1.0 pad_maximum_fusion.3
  64.0 6.7 %all-to-all-start = ((bf16[16,75,201]{2,1,0:T(8,128)(2,1)}), bf16[16,75,201]{2,1,0:T(8,128)(2,1)}, u32[]{:S(2)}, u32[]{:S(2)}) async-start(bf16[16,75,201]{2,1,0:T(8,128)(2,1)} %pad_maximum_fusion.3), calls=%async_computation | async-start | bytes 1310720 | tf_op jit(solution)/shard_map/all_to_all | solution.py:120
  70.7 1.4 %collective-permute-start.4 = (bf16[200,8,3]{0,2,1:T(4,128)(2,1)S(1)}, bf16[200,8,3]{0,2,1:T(4,128)(2,1)S(1)}, u32[]{:S(2)}, u32[]{:S(2)}) collective-permute-start(bf16[200,8,3]{0,2,1:T(4,128)(2,1)S(1)} %get-tuple-element.98), channel_id=1, source_target_pairs={{0,16},{16,32},{32,48},{48,64},{64,80},{80,96},{96,112},{112,128},... | collective-permute-start | bytes 28808 | tf_op jit(solution)/shard_map/ppermute | solution.py:16
  72.1 3.8 %collective-permute-start.5 = (bf16[200,8,3]{0,2,1:T(4,128)(2,1)S(1)}, bf16[200,8,3]{0,2,1:T(4,128)(2,1)S(1)}, u32[]{:S(2)}, u32[]{:S(2)}) collective-permute-start(bf16[200,8,3]{0,2,1:T(4,128)(2,1)S(1)} %get-tuple-element.97), channel_id=1, source_target_pairs={{16,0},{32,16},{48,32},{64,48},{80,64},{96,80},{112,96},{128,112},... | collective-permute-start | bytes 28808 | tf_op jit(solution)/shard_map/ppermute | solution.py:17
  75.8 1.0 convert.53
  76.8 11.9 %collective-permute-done.4 = bf16[200,8,3]{0,2,1:T(4,128)(2,1)S(1)} collective-permute-done((bf16[200,8,3]{0,2,1:T(4,128)(2,1)S(1)}, bf16[200,8,3]{0,2,1:T(4,128)(2,1)S(1)}, u32[]{:S(2)}, u32[]{:S(2)}) %collective-permute-start.4) | collective-permute-done | bytes 9632 | tf_op jit(solution)/shard_map/ppermute | solution.py:16
  89.7 4.9 %collective-permute-start.6 = (bf16[200,3,134]{0,2,1:T(8,128)(2,1)}, bf16[200,3,134]{0,2,1:T(8,128)(2,1)}, u32[]{:S(2)}, u32[]{:S(2)}) collective-permute-start(bf16[200,3,134]{0,2,1:T(8,128)(2,1)} %get-tuple-element.91), channel_id=1, source_target_pairs={{1,0},{2,1},{3,2},{4,3},{5,4},{6,5},{7,6},{8,7},{9,8},{10,9},{11,1... | collective-permute-start | bytes 482408 | tf_op jit(solution)/shard_map/ppermute | solution.py:17
  94.6 3.0 %collective-permute-start.7 = (bf16[200,3,134]{0,2,1:T(8,128)(2,1)}, bf16[200,3,134]{0,2,1:T(8,128)(2,1)}, u32[]{:S(2)}, u32[]{:S(2)}) collective-permute-start(bf16[200,3,134]{0,2,1:T(8,128)(2,1)} %get-tuple-element.92), channel_id=1, source_target_pairs={{0,1},{1,2},{2,3},{3,4},{4,5},{5,6},{6,7},{7,8},{8,9},{9,10},{10,1... | collective-permute-start | bytes 482408 | tf_op jit(solution)/shard_map/ppermute | solution.py:16
  97.6 1.2 reduce_sum.574
  99.6 5.6 %all-to-all-start.1 = ((bf16[8,75,201]{2,1,0:T(8,128)(2,1)}), bf16[8,75,201]{2,1,0:T(8,128)(2,1)S(1)}, u32[]{:S(2)}, u32[]{:S(2)}) async-start(bf16[8,75,201]{2,1,0:T(8,128)(2,1)} %broadcast_in_dim.11), calls=%async_computation.1 | async-start | bytes 655360 | tf_op jit(solution)/shard_map/all_to_all | solution.py:124
  105.2 1.8 %fusion.13 = bf16[25,8,8,128]{3,1,2,0:T(8,128)(2,1)S(1)} fusion(bf16[800,1024]{1,0:T(8,128)(2,1)S(1)} %copy-done.4, bf16[800,200]{0,1:T(8,128)(2,1)S(1)} %copy-done.54, f32[25,8,8,128]{3,2,1,0:T(8,128)} %convert.53, f32[1024]{0:T(1024)S(1)} %get-tuple-element.153), kind=kOutput, calls=%fused_computation.118 | convolution fusion | flops 328294400 | bytes 3191296 | tf_op jit(solution)/shard_map/dot_general | solution.py:65
  107.8 1.3 %pad_maximum_fusion.1 = (bf16[200,11,134]{0,2,1:T(8,128)(2,1)S(1)}, bf16[200,11,134]{0,2,1:T(8,128)(2,1)S(1)}) fusion(bf16[200,3,134]{0,2,1:T(8,128)(2,1)} %collective-permute-done.6, bf16[200,8,3]{0,2,1:T(4,128)(2,1)S(1)} %collective-permute-done.5, bf16[200,8,128]{0,2,1:T(8,128)(2,1)S(1)} %bitcast.206, bf16[200,8,3]{0,2,1:T(4,128)(2,1)S(1)} %collective-permute-done.4, ...), kind=kLoop, calls=%fused_computation.251 | loop fusion | flops 4716800 | bytes 1929600 | tf_op jit(solution)/shard_map/concatenate | solution.py:18
  109.1 4.4 %all-to-all-done.1 = bf16[8,75,201]{2,1,0:T(8,128)(2,1)S(1)} async-done(((bf16[8,75,201]{2,1,0:T(8,128)(2,1)}), bf16[8,75,201]{2,1,0:T(8,128)(2,1)S(1)}, u32[]{:S(2)}, u32[]{:S(2)}) %all-to-all-start.1) | async-done | bytes 241232 | tf_op jit(solution)/shard_map/all_to_all | solution.py:124
  114.2 8.5 %multiply_convert_fusion = bf16[200,8,128]{0,2,1:T(8,128)(2,1)S(1)} fusion(bf16[200,8,128]{0,2,1:T(8,128)(2,1)S(1)} %bitcast.207, bf16[200,8,3]{0,2,1:T(4,128)(2,1)S(1)} %collective-permute-done.4, bf16[200,8,3]{0,2,1:T(4,128)(2,1)S(1)} %collective-permute-done.5, bf16[200,11,134]{0,2,1:T(8,128)(2,1)S(1)} %get-tuple-element.90, ...), kind=kLoop, calls=%fused_computation.241 | loop fusion | flops 34406400 | bytes 18494496 | tf_op jit(solution)/shard_map/convert_element_type | solution.py:164
  122.7 1.0 copy.52
  (162 shorter events, 16.7 us)
Async XLA Ops:
  0.6 38.1 %copy-start = (bf16[800,200]{0,1:T(8,128)(2,1)S(1)}, bf16[800,200]{0,1:T(8,128)(2,1)}, u32[]{:S(2)}) copy-start(bf16[800,200]{0,1:T(8,128)(2,1)} %param.12) | copy-start | bytes 960004
  2.9 11.0 %collective-permute-start = (bf16[200,8,3]{0,2,1:T(4,128)(2,1)S(1)}, bf16[200,8,3]{0,2,1:T(4,128)(2,1)S(1)}, u32[]{:S(2)}, u32[]{:S(2)}) collective-permute-start(bf16[200,8,3]{0,2,1:T(4,128)(2,1)S(1)} %get-tuple-element.99), channel_id=1, source_target_pairs={{0,16},{16,32},{32,48},{48,64},{64,80},{80,96},{96,112},{112,128},... | collective-permute-start | bytes 28808 | tf_op jit(solution)/shard_map/ppermute | solution.py:16
  5.5 8.5 %collective-permute-start.1 = (bf16[200,8,3]{0,2,1:T(4,128)(2,1)S(1)}, bf16[200,8,3]{0,2,1:T(4,128)(2,1)S(1)}, u32[]{:S(2)}, u32[]{:S(2)}) collective-permute-start(bf16[200,8,3]{0,2,1:T(4,128)(2,1)S(1)} %get-tuple-element.100), channel_id=1, source_target_pairs={{16,0},{32,16},{48,32},{64,48},{80,64},{96,80},{112,96},{128,112},... | collective-permute-start | bytes 28808 | tf_op jit(solution)/shard_map/ppermute | solution.py:17
  12.2 13.3 %copy-start.15 = (f32[1,200]{1,0:T(1,128)}, f32[1,200]{1,0:T(1,128)S(1)}, u32[]{:S(2)}) copy-start(f32[1,200]{1,0:T(1,128)S(1)} %get-tuple-element.106) | copy-start | bytes 2404
  12.2 13.3 %copy-start.16 = (f32[1,200]{1,0:T(1,128)}, f32[1,200]{1,0:T(1,128)S(1)}, u32[]{:S(2)}) copy-start(f32[1,200]{1,0:T(1,128)S(1)} %get-tuple-element.107) | copy-start | bytes 2404
  12.2 13.3 %copy-start.17 = (f32[1,200]{1,0:T(1,128)}, f32[1,200]{1,0:T(1,128)S(1)}, u32[]{:S(2)}) copy-start(f32[1,200]{1,0:T(1,128)S(1)} %get-tuple-element.108) | copy-start | bytes 2404
  12.2 13.3 %copy-start.18 = (f32[1,200]{1,0:T(1,128)}, f32[1,200]{1,0:T(1,128)S(1)}, u32[]{:S(2)}) copy-start(f32[1,200]{1,0:T(1,128)S(1)} %get-tuple-element.109) | copy-start | bytes 2404
  12.2 13.3 %copy-start.19 = (f32[1,200]{1,0:T(1,128)}, f32[1,200]{1,0:T(1,128)S(1)}, u32[]{:S(2)}) copy-start(f32[1,200]{1,0:T(1,128)S(1)} %get-tuple-element.110) | copy-start | bytes 2404
  12.2 13.3 %copy-start.20 = (f32[1,200]{1,0:T(1,128)}, f32[1,200]{1,0:T(1,128)S(1)}, u32[]{:S(2)}) copy-start(f32[1,200]{1,0:T(1,128)S(1)} %get-tuple-element.111) | copy-start | bytes 2404
  12.2 13.3 %copy-start.21 = (f32[1,200]{1,0:T(1,128)}, f32[1,200]{1,0:T(1,128)S(1)}, u32[]{:S(2)}) copy-start(f32[1,200]{1,0:T(1,128)S(1)} %get-tuple-element.112) | copy-start | bytes 2404
  12.2 13.3 %copy-start.22 = (f32[1,200]{1,0:T(1,128)}, f32[1,200]{1,0:T(1,128)S(1)}, u32[]{:S(2)}) copy-start(f32[1,200]{1,0:T(1,128)S(1)} %get-tuple-element.113) | copy-start | bytes 2404
  12.2 13.3 %copy-start.23 = (f32[1,200]{1,0:T(1,128)}, f32[1,200]{1,0:T(1,128)S(1)}, u32[]{:S(2)}) copy-start(f32[1,200]{1,0:T(1,128)S(1)} %get-tuple-element.114) | copy-start | bytes 2404
  12.2 13.3 %copy-start.24 = (f32[1,200]{1,0:T(1,128)}, f32[1,200]{1,0:T(1,128)S(1)}, u32[]{:S(2)}) copy-start(f32[1,200]{1,0:T(1,128)S(1)} %get-tuple-element.115) | copy-start | bytes 2404
  12.3 13.3 %copy-start.25 = (f32[1,200]{1,0:T(1,128)}, f32[1,200]{1,0:T(1,128)S(1)}, u32[]{:S(2)}) copy-start(f32[1,200]{1,0:T(1,128)S(1)} %get-tuple-element.116) | copy-start | bytes 2404
  12.3 13.3 %copy-start.26 = (f32[1,200]{1,0:T(1,128)}, f32[1,200]{1,0:T(1,128)S(1)}, u32[]{:S(2)}) copy-start(f32[1,200]{1,0:T(1,128)S(1)} %get-tuple-element.117) | copy-start | bytes 2404
  12.3 13.3 %copy-start.27 = (f32[1,200]{1,0:T(1,128)}, f32[1,200]{1,0:T(1,128)S(1)}, u32[]{:S(2)}) copy-start(f32[1,200]{1,0:T(1,128)S(1)} %get-tuple-element.118) | copy-start | bytes 2404
  12.3 13.3 %copy-start.28 = (f32[1,200]{1,0:T(1,128)}, f32[1,200]{1,0:T(1,128)S(1)}, u32[]{:S(2)}) copy-start(f32[1,200]{1,0:T(1,128)S(1)} %get-tuple-element.119) | copy-start | bytes 2404
  12.3 13.3 %copy-start.29 = (f32[1,200]{1,0:T(1,128)}, f32[1,200]{1,0:T(1,128)S(1)}, u32[]{:S(2)}) copy-start(f32[1,200]{1,0:T(1,128)S(1)} %get-tuple-element.120) | copy-start | bytes 2404
  14.1 6.7 %collective-permute-start.2 = (bf16[200,3,134]{0,2,1:T(8,128)(2,1)S(1)}, bf16[200,3,134]{0,2,1:T(8,128)(2,1)S(1)}, u32[]{:S(2)}, u32[]{:S(2)}) collective-permute-start(bf16[200,3,134]{0,2,1:T(8,128)(2,1)S(1)} %get-tuple-element.95), channel_id=1, source_target_pairs={{0,1},{1,2},{2,3},{3,4},{4,5},{5,6},{6,7},{7,8},{8,9},{9,10},{10,1... | collective-permute-start | bytes 482408 | tf_op jit(solution)/shard_map/ppermute | solution.py:16
  18.1 7.1 %collective-permute-start.3 = (bf16[200,3,134]{0,2,1:T(8,128)(2,1)S(1)}, bf16[200,3,134]{0,2,1:T(8,128)(2,1)S(1)}, u32[]{:S(2)}, u32[]{:S(2)}) collective-permute-start(bf16[200,3,134]{0,2,1:T(8,128)(2,1)S(1)} %get-tuple-element.96), channel_id=1, source_target_pairs={{1,0},{2,1},{3,2},{4,3},{5,4},{6,5},{7,6},{8,7},{9,8},{10,9},{11,1... | collective-permute-start | bytes 482408 | tf_op jit(solution)/shard_map/ppermute | solution.py:17
  20.8 14.1 %copy-start.50 = (f32[1,200]{1,0:T(1,128)}, f32[1,200]{1,0:T(1,128)S(1)}, u32[]{:S(2)}) copy-start(f32[1,200]{1,0:T(1,128)S(1)} %get-tuple-element.141) | copy-start | bytes 2404
  57.2 4.0 %collective-permute-start.8 = (bf16[800,201]{0,1:T(8,128)(2,1)S(1)}, bf16[800,201]{0,1:T(8,128)(2,1)}, u32[]{:S(2)}, u32[]{:S(2)}) collective-permute-start(bf16[800,201]{0,1:T(8,128)(2,1)S(1)} %select_convert_fusion), channel_id=1, source_target_pairs={{0,1},{1,0},{2,3},{3,2},{4,5},{5,4},{6,7},{7,6},{8,9},{9,8},{10,11... | collective-permute-start | bytes 964808 | tf_op jit(solution)/shard_map/ppermute | solution.py:113
  59.8 1.4 %collective-permute-start.9 = (bf16[25,201]{1,0:T(8,128)(2,1)S(1)}, bf16[25,201]{1,0:T(8,128)(2,1)S(1)}, u32[]{:S(2)}, u32[]{:S(2)}) collective-permute-start(bf16[25,201]{1,0:T(8,128)(2,1)S(1)} %select_convert_fusion.3), channel_id=1, source_target_pairs={{0,1},{1,0},{2,3},{3,2},{4,5},{5,4},{6,7},{7,6},{8,9},{9,8},{10,11... | collective-permute-start | bytes 30158 | tf_op jit(solution)/shard_map/ppermute | solution.py:113
  64.0 33.7 %all-to-all-start = ((bf16[16,75,201]{2,1,0:T(8,128)(2,1)}), bf16[16,75,201]{2,1,0:T(8,128)(2,1)}, u32[]{:S(2)}, u32[]{:S(2)}) async-start(bf16[16,75,201]{2,1,0:T(8,128)(2,1)} %pad_maximum_fusion.3), calls=%async_computation | async-start | bytes 1310720 | tf_op jit(solution)/shard_map/all_to_all | solution.py:120
  70.7 18.1 %collective-permute-start.4 = (bf16[200,8,3]{0,2,1:T(4,128)(2,1)S(1)}, bf16[200,8,3]{0,2,1:T(4,128)(2,1)S(1)}, u32[]{:S(2)}, u32[]{:S(2)}) collective-permute-start(bf16[200,8,3]{0,2,1:T(4,128)(2,1)S(1)} %get-tuple-element.98), channel_id=1, source_target_pairs={{0,16},{16,32},{32,48},{48,64},{64,80},{80,96},{96,112},{112,128},... | collective-permute-start | bytes 28808 | tf_op jit(solution)/shard_map/ppermute | solution.py:16
  72.1 16.7 %collective-permute-start.5 = (bf16[200,8,3]{0,2,1:T(4,128)(2,1)S(1)}, bf16[200,8,3]{0,2,1:T(4,128)(2,1)S(1)}, u32[]{:S(2)}, u32[]{:S(2)}) collective-permute-start(bf16[200,8,3]{0,2,1:T(4,128)(2,1)S(1)} %get-tuple-element.97), channel_id=1, source_target_pairs={{16,0},{32,16},{48,32},{64,48},{80,64},{96,80},{112,96},{128,112},... | collective-permute-start | bytes 28808 | tf_op jit(solution)/shard_map/ppermute | solution.py:17
  76.8 28.3 %copy-start.4 = (bf16[800,1024]{1,0:T(8,128)(2,1)S(1)}, bf16[800,1024]{1,0:T(8,128)(2,1)}, u32[]{:S(2)}) copy-start(bf16[800,1024]{1,0:T(8,128)(2,1)} %get-tuple-element.157) | copy-start | bytes 4915204
  76.8 28.3 %copy-start.54 = (bf16[800,200]{0,1:T(8,128)(2,1)S(1)}, bf16[800,200]{0,1:T(8,128)(2,1)}, u32[]{:S(2)}) copy-start(bf16[800,200]{0,1:T(8,128)(2,1)} %param.14) | copy-start | bytes 960004
  89.7 18.1 %collective-permute-start.6 = (bf16[200,3,134]{0,2,1:T(8,128)(2,1)}, bf16[200,3,134]{0,2,1:T(8,128)(2,1)}, u32[]{:S(2)}, u32[]{:S(2)}) collective-permute-start(bf16[200,3,134]{0,2,1:T(8,128)(2,1)} %get-tuple-element.91), channel_id=1, source_target_pairs={{1,0},{2,1},{3,2},{4,3},{5,4},{6,5},{7,6},{8,7},{9,8},{10,9},{11,1... | collective-permute-start | bytes 482408 | tf_op jit(solution)/shard_map/ppermute | solution.py:17
  94.6 13.2 %collective-permute-start.7 = (bf16[200,3,134]{0,2,1:T(8,128)(2,1)}, bf16[200,3,134]{0,2,1:T(8,128)(2,1)}, u32[]{:S(2)}, u32[]{:S(2)}) collective-permute-start(bf16[200,3,134]{0,2,1:T(8,128)(2,1)} %get-tuple-element.92), channel_id=1, source_target_pairs={{0,1},{1,2},{2,3},{3,4},{4,5},{5,6},{6,7},{7,8},{8,9},{9,10},{10,1... | collective-permute-start | bytes 482408 | tf_op jit(solution)/shard_map/ppermute | solution.py:16
  99.6 13.9 %all-to-all-start.1 = ((bf16[8,75,201]{2,1,0:T(8,128)(2,1)}), bf16[8,75,201]{2,1,0:T(8,128)(2,1)S(1)}, u32[]{:S(2)}, u32[]{:S(2)}) async-start(bf16[8,75,201]{2,1,0:T(8,128)(2,1)} %broadcast_in_dim.11), calls=%async_computation.1 | async-start | bytes 655360 | tf_op jit(solution)/shard_map/all_to_all | solution.py:124
  113.6 10.1 %collective-permute-start.10 = (bf16[75,201]{1,0:T(8,128)(2,1)S(1)}, bf16[75,201]{1,0:T(8,128)(2,1)}, u32[]{:S(2)}, u32[]{:S(2)}) collective-permute-start(bf16[75,201]{1,0:T(8,128)(2,1)S(1)} %reduce_sum.575), channel_id=1, source_target_pairs={{0,1},{1,0},{2,3},{3,2},{4,5},{5,4},{6,7},{7,6},{8,9},{9,8},{10,11... | collective-permute-start | bytes 90458 | tf_op jit(solution)/shard_map/ppermute | solution.py:126
  (36 other events, 352.1 us)

commit v2 on v0

v2 whole, which is shorter than its diff:
```python
import functools

import jax
import jax.numpy as jnp
from jax import lax
from jax.experimental import pallas as pl
from jax.experimental.pallas import tpu as pltpu
from jax.sharding import PartitionSpec as P

EPS = 1e-06
BF = jnp.bfloat16
F32 = jnp.float32
HALO = 3
TAPS = 7
VMEM_BYTES = 24 * 1024 * 1024


def kernel_call(body, outs, scratch=(), n_in=0, n_any=0, micros=1):
    specs = [pl.BlockSpec(memory_space=pltpu.HBM)] * n_any
    specs += [pl.BlockSpec(memory_space=pltpu.VMEM)] * n_in
    return pl.pallas_call(
        body,
        out_shape=[jax.ShapeDtypeStruct(shape, dtype) for shape, dtype in outs],
        in_specs=specs,
        out_specs=[pl.BlockSpec(memory_space=pltpu.VMEM)] * len(outs),
        scratch_shapes=list(scratch),
        compiler_params=pltpu.CompilerParams(vmem_limit_bytes=VMEM_BYTES),
        cost_estimate=pl.CostEstimate(
            flops=micros * 1_000_000_000, bytes_accessed=micros * 3_000_000, transcendentals=0
        ),
    )


def nt_dot(left, right):
    return lax.dot_general(left, right, (((1,), (1,)), ((), ())), preferred_element_type=F32)


def tn_dot(left, right):
    return lax.dot_general(left, right, (((0,), (0,)), ((), ())), preferred_element_type=F32)


def dot(left, right):
    return jnp.dot(left, right, preferred_element_type=F32)


def load_masked(field_hbm, mask_hbm, field, mask_ref, flat, sems):
    channels, rows, lanes = field.shape
    parts = sems.shape[0] - 1
    step = channels // parts
    copies = [pltpu.make_async_copy(mask_hbm, mask_ref, sems.at[parts])]
    for k in range(parts):
        part = pl.ds(k * step, step)
        copies.append(pltpu.make_async_copy(field_hbm.at[part], field.at[part], sems.at[k]))
    for copy in copies:
        copy.start()
    for copy in copies:
        copy.wait()
    mask = mask_ref[...].astype(F32)[None]
    flat[...] = (field[...].astype(F32) * mask).reshape(channels * rows, lanes)
    return [flat[pl.ds(row, channels, stride=rows), :].astype(BF) for row in range(rows)]


def state_body(x_hbm, mask_hbm, m_ref, top_ref, bot_ref, field, mask_ref, flat, sems):
    masked = load_masked(x_hbm, mask_hbm, field, mask_ref, flat, sems)
    rows = len(masked)
    for row, value in enumerate(masked):
        m_ref[row] = value
        if row < HALO:
            top_ref[row] = value
        if row >= rows - HALO:
            bot_ref[row - rows + HALO] = value


def gated_body(cot_hbm, mask_hbm, g_ref, field, mask_ref, flat, sems):
    for row, value in enumerate(load_masked(cot_hbm, mask_hbm, field, mask_ref, flat, sems)):
        g_ref[row] = value


def columns(row, lanes):
    high = row.astype(BF)
    rest = row - high.astype(F32)
    middle = rest.astype(BF)
    low = (rest - middle.astype(F32)).astype(BF)
    spare = jnp.zeros((5, row.shape[1]), F32)
    parts = [high.astype(F32), middle.astype(F32), low.astype(F32), spare]
    parts = jnp.concatenate(parts, axis=0).astype(BF)
    return tn_dot(parts, jnp.ones((8, lanes), BF))


def weights_body(
    taps_ref, gain_ref, bias_ref, we_ref, wp_ref, spread_ref, gains_ref, biases_ref, we_t_ref, wp_t_ref
):
    count, channels, lanes = spread_ref.shape
    unit = lax.broadcasted_iota(jnp.int32, (count, lanes), 0)
    unit = unit == lax.broadcasted_iota(jnp.int32, (count, lanes), 1)
    taps = tn_dot(taps_ref[...], jnp.where(unit, 1.0, 0.0).astype(BF))
    for tap in range(count):
        spread_ref[tap] = jnp.broadcast_to(taps[:, tap : tap + 1], (channels, lanes))
    gains_ref[...] = columns(gain_ref[...], lanes)
    biases_ref[...] = columns(bias_ref[...], lanes)
    eye = lax.broadcasted_iota(jnp.int32, (channels, channels), 0)
    eye = eye == lax.broadcasted_iota(jnp.int32, (channels, channels), 1)
    eye = jnp.where(eye, 1.0, 0.0).astype(BF)
    we_t_ref[...] = nt_dot(eye, we_ref[...]).astype(BF)
    wp_t_ref[...] = nt_dot(eye, wp_ref[...]).astype(BF)


def is_first(place_ref, shape):
    return jnp.broadcast_to(place_ref[0:1, : shape[1]], shape) > 0.0


def extended_rows(place_ref, mid_ref, up_ref, down_ref):
    shape = mid_ref.shape[1:]
    has_up = jnp.broadcast_to(place_ref[1:2, : shape[1]], shape) > 0.0
    has_down = jnp.broadcast_to(place_ref[2:3, : shape[1]], shape) > 0.0
    for r in range(HALO):
        yield jnp.where(has_up, up_ref[r].astype(F32), 0.0)
    for r in range(mid_ref.shape[0]):
        yield mid_ref[r].astype(F32)
    for r in range(HALO):
        yield jnp.where(has_down, down_ref[r].astype(F32), 0.0)


def pack_body(place_ref, mid_ref, up_ref, down_ref, out_ref):
    channels, lanes = out_ref.shape
    lane = lax.broadcasted_iota(jnp.int32, (channels, lanes), 1)
    packed = jnp.zeros((channels, lanes), F32)
    for r, value in enumerate(extended_rows(place_ref, mid_ref, up_ref, down_ref)):
        if r:
            value = pltpu.roll(value, 8 * r, 1)
        packed = jnp.where(((lane + (HALO - 8 * r)) & (lanes - 1)) < 2 * HALO, value, packed)
    out_ref[...] = packed.astype(BF)


def fill_extended(ext, edge, place_ref, mid_ref, up_ref, down_ref, left_ref, right_ref):
    for r, value in enumerate(extended_rows(place_ref, mid_ref, up_ref, down_ref)):
        ext[r] = value
    channels, lanes = edge.shape
    lane = lax.broadcasted_iota(jnp.int32, (channels, lanes), 1)
    from_left = left_ref[...].astype(F32)
    from_right = right_ref[...].astype(F32)
    edge[...] = jnp.where((lane & 7) >= 4, from_left, from_right)


def joined(ext, edge, start):
    n_rows, _, lanes = ext.shape
    mid = ext[:, pl.ds(start, 8), :]
    ends = edge[pl.ds(start, 8), :]
    wings = jnp.stack(
        [ends] + [pltpu.roll(ends, lanes - 8 * r, 1) for r in range(1, n_rows)], axis=0
    )
    lane = lax.broadcasted_iota(jnp.int32, (8, lanes), 1)
    for shift in range(-HALO, HALO + 1):
        if shift == 0:
            yield shift, mid
            continue
        outside = lane < shift if shift > 0 else lane >= lanes + shift
        yield shift, jnp.where(outside[None], wings, mid)


def convolve(ext, edge, spread_ref, start, rows, flipped):
    lanes = ext.shape[2]
    total = jnp.zeros((rows, 8, lanes), F32)
    for b, (shift, value) in enumerate(joined(ext, edge, start)):
        window = pltpu.roll(value, -shift % lanes, 2) if shift else value
        for a in range(TAPS):
            tap = a * TAPS + b
            if flipped:
                tap = TAPS * TAPS - 1 - tap
            total = total + spread_ref[tap, pl.ds(start, 8), :][None] * window[a : a + rows]
    return total


def main_body(
    place_ref,
    m_ref,
    up_ref,
    down_ref,
    left_ref,
    right_ref,
    mask_ref,
    g_ref,
    spread_ref,
    gains_ref,
    biases_ref,
    we_ref,
    wp_ref,
    we_t_ref,
    wp_t_ref,
    next_ref,
    bm_ref,
    btop_ref,
    bbot_ref,
    gain_ref,
    own_ref,
    other_ref,
    ext,
    edge,
    mixed,
    act,
    back,
    normed_all,
    gated_all,
    flat,
):
    rows, channels, lanes = m_ref.shape
    hidden, deep = own_ref.shape
    chunk = hidden // 5
    pair = 2 * lanes
    fill_extended(ext, edge, place_ref, m_ref, up_ref, down_ref, left_ref, right_ref)

    def conv_step(block, carry):
        start = pl.multiple_of(block * 8, 8)
        mixed[:, pl.ds(start, 8), :] = convolve(ext, edge, spread_ref, start, rows, False)
        return carry

    lax.fori_loop(0, channels // 8, conv_step, 0, unroll=5)
    for r in range(rows):
        gated_all[:, r * lanes : (r + 1) * lanes] = jnp.concatenate(
            [g_ref[r].astype(F32), jnp.zeros((deep - channels, lanes), F32)], axis=0
        ).astype(BF)
    gain_ref[...] = jnp.zeros_like(gain_ref)
    ones_rows = jnp.ones((deep - channels, pair), F32)

    def pair_step(p, carry):
        cells = pl.ds(pl.multiple_of(p * pair, pair), pair)
        value = jnp.concatenate([mixed[2 * p], mixed[2 * p + 1]], axis=1)
        gain = jnp.concatenate([gains_ref[...]] * 2, axis=1)
        center = jnp.sum(value, axis=0, keepdims=True) * (1.0 / channels)
        centered = value - center
        spread = jnp.sum(centered * centered, axis=0, keepdims=True) * (1.0 / channels)
        inv_spread = lax.rsqrt(spread + EPS)
        whitened = centered * inv_spread
        normed = whitened * gain
        normed_all[:, cells] = jnp.concatenate([normed, ones_rows], axis=0).astype(BF)
        normed = normed.astype(BF)
        gated = jnp.concatenate([g_ref[2 * p], g_ref[2 * p + 1]], axis=1)
        for c in range(hidden // chunk):
            part = pl.ds(c * chunk, chunk)
            bias = biases_ref[part, :]
            inner = dot(we_ref[part, :], normed) + jnp.concatenate([bias, bias], axis=1)
            back_act = dot(wp_ref[part, :], gated)
            normal_cdf = 0.5 * (1.0 + lax.erf(inner * 0.7071067811865476))
            density = jnp.exp(-0.5 * inner * inner) * 0.3989422804014327
            act[part, cells] = (inner * normal_cdf).astype(BF)
            back[part, cells] = (back_act * (normal_cdf + inner * density)).astype(BF)
        branch = dot(wp_t_ref[...], act[:, cells])
        back_norm = dot(we_t_ref[...], back[:, cells])
        gain_term = back_norm * whitened
        gain_ref[...] += gain_term[:, :lanes] + gain_term[:, lanes:]
        scaled = back_norm * gain
        mean_scaled = jnp.sum(scaled, axis=0, keepdims=True) * (1.0 / channels)
        mean_product = jnp.sum(scaled * whitened, axis=0, keepdims=True) * (1.0 / channels)
        back_mixed = (inv_spread * (scaled - mean_scaled - whitened * mean_product)).astype(BF)
        for k in range(2):
            r = 2 * p + k
            mask = mask_ref[pl.ds(r, 1), :].astype(F32)
            here = slice(k * lanes, (k + 1) * lanes)
            flat[pl.ds(r, channels, stride=rows), :] = ext[r + HALO] + mask * branch[:, here]
            bm_ref[r] = back_mixed[:, here]
        return carry

    lax.fori_loop(0, rows // 2, pair_step, 0)
    next_ref[...] = flat[...].reshape(channels, rows, lanes).astype(BF)
    for r in range(HALO):
        btop_ref[r] = bm_ref[r]
        bbot_ref[r] = bm_ref[rows - HALO + r]
    first_core = is_first(place_ref, (chunk, deep))
    for c in range(hidden // chunk):
        part = pl.ds(c * chunk, chunk)
        expand = nt_dot(back[part, :], normed_all[...])
        project = nt_dot(act[part, :], gated_all[...])
        own_ref[part, :] = jnp.where(first_core, expand, project)
        other_ref[part, :] = jnp.where(first_core, project, expand).astype(BF)


def taps_body(
    place_ref,
    m_ref,
    up_ref,
    down_ref,
    left_ref,
    right_ref,
    bm_ref,
    gain_ref,
    own_ref,
    other_ref,
    ext,
    edge,
    upstream,
    sums,
):
    rows, channels, lanes = m_ref.shape
    fill_extended(ext, edge, place_ref, m_ref, up_ref, down_ref, left_ref, right_ref)
    for r in range(rows):
        upstream[r] = bm_ref[r].astype(F32)
    lane = lax.broadcasted_iota(jnp.int32, (8, lanes), 1)
    ones = jnp.ones((lanes, lanes), BF)

    def step(block, carry):
        start = pl.multiple_of(block * 8, 8)
        back = upstream[:, pl.ds(start, 8), :]
        result = jnp.zeros((8, lanes), F32)
        for b, (shift, value) in enumerate(joined(ext, edge, start)):
            turned = pltpu.roll(back, shift % lanes, 2) if shift else back
            terms = [jnp.sum(turned * value[a : a + rows], axis=0) for a in range(TAPS)]
            terms.append(gain_ref[pl.ds(start, 8), :])
            totals = dot(jnp.concatenate(terms, axis=0).astype(BF), ones)
            for a in range(TAPS):
                result = jnp.where(lane == a * TAPS + b, totals[8 * a : 8 * a + 8], result)
        result = jnp.where(lane == TAPS * TAPS, totals[8 * TAPS :], result)
        sums[pl.ds(start, 8), :] = result
        return carry

    lax.fori_loop(0, channels // 8, step, 0, unroll=5)
    half, deep = own_ref.shape
    count = (TAPS * TAPS + 1) // 2
    row = lax.broadcasted_iota(jnp.int32, (2 * half, lanes), 0)
    col = lax.broadcasted_iota(jnp.int32, (2 * half, lanes), 1)
    wanted = jnp.where(row < half, row, row - half + count)
    pick = (col == wanted) & (jnp.where(row < half, row, row - half) < count)
    pick = jnp.where(pick, 1.0, 0.0).astype(BF)
    padded = jnp.concatenate([sums[...], jnp.zeros((deep - channels, lanes), F32)], axis=0)
    turned = nt_dot(pick, padded.astype(BF))
    first_core = is_first(place_ref, (half, deep))
    own_ref[...] = jnp.where(first_core, turned[:half], turned[half:])
    other_ref[...] = jnp.where(first_core, turned[half:], turned[:half]).astype(BF)


def message_body(own_ref, got_ref, taps_ref, taps_got_ref, out_ref, total, piece):
    share = own_ref.shape[0] // out_ref.shape[0]
    depth = out_ref.shape[1]
    total[...] = own_ref[...] + got_ref[...].astype(F32)
    taps = taps_ref[...] + taps_got_ref[...].astype(F32)
    count = (TAPS * TAPS + 1) // 2
    piece[...] = jnp.zeros_like(piece)
    piece[share : share + count, :] = taps[:count]
    for k in range(out_ref.shape[0]):
        piece[:share, :] = total[k * share : (k + 1) * share, :]
        out_ref[k] = piece[...].astype(BF)


def sum_body(parts_ref, out_ref):
    total = parts_ref[0].astype(F32)
    for k in range(1, parts_ref.shape[0]):
        total = total + parts_ref[k].astype(F32)
    total = total.astype(BF)
    if len(out_ref.shape) == 2:
        out_ref[...] = total
    else:
        for k in range(out_ref.shape[0]):
            out_ref[k] = total


def final_body(place_ref, own_ref, got_ref, ge_ref, gp_ref, gk_ref, gg_ref, gb_ref, first, second):
    depth, deep = own_ref.shape
    share, channels = ge_ref.shape
    first_core = is_first(place_ref, (depth, deep))
    own = own_ref[...].astype(F32)
    got = got_ref[...].astype(F32)
    first[...] = jnp.where(first_core, own, got)
    second[...] = jnp.where(first_core, got, own)
    ge_ref[...] = first[:share, :channels]
    gp_ref[...] = second[:share, :channels]
    count = (TAPS * TAPS + 1) // 2
    gk_ref[:count, :] = first[share : share + count, :channels]
    gk_ref[count:, :] = second[share : share + count - 1, :channels]
    gg_ref[...] = second[share + count - 1 : share + count, :channels]
    lane = lax.broadcasted_iota(jnp.int32, (8, deep), 1)
    pick = jnp.where(lane == channels, 1.0, 0.0).astype(BF)
    gb_ref[...] = nt_dot(pick, first[...].astype(BF))[:1, :share]


def backward_body(
    place_ref,
    bm_ref,
    up_ref,
    down_ref,
    left_ref,
    right_ref,
    mask_ref,
    g_ref,
    spread_ref,
    out_ref,
    ext,
    edge,
    back,
    flat,
):
    rows, channels, lanes = bm_ref.shape
    fill_extended(ext, edge, place_ref, bm_ref, up_ref, down_ref, left_ref, right_ref)

    def step(block, carry):
        start = pl.multiple_of(block * 8, 8)
        back[:, pl.ds(start, 8), :] = convolve(ext, edge, spread_ref, start, rows, True)
        return carry

    lax.fori_loop(0, channels // 8, step, 0, unroll=5)
    for r in range(rows):
        mask = mask_ref[r : r + 1, :].astype(F32)
        flat[pl.ds(r, channels, stride=rows), :] = g_ref[r].astype(F32) + mask * back[r]
    out_ref[...] = flat[...].reshape(channels, rows, lanes).astype(BF)


def neighbours(top, bottom, axis):
    size = lax.axis_size(axis)
    up = [(i, (i + 1) % size) for i in range(size)]
    down = [(j, i) for i, j in up]
    return lax.ppermute(bottom, axis, up), lax.ppermute(top, axis, down)


def shards(
    ocean_state, land_sea, depth_kernel, norm_gain, w_expand, b_expand, w_project, cotangent
):
    channels, rows, lanes = ocean_state.shape
    hidden = w_expand.shape[0]
    n_lon, n_lat = lax.axis_size("lon"), lax.axis_size("lat")
    share = hidden // n_lon
    deep = -(-(channels + 3) // 16) * 16
    depth = -(-(share + 25) // 16) * 16
    cells = rows * lanes
    full = (rows, channels, lanes)
    edges = (HALO, channels, lanes)
    tile = (channels, lanes)
    flat = pltpu.VMEM((channels * rows, lanes), F32)
    ext_s = pltpu.VMEM((rows + 2 * HALO, channels, lanes), F32)
    edge_s = pltpu.VMEM(tile, F32)
    lat = lax.axis_index("lat")
    kind = lax.broadcasted_iota(jnp.int32, (8, 256), 0)
    value = jnp.where(kind == 0, 1 - lat % 2, jnp.where(kind == 1, lat, n_lat - 1 - lat))
    place = value.astype(F32)
    swap = [(i, i ^ 1) for i in range(n_lat)]

    load_s = [
        pltpu.VMEM(ocean_state.shape, BF),
        pltpu.VMEM((rows, lanes), jnp.int32),
        flat,
        pltpu.SemaphoreType.DMA((6,)),
    ]
    masked, top, bottom = kernel_call(
        state_body, [(full, BF), (edges, BF), (edges, BF)], load_s, n_any=2
    )(ocean_state, land_sea)
    up, down = neighbours(top, bottom, "lat")
    (gated,) = kernel_call(gated_body, [(full, BF)], load_s, n_any=2)(cotangent, land_sea)
    spread, gains, biases, we_t, wp_t = kernel_call(
        weights_body,
        [
            ((TAPS * TAPS, *tile), F32),
            (tile, F32),
            ((hidden, lanes), F32),
            ((channels, hidden), BF),
            ((channels, hidden), BF),
        ],
        n_in=5,
        micros=3,
    )(depth_kernel, norm_gain[None], b_expand[None], w_expand, w_project)
    (pack,) = kernel_call(pack_body, [(tile, BF)], n_in=4)(place, masked, up, down)
    left, right = neighbours(pack, pack, "lon")

    next_state, back_mixed, btop, bbottom, gain, own, other = kernel_call(
        main_body,
        [
            ((channels, rows, lanes), BF),
            (full, BF),
            (edges, BF),
            (edges, BF),
            (tile, F32),
            ((hidden, deep), F32),
            ((hidden, deep), BF),
        ],
        [
            ext_s,
            edge_s,
            pltpu.VMEM(full, F32),
            pltpu.VMEM((hidden, cells), BF),
            pltpu.VMEM((hidden, cells), BF),
            pltpu.VMEM((deep, cells), BF),
            pltpu.VMEM((deep, cells), BF),
            flat,
        ],
        n_in=15,
        micros=12,
    )(
        place,
        masked,
        up,
        down,
        left,
        right,
        land_sea,
        gated,
        spread,
        gains,
        biases,
        w_expand,
        w_project,
        we_t,
        wp_t,
    )
    got = lax.ppermute(other, "lat", swap)
    bup, bdown = neighbours(btop, bbottom, "lat")
    taps_own, taps_other = kernel_call(
        taps_body,
        [((32, deep), F32), ((32, deep), BF)],
        [ext_s, edge_s, pltpu.VMEM(full, F32), edge_s],
        n_in=8,
        micros=6,
    )(place, masked, up, down, left, right, back_mixed, gain)
    taps_got = lax.ppermute(taps_other, "lat", swap)
    (message,) = kernel_call(
        message_body,
        [((n_lon, depth, deep), BF)],
        [pltpu.VMEM((hidden, deep), F32), pltpu.VMEM((depth, deep), F32)],
        n_in=4,
    )(own, got, taps_own, taps_got)
    (back_pack,) = kernel_call(pack_body, [(tile, BF)], n_in=4)(
        place, back_mixed, bup, bdown
    )
    bleft, bright = neighbours(back_pack, back_pack, "lon")
    message, bleft, bright = lax.optimization_barrier((message, bleft, bright))

    parts = lax.all_to_all(message, "lon", 0, 0)
    (grad_state,) = kernel_call(
        backward_body,
        [((channels, rows, lanes), BF)],
        [ext_s, edge_s, pltpu.VMEM(full, F32), flat],
        n_in=9,
        micros=8,
    )(place, back_mixed, bup, bdown, bleft, bright, land_sea, gated, spread)
    parts, grad_state = lax.optimization_barrier((parts, grad_state))
    (copies,) = kernel_call(sum_body, [((n_lat // 2, depth, deep), BF)], n_in=1)(parts)
    groups = [list(range(c, n_lat, 2)) for c in range(2)]
    parts = lax.all_to_all(copies, "lat", 0, 0, axis_index_groups=groups)
    (sums,) = kernel_call(sum_body, [((depth, deep), BF)], n_in=1)(parts)
    sums_got = lax.ppermute(sums, "lat", swap)

    grad_expand, grad_project, grad_kernel, grad_gain, grad_bias = kernel_call(
        final_body,
        [
            ((share, channels), F32),
            ((share, channels), F32),
            ((TAPS * TAPS, channels), F32),
            ((1, channels), F32),
            ((1, share), F32),
        ],
        [pltpu.VMEM((depth, deep), F32)] * 2,
        n_in=3,
    )(place, sums, sums_got)
    return (
        next_state,
        grad_state,
        grad_kernel,
        grad_gain.reshape(channels),
        grad_expand,
        grad_project,
        grad_bias.reshape(share),
    )


def solution(mesh):
    placed = (
        P(None, "lat", "lon"),
        P("lat", "lon"),
        P(),
        P(),
        P(),
        P(),
        P(),
        P(None, "lat", "lon"),
    )
    return jax.shard_map(
        shards,
        mesh=mesh,
        in_specs=placed,
        out_specs=(
            P(None, "lat", "lon"),
            P(None, "lat", "lon"),
            P(),
            P(),
            P("lon", None),
            P("lon", None),
            P("lon"),
        ),
        check_vma=False,
    )
```

time: 337 us -> 93.6 us (0.28)
  waiting for transfers between devices: 159 us -> 20.3 us
  blocking collectives: 77.7 us -> 11.1 us
  other arithmetic: 31.7 us -> 0.09 us
  Pallas kernels: 0 us -> 26.9 us
  between operations: 14.9 us -> 0.8 us
  matrix products: 11.4 us -> 0 us
  local copies, waits for them, and re-layouts: 13.7 us -> 7.13 us
    psum x1 -> x0, waiting for transfers between devices: 154 us -> none  [shards(): lax.psum((expand_term, proj_term, bias_term, gain_term, kernel_term), ('l...]
    psum x1 -> x0, blocking collectives: 77.7 us -> none  [shards(): lax.psum((expand_term, proj_term, bias_term, gain_term, kernel_term), ('l...]
    pallas_call x0 -> x12, Pallas kernels: none -> 26.9 us  [the longest x1 11 us: shards(): kernel_call(main_body, [((channels, rows, lanes), BF), (full, BF), (edges...]
    reduce_sum x6 -> x0, other arithmetic: 18.6 us -> none  [the longest x4 10 us: kernel_grad(): rows_out.append(jnp.sum(upstream * window.astype(jnp.float32), axis=(1, 2)))]
    dot_general x6 -> x0, matrix products: 11.4 us -> none  [the longest x1 2.39 us: cell_part(): lax.dot_general(w_project, activ, (((0,), (0,)), ((), ())), preferred_ele...]
    all_to_all x0 -> x1, blocking collectives: none -> 11.1 us  [shards(): parts = lax.all_to_all(copies, 'lat', 0, 0, axis_index_groups=groups)]
    convert_element_type x6 -> x1, other arithmetic: 10.3 us -> 0.08 us  [shards(): place = value.astype(F32)]
    all_to_all x0 -> x1, waiting for transfers between devices: none -> 9.59 us  [shards(): parts = lax.all_to_all(message, 'lon', 0, 0)]
  transfers between devices with their start and end apart: 9 -> 12, of which waited for: 3 -> 6; matrix products, arithmetic and copies ran while one was open for 7% -> 3% of each run, Pallas kernels for 0% -> 15%
where the time goes in v2:
time: 93.6 us; the launch traced here: 93.2 us
  Pallas kernels  26.9 us (29%)
  starting transfers between devices  26.9 us (29%)
  waiting for transfers between devices  20.3 us (22%)
  blocking collectives  11.1 us (12%)
  local copies, waits for them, and re-layouts  7.13 us (8%)
    ppermute x8, starting transfers between devices, neighbours(): return (lax.ppermute(bottom, axis, up), lax.ppermute(top, axis, down))  16.7 us
    all_to_all x1, blocking collectives, shards(): parts = lax.all_to_all(copies, 'lat', 0, 0, axis_index_groups=groups)  11.1 us
    pallas_call x1, Pallas kernels, shards(): kernel_call(main_body, [((channels, rows, lanes), BF), (full, BF), (edges...  11 us
    ppermute x8, waiting for transfers between devices, neighbours(): return (lax.ppermute(bottom, axis, up), lax.ppermute(top, axis, down))  9.82 us
    all_to_all x1, waiting for transfers between devices, shards(): parts = lax.all_to_all(message, 'lon', 0, 0)  9.59 us
    unnamed x18, local copies, waits for them, and re-layouts  6.44 us
    pallas_call x1, Pallas kernels, shards(): kernel_call(backward_body, [((channels, rows, lanes), BF)], [ext_s, edge_...  5.5 us
    pallas_call x1, Pallas kernels, shards(): kernel_call(taps_body, [((32, deep), F32), ((32, deep), BF)], [ext_s, edg...  4.6 us
  transfers between devices with their start and end apart: 12, of which 6 were waited for; matrix products, arithmetic and copies ran while one was open for 3% of the time, Pallas kernels for 15%

profile of v2, /device:TPU:1, one launch (start us, length us, event | category | flops | bytes accessed | tf_op | source)
XLA Modules:
  0.0 93.2 jit_solution(18241251803430393026)
XLA Ops:
  0.6 1.0 %copy-done = bf16[200,8,128]{2,1,0:T(8,128)(2,1)S(1)} copy-done((bf16[200,8,128]{2,1,0:T(8,128)(2,1)S(1)}, bf16[200,8,128]{2,1,0:T(8,128)(2,1)}, u32[]{:S(2)}) %copy-start) | copy-done | bytes 409624
  1.6 0.7 copy-done.3
  2.3 0.8 shard_map.135
  3.2 2.7 %collective-permute-start = (bf16[3,200,128]{2,1,0:T(8,128)(2,1)S(1)}, bf16[3,200,128]{2,1,0:T(8,128)(2,1)S(1)}, u32[]{:S(2)}, u32[]{:S(2)}) collective-permute-start(bf16[3,200,128]{2,1,0:T(8,128)(2,1)S(1)} %get-tuple-element.35), channel_id=1, source_target_pairs={{0,1},{1,2},{2,3},{3,4},{4,5},{5,6},{6,7},{7,8},{8,9},{9,10},{10,1... | collective-permute-start | bytes 460808 | tf_op jit(solution)/shard_map/ppermute | solution.py:409
  5.8 0.7 collective-permute-start.1
  6.6 0.7 broadcast_in_dim.22.bias_ref
  7.3 1.2 %copy.15.we_ref = bf16[800,200]{1,0:T(8,128)(2,1)S(1)} copy(bf16[800,200]{0,1:T(8,128)(2,1)} %param.12) | data formatting | bytes 640000 | tf_op args[4]
  8.4 1.2 %copy.16.wp_ref = bf16[800,200]{1,0:T(8,128)(2,1)S(1)} copy(bf16[800,200]{0,1:T(8,128)(2,1)} %param.14) | data formatting | bytes 640000 | tf_op args[6]
  9.7 1.7 %shard_map.138 = (f32[49,200,128]{2,1,0:T(8,128)S(1)}, f32[200,128]{1,0:T(8,128)S(1)}, f32[800,128]{1,0:T(8,128)S(1)}, bf16[200,800]{1,0:T(8,128)(2,1)S(1)}, bf16[200,800]{1,0:T(8,128)(2,1)S(1)}) custom-call(bf16[49,200]{1,0:T(8,128)(2,1)S(1)} %copy-done.2, f32[1,200]{1,0:T(1,128)S(1)} %bitcast.3, f32[1,800]{1,0:T(1,128)S(1)} %broadcast_in_dim.22.bias_ref, ...), custom_call_target="tpu_custom_call" | custom-call | flops 3000000000 | bytes 9000000 | tf_op jit(solution)/shard_map/pallas_call | solution.py:445
  11.5 0.3 shard_map.136
  11.7 7.6 %collective-permute-start.3 = (bf16[200,128]{1,0:T(8,128)(2,1)S(1)}, bf16[200,128]{1,0:T(8,128)(2,1)S(1)}, u32[]{:S(2)}, u32[]{:S(2)}) collective-permute-start(bf16[200,128]{1,0:T(8,128)(2,1)S(1)} %shard_map.136), channel_id=1, source_target_pairs={{16,0},{32,16},{48,32},{64,48},{80,64},{96,80},{112,96},{128,112},... | collective-permute-start | bytes 153608 | tf_op jit(solution)/shard_map/ppermute | solution.py:409
  19.3 0.8 shard_map.137.g_ref
  20.2 0.3 collective-permute-done.3.right_ref
  20.5 5.4 %collective-permute-done.2.left_ref = bf16[200,128]{1,0:T(8,128)(2,1)S(1)} collective-permute-done((bf16[200,128]{1,0:T(8,128)(2,1)S(1)}, bf16[200,128]{1,0:T(8,128)(2,1)S(1)}, u32[]{:S(2)}, u32[]{:S(2)}) %collective-permute-start.2) | collective-permute-done | bytes 51232 | tf_op jit(solution)/shard_map/ppermute | solution.py:409
  25.9 11.0 %shard_map.139 = (bf16[200,8,128]{2,1,0:T(8,128)(2,1)}, bf16[8,200,128]{2,1,0:T(8,128)(2,1)S(1)}, bf16[3,200,128]{2,1,0:T(8,128)(2,1)S(1)}, bf16[3,200,128]{2,1,...) custom-call(f32[8,256]{1,0:T(8,128)S(1)} %select_convert_fusion.place_ref, ...), custom_call_target="tpu_custom_call" | custom-call | flops 12000000000 | bytes 36000000 | tf_op jit(solution)/shard_map/pallas_call | solution.py:460
  36.9 3.1 %collective-permute-start.6 = (bf16[3,200,128]{2,1,0:T(8,128)(2,1)S(1)}, bf16[3,200,128]{2,1,0:T(8,128)(2,1)S(1)}, u32[]{:S(2)}, u32[]{:S(2)}) collective-permute-start(bf16[3,200,128]{2,1,0:T(8,128)(2,1)S(1)} %get-tuple-element.49), channel_id=1, source_target_pairs={{0,1},{1,2},{2,3},{3,4},{4,5},{5,6},{6,7},{7,8},{8,9},{9,10},{10,1... | collective-permute-start | bytes 460808 | tf_op jit(solution)/shard_map/ppermute | solution.py:409
  40.1 1.0 %collective-permute-start.7 = (bf16[3,200,128]{2,1,0:T(8,128)(2,1)S(1)}, bf16[3,200,128]{2,1,0:T(8,128)(2,1)S(1)}, u32[]{:S(2)}, u32[]{:S(2)}) collective-permute-start(bf16[3,200,128]{2,1,0:T(8,128)(2,1)S(1)} %get-tuple-element.50), channel_id=1, source_target_pairs={{1,0},{2,1},{3,2},{4,3},{5,4},{6,5},{7,6},{8,7},{9,8},{10,9},{11,1... | collective-permute-start | bytes 460808 | tf_op jit(solution)/shard_map/ppermute | solution.py:409
  41.1 3.9 %collective-permute-start.4 = (bf16[800,208]{1,0:T(8,128)(2,1)S(1)}, bf16[800,208]{1,0:T(8,128)(2,1)S(1)}, u32[]{:S(2)}, u32[]{:S(2)}) collective-permute-start(bf16[800,208]{1,0:T(8,128)(2,1)S(1)} %get-tuple-element.44), channel_id=1, source_target_pairs={{0,1},{1,0},{2,3},{3,2},{4,5},{5,4},{6,7},{7,6},{8,9},{9,8},{10,11... | collective-permute-start | bytes 998408 | tf_op jit(solution)/shard_map/ppermute | solution.py:500
  44.9 4.6 %shard_map.140 = (f32[32,208]{1,0:T(8,128)S(1)}, bf16[32,208]{1,0:T(8,128)(2,1)S(1)}) custom-call(f32[8,256]{1,0:T(8,128)S(1)} %select_convert_fusion.place_ref, bf16[8,200,128]{2,1,0:T(8,128)(2,1)S(1)} %get-tuple-element.34.mid_ref.m_ref, bf16[3,200,128]{2,1,0:T(8,128)(2,1)S(1)} %collective-permute-done.up_ref, ...), custom_call_target="tpu_custom_call" | custom-call | flops 6000000000 | bytes 18000000 | tf_op jit(solution)/shard_map/pallas_call | solution.py:502
  49.8 0.3 shard_map.142
  50.2 1.5 %collective-permute-start.8 = (bf16[200,128]{1,0:T(8,128)(2,1)S(1)}, bf16[200,128]{1,0:T(8,128)(2,1)S(1)}, u32[]{:S(2)}, u32[]{:S(2)}) collective-permute-start(bf16[200,128]{1,0:T(8,128)(2,1)S(1)} %shard_map.142), channel_id=1, source_target_pairs={{0,16},{16,32},{32,48},{48,64},{64,80},{80,96},{96,112},{112,128},... | collective-permute-start | bytes 153608 | tf_op jit(solution)/shard_map/ppermute | solution.py:409
  51.6 1.1 %shard_map.141 = bf16[16,80,208]{2,1,0:T(8,128)(2,1)} custom-call(f32[800,208]{1,0:T(8,128)S(1)} %get-tuple-element.43.own_ref, bf16[800,208]{1,0:T(8,128)(2,1)S(1)} %collective-permute-done.4.got_ref, f32[32,208]{1,0:T(8,128)S(1)} %get-tuple-element.47.taps_ref, bf16[32,208]{1,0:T(8,128)(2,1)S(1)} %collective-permute-done.5.taps_got_ref), custom_call_target="tpu_custom_call" | custom-call | flops 1000000000 | bytes 3000000 | tf_op jit(solution)/shard_map/pallas_call | solution.py:510
  52.7 0.4 collective-permute-done.9.right_ref
  53.1 3.7 %collective-permute-done.8.left_ref = bf16[200,128]{1,0:T(8,128)(2,1)S(1)} collective-permute-done((bf16[200,128]{1,0:T(8,128)(2,1)S(1)}, bf16[200,128]{1,0:T(8,128)(2,1)S(1)}, u32[]{:S(2)}, u32[]{:S(2)}) %collective-permute-start.8) | collective-permute-done | bytes 51232 | tf_op jit(solution)/shard_map/ppermute | solution.py:409
  56.8 3.6 %all-to-all-start = ((bf16[16,80,208]{2,1,0:T(8,128)(2,1)}), bf16[16,80,208]{2,1,0:T(8,128)(2,1)S(1)}, u32[]{:S(2)}, u32[]{:S(2)}) async-start(bf16[16,80,208]{2,1,0:T(8,128)(2,1)} %shard_map.141), calls=%async_computation | async-start | bytes 1310720 | tf_op jit(solution)/shard_map/all_to_all | solution.py:522
  60.4 2.4 %copy-done.7 = f32[49,200,128]{2,1,0:T(8,128)S(1)} copy-done((f32[49,200,128]{2,1,0:T(8,128)S(1)}, f32[49,200,128]{2,1,0:T(8,128)}, u32[]{:S(2)}) %copy-start.7) | copy-done | bytes 5017624
  62.8 5.5 %shard_map.143 = bf16[200,8,128]{2,1,0:T(8,128)(2,1)} custom-call(f32[8,256]{1,0:T(8,128)S(1)} %select_convert_fusion.place_ref, bf16[8,200,128]{2,1,0:T(8,128)(2,1)S(1)} %get-tuple-element.45.bm_ref.mid_ref, bf16[3,200,128]{2,1,0:T(8,128)(2,1)S(1)} %collective-permute-done.6.up_ref, bf16[3,200,128]{2,1,0:T(8,128)(2,1)S(1)} %collective-permute-done.7.down_ref, ...), custom_call_target="tpu_custom_call" | custom-call | flops 8000000000 | bytes 24000000 | tf_op jit(solution)/shard_map/pallas_call | solution.py:523
  68.3 9.6 %all-to-all-done.parts_ref = bf16[16,80,208]{2,1,0:T(8,128)(2,1)S(1)} async-done(((bf16[16,80,208]{2,1,0:T(8,128)(2,1)}), bf16[16,80,208]{2,1,0:T(8,128)(2,1)S(1)}, u32[]{:S(2)}, u32[]{:S(2)}) %all-to-all-start) | async-done | bytes 532512 | tf_op jit(solution)/shard_map/all_to_all | solution.py:522
  78.0 11.1 %all_to_all.10.parts_ref = bf16[8,80,208]{2,1,0:T(8,128)(2,1)S(1)} all-to-all(bf16[8,80,208]{2,1,0:T(8,128)(2,1)S(1)} %shard_map.144), channel_id=1, replica_groups={{0,2,4,6,8,10,12,14},{1,3,5,7,9,11,13,15},{16,18,20,22,24,26,28,30},{17..., dimensions={0} | all-to-all | bytes 532480 | tf_op jit(solution)/shard_map/all_to_all | solution.py:533
  89.2 2.5 %collective-permute-start.10 = (bf16[80,208]{1,0:T(8,128)(2,1)S(1)}, bf16[80,208]{1,0:T(8,128)(2,1)S(1)}, u32[]{:S(2)}, u32[]{:S(2)}) collective-permute-start(bf16[80,208]{1,0:T(8,128)(2,1)S(1)} %shard_map.145.own_ref), channel_id=1, source_target_pairs={{0,1},{1,0},{2,3},{3,2},{4,5},{5,4},{6,7},{7,6},{8,9},{9,8},{10,11... | collective-permute-start | bytes 99848 | tf_op jit(solution)/shard_map/ppermute | solution.py:535
  91.6 0.9 collective-permute-done.10.got_ref
  92.5 0.7 shard_map.146
  (27 shorter events, 0.6 us)
Async XLA Ops:
  0.6 1.0 %copy-start = (bf16[200,8,128]{2,1,0:T(8,128)(2,1)S(1)}, bf16[200,8,128]{2,1,0:T(8,128)(2,1)}, u32[]{:S(2)}) copy-start(bf16[200,8,128]{2,1,0:T(8,128)(2,1)} %x_hbm.1) | copy-start | bytes 1228804
  1.6 0.7 copy-start.3
  2.3 7.3 %copy-start.2 = (bf16[49,200]{1,0:T(8,128)(2,1)S(1)}, bf16[49,200]{1,0:T(8,128)(2,1)}, u32[]{:S(2)}) copy-start(bf16[49,200]{1,0:T(8,128)(2,1)} %taps_ref.1) | copy-start | bytes 58804
  2.3 7.3 %copy-start.5 = (f32[200]{0:T(256)S(1)}, f32[200]{0:T(256)}, u32[]{:S(2)}) copy-start(f32[200]{0:T(256)} %param.11) | copy-start | bytes 2404
  3.2 8.3 %collective-permute-start = (bf16[3,200,128]{2,1,0:T(8,128)(2,1)S(1)}, bf16[3,200,128]{2,1,0:T(8,128)(2,1)S(1)}, u32[]{:S(2)}, u32[]{:S(2)}) collective-permute-start(bf16[3,200,128]{2,1,0:T(8,128)(2,1)S(1)} %get-tuple-element.35), channel_id=1, source_target_pairs={{0,1},{1,2},{2,3},{3,4},{4,5},{5,6},{6,7},{7,8},{8,9},{9,10},{10,1... | collective-permute-start | bytes 460808 | tf_op jit(solution)/shard_map/ppermute | solution.py:409
  5.8 5.6 %collective-permute-start.1 = (bf16[3,200,128]{2,1,0:T(8,128)(2,1)S(1)}, bf16[3,200,128]{2,1,0:T(8,128)(2,1)S(1)}, u32[]{:S(2)}, u32[]{:S(2)}) collective-permute-start(bf16[3,200,128]{2,1,0:T(8,128)(2,1)S(1)} %get-tuple-element.36), channel_id=1, source_target_pairs={{1,0},{2,1},{3,2},{4,3},{5,4},{6,5},{7,6},{8,7},{9,8},{10,9},{11,1... | collective-permute-start | bytes 460808 | tf_op jit(solution)/shard_map/ppermute | solution.py:409
  9.6 9.7 %copy-start.1 = (bf16[200,8,128]{2,1,0:T(8,128)(2,1)S(1)}, bf16[200,8,128]{2,1,0:T(8,128)(2,1)}, u32[]{:S(2)}) copy-start(bf16[200,8,128]{2,1,0:T(8,128)(2,1)} %cot_hbm.1) | copy-start | bytes 1228804
  9.6 9.7 %copy-start.4 = (s32[8,128]{1,0:T(8,128)S(1)}, s32[8,128]{1,0:T(8,128)}, u32[]{:S(2)}) copy-start(s32[8,128]{1,0:T(8,128)} %mask_ref.3) | copy-start | bytes 12292
  11.4 25.6 %copy-start.6 = (f32[49,200,128]{2,1,0:T(8,128)}, f32[49,200,128]{2,1,0:T(8,128)S(1)}, u32[]{:S(2)}) copy-start(f32[49,200,128]{2,1,0:T(8,128)S(1)} %get-tuple-element.37.spread_ref) | copy-start | bytes 15052804
  11.7 8.8 %collective-permute-start.3 = (bf16[200,128]{1,0:T(8,128)(2,1)S(1)}, bf16[200,128]{1,0:T(8,128)(2,1)S(1)}, u32[]{:S(2)}, u32[]{:S(2)}) collective-permute-start(bf16[200,128]{1,0:T(8,128)(2,1)S(1)} %shard_map.136), channel_id=1, source_target_pairs={{16,0},{32,16},{48,32},{64,48},{80,64},{96,80},{112,96},{128,112},... | collective-permute-start | bytes 153608 | tf_op jit(solution)/shard_map/ppermute | solution.py:409
  19.3 6.6 %collective-permute-start.2 = (bf16[200,128]{1,0:T(8,128)(2,1)S(1)}, bf16[200,128]{1,0:T(8,128)(2,1)S(1)}, u32[]{:S(2)}, u32[]{:S(2)}) collective-permute-start(bf16[200,128]{1,0:T(8,128)(2,1)S(1)} %shard_map.136), channel_id=1, source_target_pairs={{0,16},{16,32},{32,48},{48,64},{64,80},{80,96},{96,112},{112,128},... | collective-permute-start | bytes 153608 | tf_op jit(solution)/shard_map/ppermute | solution.py:409
  36.9 12.8 %collective-permute-start.6 = (bf16[3,200,128]{2,1,0:T(8,128)(2,1)S(1)}, bf16[3,200,128]{2,1,0:T(8,128)(2,1)S(1)}, u32[]{:S(2)}, u32[]{:S(2)}) collective-permute-start(bf16[3,200,128]{2,1,0:T(8,128)(2,1)S(1)} %get-tuple-element.49), channel_id=1, source_target_pairs={{0,1},{1,2},{2,3},{3,4},{4,5},{5,6},{6,7},{7,8},{8,9},{9,10},{10,1... | collective-permute-start | bytes 460808 | tf_op jit(solution)/shard_map/ppermute | solution.py:409
  40.1 9.7 %collective-permute-start.7 = (bf16[3,200,128]{2,1,0:T(8,128)(2,1)S(1)}, bf16[3,200,128]{2,1,0:T(8,128)(2,1)S(1)}, u32[]{:S(2)}, u32[]{:S(2)}) collective-permute-start(bf16[3,200,128]{2,1,0:T(8,128)(2,1)S(1)} %get-tuple-element.50), channel_id=1, source_target_pairs={{1,0},{2,1},{3,2},{4,3},{5,4},{6,5},{7,6},{8,7},{9,8},{10,9},{11,1... | collective-permute-start | bytes 460808 | tf_op jit(solution)/shard_map/ppermute | solution.py:409
  41.1 10.5 %collective-permute-start.4 = (bf16[800,208]{1,0:T(8,128)(2,1)S(1)}, bf16[800,208]{1,0:T(8,128)(2,1)S(1)}, u32[]{:S(2)}, u32[]{:S(2)}) collective-permute-start(bf16[800,208]{1,0:T(8,128)(2,1)S(1)} %get-tuple-element.44), channel_id=1, source_target_pairs={{0,1},{1,0},{2,3},{3,2},{4,5},{5,4},{6,7},{7,6},{8,9},{9,8},{10,11... | collective-permute-start | bytes 998408 | tf_op jit(solution)/shard_map/ppermute | solution.py:500
  49.5 2.1 %collective-permute-start.5 = (bf16[32,208]{1,0:T(8,128)(2,1)S(1)}, bf16[32,208]{1,0:T(8,128)(2,1)S(1)}, u32[]{:S(2)}, u32[]{:S(2)}) collective-permute-start(bf16[32,208]{1,0:T(8,128)(2,1)S(1)} %get-tuple-element.48), channel_id=1, source_target_pairs={{0,1},{1,0},{2,3},{3,2},{4,5},{5,4},{6,7},{7,6},{8,9},{9,8},{10,11... | collective-permute-start | bytes 39944 | tf_op jit(solution)/shard_map/ppermute | solution.py:509
  50.1 3.0 %collective-permute-start.9 = (bf16[200,128]{1,0:T(8,128)(2,1)S(1)}, bf16[200,128]{1,0:T(8,128)(2,1)S(1)}, u32[]{:S(2)}, u32[]{:S(2)}) collective-permute-start(bf16[200,128]{1,0:T(8,128)(2,1)S(1)} %shard_map.142), channel_id=1, source_target_pairs={{16,0},{32,16},{48,32},{64,48},{80,64},{96,80},{112,96},{128,112},... | collective-permute-start | bytes 153608 | tf_op jit(solution)/shard_map/ppermute | solution.py:409
  50.2 6.7 %collective-permute-start.8 = (bf16[200,128]{1,0:T(8,128)(2,1)S(1)}, bf16[200,128]{1,0:T(8,128)(2,1)S(1)}, u32[]{:S(2)}, u32[]{:S(2)}) collective-permute-start(bf16[200,128]{1,0:T(8,128)(2,1)S(1)} %shard_map.142), channel_id=1, source_target_pairs={{0,16},{16,32},{32,48},{48,64},{64,80},{80,96},{96,112},{112,128},... | collective-permute-start | bytes 153608 | tf_op jit(solution)/shard_map/ppermute | solution.py:409
  56.8 21.1 %all-to-all-start = ((bf16[16,80,208]{2,1,0:T(8,128)(2,1)}), bf16[16,80,208]{2,1,0:T(8,128)(2,1)S(1)}, u32[]{:S(2)}, u32[]{:S(2)}) async-start(bf16[16,80,208]{2,1,0:T(8,128)(2,1)} %shard_map.141), calls=%async_computation | async-start | bytes 1310720 | tf_op jit(solution)/shard_map/all_to_all | solution.py:522
  60.4 2.4 %copy-start.7 = (f32[49,200,128]{2,1,0:T(8,128)S(1)}, f32[49,200,128]{2,1,0:T(8,128)}, u32[]{:S(2)}) copy-start(f32[49,200,128]{2,1,0:T(8,128)} %copy-done.6) | copy-start | bytes 15052804
  89.2 3.3 %collective-permute-start.10 = (bf16[80,208]{1,0:T(8,128)(2,1)S(1)}, bf16[80,208]{1,0:T(8,128)(2,1)S(1)}, u32[]{:S(2)}, u32[]{:S(2)}) collective-permute-start(bf16[80,208]{1,0:T(8,128)(2,1)S(1)} %shard_map.145.own_ref), channel_id=1, source_target_pairs={{0,1},{1,0},{2,3},{3,2},{4,5},{5,4},{6,7},{7,6},{8,9},{9,8},{10,11... | collective-permute-start | bytes 99848 | tf_op jit(solution)/shard_map/ppermute | solution.py:535

commit v3 on v2

v3 whole, which is shorter than its diff:
```python
import functools

import jax
import jax.numpy as jnp
from jax import lax
from jax.experimental import pallas as pl
from jax.experimental.pallas import tpu as pltpu
from jax.sharding import PartitionSpec as P

EPS = 1e-06
BF = jnp.bfloat16
F32 = jnp.float32
HALO = 3
TAPS = 7
HALF_TAPS = 25
WHOLE_ROWS = 13
CUT_ROWS = 12
SPARE_LANE = 204
VMEM_BYTES = 16 * 1024 * 1024


def kernel_call(body, outs, scratch=(), n_in=0, n_any=0, micros=1):
    specs = [pl.BlockSpec(memory_space=pltpu.HBM)] * n_any
    specs += [pl.BlockSpec(memory_space=pltpu.VMEM)] * n_in
    return pl.pallas_call(
        body,
        out_shape=[jax.ShapeDtypeStruct(shape, dtype) for shape, dtype in outs],
        in_specs=specs,
        out_specs=[pl.BlockSpec(memory_space=pltpu.VMEM)] * len(outs),
        scratch_shapes=list(scratch),
        compiler_params=pltpu.CompilerParams(vmem_limit_bytes=VMEM_BYTES),
        cost_estimate=pl.CostEstimate(
            flops=micros * 1_000_000_000, bytes_accessed=micros * 3_000_000, transcendentals=0
        ),
    )


def nt_dot(left, right):
    return lax.dot_general(left, right, (((1,), (1,)), ((), ())), preferred_element_type=F32)


def tn_dot(left, right):
    return lax.dot_general(left, right, (((0,), (0,)), ((), ())), preferred_element_type=F32)


def dot(left, right):
    return jnp.dot(left, right, preferred_element_type=F32)


def by_rows(field_ref, flat):
    channels, rows, lanes = field_ref.shape
    flat[...] = field_ref[...].astype(F32).reshape(channels * rows, lanes)
    return [flat[pl.ds(row, channels, stride=rows), :] for row in range(rows)]


def state_body(x_ref, place_ref, m_ref, near_ref, far_ref, flat):
    masked = by_rows(x_ref, flat)
    for row, value in enumerate(masked):
        m_ref[row] = value.astype(BF)
    send_edges(place_ref, masked, near_ref, far_ref)


def send_edges(place_ref, values, near_ref, far_ref):
    first = is_first(place_ref, values[0].shape)
    for r in range(HALO):
        top, bottom = values[r], values[len(values) - HALO + r]
        near_ref[r] = jnp.where(first, bottom, top).astype(BF)
        far_ref[r] = jnp.where(first, top, bottom).astype(BF)


def gated_body(cot_ref, g_ref, flat):
    for row, value in enumerate(by_rows(cot_ref, flat)):
        g_ref[row] = value.astype(BF)


def spread_body(taps_ref, spread_ref):
    count, channels, lanes = spread_ref.shape
    unit = lax.broadcasted_iota(jnp.int32, (count, lanes), 0)
    unit = unit == lax.broadcasted_iota(jnp.int32, (count, lanes), 1)
    taps = tn_dot(taps_ref[...], jnp.where(unit, 1.0, 0.0).astype(BF))
    for tap in range(count):
        spread_ref[tap] = jnp.broadcast_to(taps[:, tap : tap + 1], (channels, lanes))


def columns(row, lanes):
    high = row.astype(BF)
    rest = row - high.astype(F32)
    middle = rest.astype(BF)
    low = (rest - middle.astype(F32)).astype(BF)
    spare = jnp.zeros((5, row.shape[1]), F32)
    parts = [high.astype(F32), middle.astype(F32), low.astype(F32), spare]
    parts = jnp.concatenate(parts, axis=0).astype(BF)
    return tn_dot(parts, jnp.ones((8, lanes), BF))


def weights_body(
    taps_ref, gain_ref, bias_ref, we_in_ref, wp_in_ref, spread_ref, gains_ref, biases_ref, we_ref, wp_ref
):
    count, channels, lanes = spread_ref.shape
    spread_body(taps_ref, spread_ref)
    gains_ref[...] = columns(gain_ref[...].reshape(1, channels), lanes)
    biases_ref[...] = columns(bias_ref[...].reshape(1, bias_ref.shape[0]), lanes)
    we_ref[...] = we_in_ref[...].astype(F32).T.astype(BF)
    wp_ref[...] = wp_in_ref[...].astype(F32).T.astype(BF)


def flag(place_ref, row, shape):
    return jnp.broadcast_to(place_ref[row : row + 1, : shape[1]], shape) > 0.0


def is_first(place_ref, shape):
    return flag(place_ref, 0, shape)


def extended_rows(place_ref, mid_ref, near_ref, far_ref):
    shape = mid_ref.shape[1:]
    first = is_first(place_ref, shape)
    has_up = jnp.broadcast_to(place_ref[1:2, : shape[1]], shape) > 0.0
    has_down = jnp.broadcast_to(place_ref[2:3, : shape[1]], shape) > 0.0
    near = [near_ref[r].astype(F32) for r in range(HALO)]
    far = [far_ref[r].astype(F32) for r in range(HALO)]
    for r in range(HALO):
        yield jnp.where(has_up, jnp.where(first, far[r], near[r]), 0.0)
    for r in range(mid_ref.shape[0]):
        yield mid_ref[r].astype(F32)
    for r in range(HALO):
        yield jnp.where(has_down, jnp.where(first, near[r], far[r]), 0.0)


def pack_body(place_ref, mid_ref, near_ref, far_ref, out_ref):
    channels, lanes = out_ref.shape
    lane = lax.broadcasted_iota(jnp.int32, (channels, lanes), 1)
    packed = jnp.zeros((channels, lanes), F32)
    for r, value in enumerate(extended_rows(place_ref, mid_ref, near_ref, far_ref)):
        if r:
            value = pltpu.roll(value, 8 * r, 1)
        packed = jnp.where(((lane + (HALO - 8 * r)) & (lanes - 1)) < 2 * HALO, value, packed)
    out_ref[...] = packed.astype(BF)


def fill_extended(ext, edge, place_ref, mid_ref, near_ref, far_ref, lon_near_ref, lon_far_ref):
    for r, value in enumerate(extended_rows(place_ref, mid_ref, near_ref, far_ref)):
        ext[r] = value
    shape = edge.shape
    lane = lax.broadcasted_iota(jnp.int32, shape, 1)
    side = jnp.where((lane & 7) >= 4, 1.0, 0.0)
    near_is_right = jnp.broadcast_to(place_ref[3:4, : shape[1]], shape)
    near = lon_near_ref[...].astype(F32)
    edge[...] = jnp.where(side != near_is_right, near, lon_far_ref[...].astype(F32))


def joined(ext, edge, start):
    n_rows, _, lanes = ext.shape
    mid = ext[:, pl.ds(start, 8), :]
    ends = edge[pl.ds(start, 8), :]
    wings = jnp.stack(
        [ends] + [pltpu.roll(ends, lanes - 8 * r, 1) for r in range(1, n_rows)], axis=0
    )
    lane = lax.broadcasted_iota(jnp.int32, (8, lanes), 1)
    for shift in range(-HALO, HALO + 1):
        if shift == 0:
            yield shift, mid
            continue
        outside = lane < shift if shift > 0 else lane >= lanes + shift
        yield shift, jnp.where(outside[None], wings, mid)


def convolve(ext, edge, spread_ref, start, rows, flipped):
    lanes = ext.shape[2]
    total = jnp.zeros((rows, 8, lanes), F32)
    for b, (shift, value) in enumerate(joined(ext, edge, start)):
        window = pltpu.roll(value, -shift % lanes, 2) if shift else value
        for a in range(TAPS):
            tap = a * TAPS + b
            if flipped:
                tap = TAPS * TAPS - 1 - tap
            total = total + spread_ref[tap, pl.ds(start, 8), :][None] * window[a : a + rows]
    return total


def main_body(
    place_ref,
    m_ref,
    near_ref,
    far_ref,
    lon_near_ref,
    lon_far_ref,
    mask_ref,
    g_ref,
    spread_ref,
    gains_ref,
    biases_ref,
    we_ref,
    wp_ref,
    we_t_ref,
    wp_t_ref,
    next_ref,
    bm_ref,
    bnear_ref,
    bfar_ref,
    gain_ref,
    own_ref,
    other_ref,
    ext,
    edge,
    mixed,
    units,
    sides,
    flat,
):
    rows, channels, lanes = m_ref.shape
    hidden, deep = own_ref.shape
    chunk = hidden // 5
    pair = 2 * lanes
    fill_extended(ext, edge, place_ref, m_ref, near_ref, far_ref, lon_near_ref, lon_far_ref)

    def conv_step(block, carry):
        start = pl.multiple_of(block * 8, 8)
        mixed[:, pl.ds(start, 8), :] = convolve(ext, edge, spread_ref, start, rows, False)
        return carry

    lax.fori_loop(0, channels // 8, conv_step, 0, unroll=5)
    for r in range(rows):
        sides[1, :, r * lanes : (r + 1) * lanes] = jnp.concatenate(
            [g_ref[r].astype(F32), jnp.zeros((deep - channels, lanes), F32)], axis=0
        ).astype(BF)
    gain_ref[...] = jnp.zeros_like(gain_ref)
    tail_row = lax.broadcasted_iota(jnp.int32, (deep - channels, pair), 0)
    ones_rows = jnp.where(tail_row == 0, 1.0, 0.0)

    def pair_step(p, carry):
        cells = pl.ds(pl.multiple_of(p * pair, pair), pair)
        value = jnp.concatenate([mixed[2 * p], mixed[2 * p + 1]], axis=1)
        gain = jnp.concatenate([gains_ref[...]] * 2, axis=1)
        center = jnp.sum(value, axis=0, keepdims=True) * (1.0 / channels)
        centered = value - center
        spread = jnp.sum(centered * centered, axis=0, keepdims=True) * (1.0 / channels)
        inv_spread = lax.rsqrt(spread + EPS)
        whitened = centered * inv_spread
        normed = whitened * gain
        sides[0, :, cells] = jnp.concatenate([normed, ones_rows], axis=0).astype(BF)
        normed = normed.astype(BF)
        gated = jnp.concatenate([g_ref[2 * p], g_ref[2 * p + 1]], axis=1)
        for c in range(hidden // chunk):
            part = pl.ds(c * chunk, chunk)
            bias = biases_ref[part, :]
            inner = dot(we_ref[part, :], normed) + jnp.concatenate([bias, bias], axis=1)
            back_act = dot(wp_ref[part, :], gated)
            normal_cdf = 0.5 * (1.0 + lax.erf(inner * 0.7071067811865476))
            density = jnp.exp(-0.5 * inner * inner) * 0.3989422804014327
            units[1, part, cells] = (inner * normal_cdf).astype(BF)
            units[0, part, cells] = (back_act * (normal_cdf + inner * density)).astype(BF)
        branch = dot(wp_t_ref[...], units[1, :, cells])
        back_norm = dot(we_t_ref[...], units[0, :, cells])
        gain_term = back_norm * whitened
        gain_ref[...] += gain_term[:, :lanes] + gain_term[:, lanes:]
        scaled = back_norm * gain
        mean_scaled = jnp.sum(scaled, axis=0, keepdims=True) * (1.0 / channels)
        mean_product = jnp.sum(scaled * whitened, axis=0, keepdims=True) * (1.0 / channels)
        back_mixed = (inv_spread * (scaled - mean_scaled - whitened * mean_product)).astype(BF)
        for k in range(2):
            r = 2 * p + k
            mask = mask_ref[pl.ds(r, 1), :].astype(F32)
            here = slice(k * lanes, (k + 1) * lanes)
            flat[pl.ds(r, channels, stride=rows), :] = ext[r + HALO] + mask * branch[:, here]
            bm_ref[r] = back_mixed[:, here]
        return carry

    lax.fori_loop(0, rows // 2, pair_step, 0)
    next_ref[...] = flat[...].reshape(channels, rows, lanes).astype(BF)
    send_edges(place_ref, [bm_ref[r].astype(F32) for r in range(rows)], bnear_ref, bfar_ref)
    core = lax.axis_index("lat") % 2
    for out, which in ((own_ref, core), (other_ref, 1 - core)):
        for c in range(hidden // chunk):
            part = slice(c * chunk, (c + 1) * chunk)
            out[part, :] = nt_dot(units[which, part, :], sides[which]).astype(out.dtype)


def taps_body(
    place_ref,
    m_ref,
    near_ref,
    far_ref,
    lon_near_ref,
    lon_far_ref,
    bm_ref,
    gain_ref,
    own_ref,
    other_ref,
    ext,
    edge,
    upstream,
    sums,
    moved,
):
    rows, channels, lanes = m_ref.shape
    fill_extended(ext, edge, place_ref, m_ref, near_ref, far_ref, lon_near_ref, lon_far_ref)
    for r in range(rows):
        upstream[r] = bm_ref[r].astype(F32)
    lane = lax.broadcasted_iota(jnp.int32, (8, lanes), 1)
    ones = jnp.ones((lanes, lanes), BF)

    def step(block, carry):
        start = pl.multiple_of(block * 8, 8)
        back = upstream[:, pl.ds(start, 8), :]
        result = jnp.zeros((8, lanes), F32)
        for b, (shift, value) in enumerate(joined(ext, edge, start)):
            turned = pltpu.roll(back, shift % lanes, 2) if shift else back
            terms = [jnp.sum(turned * value[a : a + rows], axis=0) for a in range(TAPS)]
            terms.append(gain_ref[pl.ds(start, 8), :])
            totals = dot(jnp.concatenate(terms, axis=0).astype(BF), ones)
            for a in range(TAPS):
                result = jnp.where(lane == a * TAPS + b, totals[8 * a : 8 * a + 8], result)
        result = jnp.where(lane == TAPS * TAPS, totals[8 * TAPS :], result)
        sums[pl.ds(start, 8), :] = result
        return carry

    lax.fori_loop(0, channels // 8, step, 0, unroll=5)
    block, wide = own_ref.shape
    row = lax.broadcasted_iota(jnp.int32, (2 * block, lanes), 0)
    col = lax.broadcasted_iota(jnp.int32, (2 * block, lanes), 1)
    second, inside = row // block, row % block

    def picked(first_row, first_tap, count):
        tap = inside - first_row + first_tap + second * HALF_TAPS
        pick = (col == tap) & (inside >= first_row) & (inside < first_row + count)
        return nt_dot(jnp.where(pick, 1.0, 0.0).astype(BF), moved[...].astype(BF))

    moved[...] = jnp.zeros_like(moved)
    moved[:channels, :] = sums[...]
    turned = picked(block - 1 - WHOLE_ROWS, 0, WHOLE_ROWS)
    moved[...] = jnp.zeros_like(moved)
    cut = channels // 4
    for q in range(4):
        moved[SPARE_LANE : SPARE_LANE + cut, :] = sums[q * cut : (q + 1) * cut, :]
        turned = turned + picked(q * CUT_ROWS, WHOLE_ROWS, CUT_ROWS)
    first = is_first(place_ref, (block, wide))
    own_ref[...] = jnp.where(first, turned[:block], turned[block:])
    other_ref[...] = jnp.where(first, turned[block:], turned[:block]).astype(BF)


def message_body(own_ref, got_ref, taps_ref, taps_got_ref, out_ref, total, taps, piece):
    hidden, deep = own_ref.shape
    share = hidden // out_ref.shape[0]
    total[...] = own_ref[...] + got_ref[...].astype(F32)
    taps[...] = taps_ref[...] + taps_got_ref[...].astype(F32)
    piece[...] = taps[...]
    for k in range(out_ref.shape[0]):
        rows = total[k * share : (k + 1) * share, :]
        piece[:share, :deep] = rows + taps[:share, :deep]
        out_ref[k] = piece[...].astype(BF)


def sum_body(parts_ref, out_ref):
    total = parts_ref[0].astype(F32)
    for k in range(1, parts_ref.shape[0]):
        total = total + parts_ref[k].astype(F32)
    total = total.astype(BF)
    for k in range(out_ref.shape[0]):
        out_ref[k] = total


def final_body(parts_ref, ge_ref, gp_ref, gk_ref, gg_ref, gb_ref, halves):
    share, channels = ge_ref.shape
    _, depth, wide = parts_ref.shape
    for k in range(2):
        total = parts_ref[k].astype(F32)
        for j in range(k + 2, parts_ref.shape[0], 2):
            total = total + parts_ref[j].astype(F32)
        halves[k] = total
    ge_ref[...] = halves[0, :share, :channels]
    gp_ref[...] = halves[1, :share, :channels]
    cut = channels // 4
    lane = lax.broadcasted_iota(jnp.int32, (16, wide), 1)
    for k in range(2):
        start = k * HALF_TAPS
        whole = depth - 1 - WHOLE_ROWS
        gk_ref[start : start + WHOLE_ROWS, :] = halves[k, whole : depth - 1, :channels]
        rest = jnp.zeros((16, wide), F32)
        for q in range(4):
            value = halves[k, q * CUT_ROWS : q * CUT_ROWS + 16, :]
            value = pltpu.roll(value, (q * cut - SPARE_LANE) % wide, 1)
            rest = jnp.where((lane >= q * cut) & (lane < (q + 1) * cut), value, rest)
        count = min(CUT_ROWS, TAPS * TAPS - start - WHOLE_ROWS)
        start = start + WHOLE_ROWS
        gk_ref[start : start + count, :] = rest[:count, :channels]
    gg_ref[...] = rest[CUT_ROWS - 1 : CUT_ROWS, :channels]
    pick = lax.broadcasted_iota(jnp.int32, (8, wide), 1) == channels
    pick = jnp.where(pick, 1.0, 0.0).astype(BF)
    high = halves[0].astype(BF)
    low = (halves[0] - high.astype(F32)).astype(BF)
    gb_ref[...] = (nt_dot(pick, high) + nt_dot(pick, low))[:1, :share]


def backward_body(
    place_ref,
    bm_ref,
    near_ref,
    far_ref,
    lon_near_ref,
    lon_far_ref,
    mask_ref,
    g_ref,
    taps_ref,
    out_ref,
    ext,
    edge,
    back,
    flat,
    spread,
):
    rows, channels, lanes = bm_ref.shape
    spread_body(taps_ref, spread)
    fill_extended(ext, edge, place_ref, bm_ref, near_ref, far_ref, lon_near_ref, lon_far_ref)

    def step(block, carry):
        start = pl.multiple_of(block * 8, 8)
        back[:, pl.ds(start, 8), :] = convolve(ext, edge, spread, start, rows, True)
        return carry

    lax.fori_loop(0, channels // 8, step, 0, unroll=5)
    for r in range(rows):
        mask = mask_ref[r : r + 1, :].astype(F32)
        flat[pl.ds(r, channels, stride=rows), :] = g_ref[r].astype(F32) + mask * back[r]
    out_ref[...] = flat[...].reshape(channels, rows, lanes).astype(BF)


def swap_lon(pack):
    size = lax.axis_size("lon")
    near = [(i, i ^ 1) for i in range(size)]
    far = [(i, ((i ^ 1) + (2 if i % 2 else -2)) % size) for i in range(size)]
    from_far = lax.ppermute(pack, "lon", far)
    return lax.ppermute(pack, "lon", near), from_far


def swap_lat(first, second):
    size = lax.axis_size("lat")
    near = [(i, i ^ 1) for i in range(size)]
    far = [(i, ((i ^ 1) + (2 if i % 2 else -2)) % size) for i in range(size)]
    return lax.ppermute(second, "lat", near), lax.ppermute(first, "lat", far)


def shards(
    ocean_state, land_sea, depth_kernel, norm_gain, w_expand, b_expand, w_project, cotangent
):
    channels, rows, lanes = ocean_state.shape
    hidden = w_expand.shape[0]
    n_lon, n_lat = lax.axis_size("lon"), lax.axis_size("lat")
    share = hidden // n_lon
    deep = -(-(channels + 3) // 16) * 16
    depth = share + WHOLE_ROWS + 1
    wide = 256
    cells = rows * lanes
    full = (rows, channels, lanes)
    edges = (HALO, channels, lanes)
    tile = (channels, lanes)
    flat = pltpu.VMEM((channels * rows, lanes), F32)
    ext_s = pltpu.VMEM((rows + 2 * HALO, channels, lanes), F32)
    edge_s = pltpu.VMEM(tile, F32)
    lat = lax.axis_index("lat")
    kind = lax.broadcasted_iota(jnp.int32, (8, 256), 0)
    value = jnp.where(kind == 0, 1 - lat % 2, jnp.where(kind == 1, lat, n_lat - 1 - lat))
    value = jnp.where(kind == 3, 1 - lax.axis_index("lon") % 2, value)
    place = jnp.where(kind == 4, 1 - lat // 2 % 2, value).astype(F32)
    swap = [(i, i ^ 1) for i in range(n_lat)]
    zero = jnp.zeros((), BF)
    masked, near, far = kernel_call(
        state_body, [(full, BF), (edges, BF), (edges, BF)], [flat], n_in=2
    )(jnp.where(land_sea[None] != 0, ocean_state, zero), place)
    near, far = swap_lat(far, near)
    (gated,) = kernel_call(gated_body, [(full, BF)], [flat], n_in=1)(
        jnp.where(land_sea[None] > 0, cotangent, zero)
    )
    (pack,) = kernel_call(pack_body, [(tile, BF)], n_in=4)(place, masked, near, far)
    later = (depth_kernel, norm_gain, b_expand, w_expand.T, w_project.T)
    pack, later = lax.optimization_barrier((pack, later))
    lon_near, lon_far = swap_lon(pack)
    spread, gains, biases, we, wp = kernel_call(
        weights_body,
        [
            ((TAPS * TAPS, *tile), F32),
            (tile, F32),
            ((hidden, lanes), F32),
            ((hidden, channels), BF),
            ((hidden, channels), BF),
        ],
        n_in=5,
        micros=3,
    )(*later)
    we_t, wp_t = later[3:]
    next_state, back_mixed, bnear, bfar, gain, own, other = kernel_call(
        main_body,
        [
            ((channels, rows, lanes), BF),
            (full, BF),
            (edges, BF),
            (edges, BF),
            (tile, F32),
            ((hidden, deep), F32),
            ((hidden, deep), BF),
        ],
        [
            ext_s,
            edge_s,
            pltpu.VMEM(full, F32),
            pltpu.VMEM((2, hidden, cells), BF),
            pltpu.VMEM((2, deep, cells), BF),
            flat,
        ],
        n_in=15,
        micros=12,
    )(
        place,
        masked,
        near,
        far,
        lon_near,
        lon_far,
        land_sea,
        gated,
        spread,
        gains,
        biases,
        we,
        wp,
        we_t,
        wp_t,
    )
    got = lax.ppermute(other, "lat", swap)
    bnear, bfar = swap_lat(bfar, bnear)
    taps_own, taps_other = kernel_call(
        taps_body,
        [((depth, wide), F32), ((depth, wide), BF)],
        [ext_s, edge_s, pltpu.VMEM(full, F32), edge_s, pltpu.VMEM((wide, lanes), F32)],
        n_in=8,
        micros=6,
    )(place, masked, near, far, lon_near, lon_far, back_mixed, gain)
    taps_got = lax.ppermute(taps_other, "lat", swap)
    (message,) = kernel_call(
        message_body,
        [((n_lon, depth, wide), BF)],
        [
            pltpu.VMEM((hidden, deep), F32),
            pltpu.VMEM((depth, wide), F32),
            pltpu.VMEM((depth, wide), F32),
        ],
        n_in=4,
    )(own, got, taps_own, taps_got)
    (back_pack,) = kernel_call(pack_body, [(tile, BF)], n_in=4)(
        place, back_mixed, bnear, bfar
    )
    blon_near, blon_far = swap_lon(back_pack)
    parts = lax.all_to_all(message, "lon", 0, 0)
    (copies,) = kernel_call(sum_body, [((n_lat, depth, wide), BF)], n_in=1)(parts)
    parts = lax.all_to_all(copies, "lat", 0, 0)
    (grad_state,) = kernel_call(
        backward_body,
        [((channels, rows, lanes), BF)],
        [ext_s, edge_s, pltpu.VMEM(full, F32), flat, pltpu.VMEM((TAPS * TAPS, *tile), F32)],
        n_in=9,
        micros=8,
    )(
        place, back_mixed, bnear, bfar, blon_near, blon_far, land_sea, gated, depth_kernel
    )
    parts, grad_state = lax.optimization_barrier((parts, grad_state))

    grad_expand, grad_project, grad_kernel, grad_gain, grad_bias = kernel_call(
        final_body,
        [
            ((share, channels), F32),
            ((share, channels), F32),
            ((TAPS * TAPS, channels), F32),
            ((1, channels), F32),
            ((1, share), F32),
        ],
        [pltpu.VMEM((2, depth, wide), F32)],
        n_in=1,
    )(parts)
    return (
        next_state,
        grad_state,
        grad_kernel,
        grad_gain.reshape(channels),
        grad_expand,
        grad_project,
        grad_bias.reshape(share),
    )


def solution(mesh):
    placed = (
        P(None, "lat", "lon"),
        P("lat", "lon"),
        P(),
        P(),
        P(),
        P(),
        P(),
        P(None, "lat", "lon"),
    )
    return jax.shard_map(
        shards,
        mesh=mesh,
        in_specs=placed,
        out_specs=(
            P(None, "lat", "lon"),
            P(None, "lat", "lon"),
            P(),
            P(),
            P("lon", None),
            P("lon", None),
            P("lon"),
        ),
        check_vma=False,
    )
```

time: 93.6 us -> 81.2 us (0.87)
  blocking collectives: 11.1 us -> 0 us
  local copies, waits for them, and re-layouts: 7.13 us -> 0.04 us
  starting transfers between devices: 26.9 us -> 30.4 us
  other arithmetic: 0.09 us -> 2.85 us
  waiting for transfers between devices: 20.3 us -> 17.8 us
  Pallas kernels: 26.9 us -> 28.8 us
    all_to_all x1 -> x0, blocking collectives: 11.1 us -> none  [shards(): parts = lax.all_to_all(copies, 'lat', 0, 0, axis_index_groups=groups)]
    all_to_all x0 -> x1, starting transfers between devices: none -> 6.64 us  [shards(): parts = lax.all_to_all(copies, 'lat', 0, 0)]
    unnamed x18 -> x12, local copies, waits for them, and re-layouts: 6.44 us -> 0.04 us
    all_to_all x1, waiting for transfers between devices: 9.59 us -> 4.08 us  [shards(): parts = lax.all_to_all(message, 'lon', 0, 0)]
    ppermute x9 -> x8, starting transfers between devices: 19.2 us -> 15.9 us  [the longest x2 12 us: swap_lon(): from_far = lax.ppermute(pack, 'lon', far)]
    all_to_all x0 -> x1, waiting for transfers between devices: none -> 2.73 us  [shards(): parts = lax.all_to_all(copies, 'lat', 0, 0)]
    select_n x0 -> x2, other arithmetic: none -> 2.07 us  [the longest x1 1.03 us: shards(): jnp.where(land_sea[None] != 0, ocean_state, zero)]
    pallas_call x1, Pallas kernels: 5.5 us -> 7.14 us  [shards(): kernel_call(backward_body, [((channels, rows, lanes), BF)], [ext_s, edge_...]
  transfers between devices with their start and end apart: 12 -> 12, of which waited for: 6 -> 7; matrix products, arithmetic and copies ran while one was open for 3% -> 1% of each run, Pallas kernels for 15% -> 19%
where the time goes in v3:
time: 81.2 us; the launch traced here: 80.8 us
  starting transfers between devices  30.4 us (37%)
  Pallas kernels  28.8 us (35%)
  waiting for transfers between devices  17.8 us (22%)
  other arithmetic  2.85 us (4%)
  between operations  0.88 us (1%)
    ppermute x2, starting transfers between devices, swap_lon(): from_far = lax.ppermute(pack, 'lon', far)  12 us
    pallas_call x1, Pallas kernels, shards(): kernel_call(main_body, [((channels, rows, lanes), BF), (full, BF), (edges...  11.2 us
    ppermute x4, waiting for transfers between devices, swap_lat(): return (lax.ppermute(second, 'lat', near), lax.ppermute(first, 'lat', far))  8.61 us
    pallas_call x1, Pallas kernels, shards(): kernel_call(backward_body, [((channels, rows, lanes), BF)], [ext_s, edge_...  7.14 us
    all_to_all x1, starting transfers between devices, shards(): parts = lax.all_to_all(copies, 'lat', 0, 0)  6.64 us
    all_to_all x1, starting transfers between devices, shards(): parts = lax.all_to_all(message, 'lon', 0, 0)  4.73 us
    pallas_call x1, Pallas kernels, shards(): kernel_call(taps_body, [((depth, wide), F32), ((depth, wide), BF)], [ext_...  4.71 us
    all_to_all x1, waiting for transfers between devices, shards(): parts = lax.all_to_all(message, 'lon', 0, 0)  4.08 us
  transfers between devices with their start and end apart: 12, of which 7 were waited for; matrix products, arithmetic and copies ran while one was open for 1% of the time, Pallas kernels for 19%

profile of v3, /device:TPU:1, one launch (start us, length us, event | category | flops | bytes accessed | tf_op | source)
XLA Modules:
  0.0 80.8 jit_solution(15794010289139236032)
XLA Ops:
  0.7 0.7 broadcast_compare_fusion
  1.4 1.0 %broadcast_select_fusion.1.x_ref = bf16[200,8,128]{2,1,0:T(8,128)(2,1)S(1)} fusion(bf16[200,8,128]{2,1,0:T(8,128)(2,1)} %param.8, pred[8,128]{1,0:T(8,128)(4,1)S(1)} %get-tuple-element.68), kind=kLoop, calls=%fused_computation.1 | loop fusion | flops 204800 | bytes 820224 | tf_op jit(solution)/shard_map/jit(_where)/select_n | solution.py:469
  2.5 0.1 select_convert_fusion.place_ref
  2.5 0.3 shard_map.135
  2.8 0.0 copy-start.1
  2.8 0.0 copy-start.2
  2.9 3.3 %collective-permute-start = (bf16[3,200,128]{2,1,0:T(8,128)(2,1)S(1)}, bf16[3,200,128]{2,1,0:T(8,128)(2,1)S(1)}, u32[]{:S(2)}, u32[]{:S(2)}) collective-permute-start(bf16[3,200,128]{2,1,0:T(8,128)(2,1)S(1)} %get-tuple-element.38), channel_id=1, source_target_pairs={{0,1},{1,0},{2,3},{3,2},{4,5},{5,4},{6,7},{7,6},{8,9},{9,8},{10,11... | collective-permute-start | bytes 460808 | tf_op jit(solution)/shard_map/ppermute | solution.py:440
  6.2 1.0 %broadcast_select_fusion.cot_ref = bf16[200,8,128]{2,1,0:T(8,128)(2,1)S(1)} fusion(bf16[200,8,128]{2,1,0:T(8,128)(2,1)} %param.15, pred[8,128]{1,0:T(8,128)(4,1)S(1)} %get-tuple-element.67), kind=kLoop, calls=%fused_computation | loop fusion | flops 204800 | bytes 820224 | tf_op jit(solution)/shard_map/jit(_where)/select_n | solution.py:472
  7.2 0.2 shard_map.137.g_ref
  7.4 3.7 %collective-permute-done.1.far_ref = bf16[3,200,128]{2,1,0:T(8,128)(2,1)S(1)} collective-permute-done((bf16[3,200,128]{2,1,0:T(8,128)(2,1)S(1)}, bf16[3,200,128]{2,1,0:T(8,128)(2,1)S(1)}, u32[]{:S(2)}, u32[]{:S(2)}) %collective-permute-start.1) | collective-permute-done | bytes 153632 | tf_op jit(solution)/shard_map/ppermute | solution.py:440
  11.1 0.3 shard_map.136
  11.4 6.6 %collective-permute-start.3 = (bf16[200,128]{1,0:T(8,128)(2,1)S(1)}, bf16[200,128]{1,0:T(8,128)(2,1)S(1)}, u32[]{:S(2)}, u32[]{:S(2)}) collective-permute-start(bf16[200,128]{1,0:T(8,128)(2,1)S(1)} %shard_map.136), channel_id=1, source_target_pairs={{0,240},{16,32},{32,16},{48,64},{64,48},{80,96},{96,80},{112,128},... | collective-permute-start | bytes 153608 | tf_op jit(solution)/shard_map/ppermute | solution.py:432
  18.0 2.0 %shard_map.138 = (f32[49,200,128]{2,1,0:T(8,128)S(1)}, f32[200,128]{1,0:T(8,128)S(1)}, f32[800,128]{1,0:T(8,128)S(1)}, bf16[800,200]{1,0:T(8,128)(2,1)S(1)}, bf16[800,200]{1,0:T(8,128)(2,1)S(1)}) custom-call(bf16[49,200]{1,0:T(8,128)(2,1)S(1)} %copy-done.3, f32[200]{0:T(256)S(1)} %copy-done.5, f32[800]{0:T(1024)S(1)} %copy-done.4, ...), custom_call_target="tpu_custom_call" | custom-call | flops 3000000000 | bytes 9000000 | tf_op jit(solution)/shard_map/pallas_call | solution.py:478
  20.0 1.2 %collective-permute-done.2.lon_near_ref = bf16[200,128]{1,0:T(8,128)(2,1)S(1)} collective-permute-done((bf16[200,128]{1,0:T(8,128)(2,1)S(1)}, bf16[200,128]{1,0:T(8,128)(2,1)S(1)}, u32[]{:S(2)}, u32[]{:S(2)}) %collective-permute-start.2) | collective-permute-done | bytes 51232 | tf_op jit(solution)/shard_map/ppermute | solution.py:433
  21.2 11.2 %shard_map.139 = (bf16[200,8,128]{2,1,0:T(8,128)(2,1)}, bf16[8,200,128]{2,1,0:T(8,128)(2,1)S(1)}, bf16[3,200,128]{2,1,0:T(8,128)(2,1)S(1)}, bf16[3,200,128]{2,1,...) custom-call(f32[8,256]{1,0:T(8,128)S(1)} %select_convert_fusion.place_ref, ...), custom_call_target="tpu_custom_call" | custom-call | flops 12000000000 | bytes 36000000 | tf_op jit(solution)/shard_map/pallas_call | solution.py:491
  32.4 3.0 %collective-permute-start.4 = (bf16[800,208]{1,0:T(8,128)(2,1)S(1)}, bf16[800,208]{1,0:T(8,128)(2,1)S(1)}, u32[]{:S(2)}, u32[]{:S(2)}) collective-permute-start(bf16[800,208]{1,0:T(8,128)(2,1)S(1)} %get-tuple-element.53), channel_id=1, source_target_pairs={{0,1},{1,0},{2,3},{3,2},{4,5},{5,4},{6,7},{7,6},{8,9},{9,8},{10,11... | collective-permute-start | bytes 998408 | tf_op jit(solution)/shard_map/ppermute | solution.py:529
  35.4 4.7 %shard_map.140 = (f32[64,256]{1,0:T(8,128)S(1)}, bf16[64,256]{1,0:T(8,128)(2,1)S(1)}) custom-call(f32[8,256]{1,0:T(8,128)S(1)} %select_convert_fusion.place_ref, bf16[8,200,128]{2,1,0:T(8,128)(2,1)S(1)} %get-tuple-element.37.mid_ref.m_ref, bf16[3,200,128]{2,1,0:T(8,128)(2,1)S(1)} %collective-permute-done.near_ref, ...), custom_call_target="tpu_custom_call" | custom-call | flops 6000000000 | bytes 18000000 | tf_op jit(solution)/shard_map/pallas_call | solution.py:531
  40.2 0.1 collective-permute-start.5
  40.3 1.2 %collective-permute-done.5.taps_got_ref = bf16[64,256]{1,0:T(8,128)(2,1)S(1)} collective-permute-done((bf16[64,256]{1,0:T(8,128)(2,1)S(1)}, bf16[64,256]{1,0:T(8,128)(2,1)S(1)}, u32[]{:S(2)}, u32[]{:S(2)}) %collective-permute-start.5) | collective-permute-done | bytes 32800 | tf_op jit(solution)/shard_map/ppermute | solution.py:538
  41.5 1.1 %shard_map.141 = bf16[16,64,256]{2,1,0:T(8,128)(2,1)} custom-call(f32[800,208]{1,0:T(8,128)S(1)} %get-tuple-element.52.own_ref, bf16[800,208]{1,0:T(8,128)(2,1)S(1)} %collective-permute-done.4.got_ref, f32[64,256]{1,0:T(8,128)S(1)} %get-tuple-element.56.taps_ref, bf16[64,256]{1,0:T(8,128)(2,1)S(1)} %collective-permute-done.5.taps_got_ref), custom_call_target="tpu_custom_call" | custom-call | flops 1000000000 | bytes 3000000 | tf_op jit(solution)/shard_map/pallas_call | solution.py:539
  42.5 4.7 %all-to-all-start = ((bf16[16,64,256]{2,1,0:T(8,128)(2,1)}), bf16[16,64,256]{2,1,0:T(8,128)(2,1)S(1)}, u32[]{:S(2)}, u32[]{:S(2)}) async-start(bf16[16,64,256]{2,1,0:T(8,128)(2,1)} %shard_map.141), calls=%async_computation | async-start | bytes 1048576 | tf_op jit(solution)/shard_map/all_to_all | solution.py:553
  47.3 0.5 collective-permute-start.6
  47.8 1.0 %collective-permute-done.6.near_ref = bf16[3,200,128]{2,1,0:T(8,128)(2,1)S(1)} collective-permute-done((bf16[3,200,128]{2,1,0:T(8,128)(2,1)S(1)}, bf16[3,200,128]{2,1,0:T(8,128)(2,1)S(1)}, u32[]{:S(2)}, u32[]{:S(2)}) %collective-permute-start.6) | collective-permute-done | bytes 153632 | tf_op jit(solution)/shard_map/ppermute | solution.py:440
  48.8 3.9 %collective-permute-done.7.far_ref = bf16[3,200,128]{2,1,0:T(8,128)(2,1)S(1)} collective-permute-done((bf16[3,200,128]{2,1,0:T(8,128)(2,1)S(1)}, bf16[3,200,128]{2,1,0:T(8,128)(2,1)S(1)}, u32[]{:S(2)}, u32[]{:S(2)}) %collective-permute-start.7) | collective-permute-done | bytes 153632 | tf_op jit(solution)/shard_map/ppermute | solution.py:440
  52.7 0.3 shard_map.143
  53.0 5.4 %collective-permute-start.9 = (bf16[200,128]{1,0:T(8,128)(2,1)S(1)}, bf16[200,128]{1,0:T(8,128)(2,1)S(1)}, u32[]{:S(2)}, u32[]{:S(2)}) collective-permute-start(bf16[200,128]{1,0:T(8,128)(2,1)S(1)} %shard_map.143), channel_id=1, source_target_pairs={{0,240},{16,32},{32,16},{48,64},{64,48},{80,96},{96,80},{112,128},... | collective-permute-start | bytes 153608 | tf_op jit(solution)/shard_map/ppermute | solution.py:432
  58.5 4.1 %all-to-all-done.parts_ref = bf16[16,64,256]{2,1,0:T(8,128)(2,1)S(1)} async-done(((bf16[16,64,256]{2,1,0:T(8,128)(2,1)}), bf16[16,64,256]{2,1,0:T(8,128)(2,1)S(1)}, u32[]{:S(2)}, u32[]{:S(2)}) %all-to-all-start) | async-done | bytes 524320 | tf_op jit(solution)/shard_map/all_to_all | solution.py:553
  62.5 0.9 %shard_map.142 = bf16[16,64,256]{2,1,0:T(8,128)(2,1)} custom-call(bf16[16,64,256]{2,1,0:T(8,128)(2,1)S(1)} %all-to-all-done.parts_ref), custom_call_target="tpu_custom_call" | custom-call | flops 1000000000 | bytes 3000000 | tf_op jit(solution)/shard_map/pallas_call | solution.py:554
  63.4 6.6 %all-to-all-start.1 = ((bf16[16,64,256]{2,1,0:T(8,128)(2,1)}), bf16[16,64,256]{2,1,0:T(8,128)(2,1)S(1)}, u32[]{:S(2)}, u32[]{:S(2)}) async-start(bf16[16,64,256]{2,1,0:T(8,128)(2,1)} %shard_map.142), calls=%async_computation.1 | async-start | bytes 1048576 | tf_op jit(solution)/shard_map/all_to_all | solution.py:555
  70.1 7.1 %shard_map.144 = bf16[200,8,128]{2,1,0:T(8,128)(2,1)} custom-call(f32[8,256]{1,0:T(8,128)S(1)} %select_convert_fusion.place_ref, bf16[8,200,128]{2,1,0:T(8,128)(2,1)S(1)} %get-tuple-element.54.bm_ref.mid_ref, bf16[3,200,128]{2,1,0:T(8,128)(2,1)S(1)} %collective-permute-done.6.near_ref, bf16[3,200,128]{2,1,0:T(8,128)(2,1)S(1)} %collective-permute-done.7.far_ref, ...), custom_call_target="tpu_custom_call" | custom-call | flops 8000000000 | bytes 24000000 | tf_op jit(solution)/shard_map/pallas_call | solution.py:556
  77.2 2.7 %all-to-all-done.1.parts_ref = bf16[16,64,256]{2,1,0:T(8,128)(2,1)S(1)} async-done(((bf16[16,64,256]{2,1,0:T(8,128)(2,1)}), bf16[16,64,256]{2,1,0:T(8,128)(2,1)S(1)}, u32[]{:S(2)}, u32[]{:S(2)}) %all-to-all-start.1) | async-done | bytes 524320 | tf_op jit(solution)/shard_map/all_to_all | solution.py:555
  80.0 0.8 shard_map.145
  (22 shorter events, 0.1 us)
Async XLA Ops:
  2.8 15.2 %copy-start.1 = (bf16[800,200]{0,1:T(8,128)(2,1)S(1)}, bf16[800,200]{0,1:T(8,128)(2,1)}, u32[]{:S(2)}) copy-start(bf16[800,200]{0,1:T(8,128)(2,1)} %param.12) | copy-start | bytes 960004
  2.8 15.2 %copy-start.2 = (bf16[800,200]{0,1:T(8,128)(2,1)S(1)}, bf16[800,200]{0,1:T(8,128)(2,1)}, u32[]{:S(2)}) copy-start(bf16[800,200]{0,1:T(8,128)(2,1)} %param.14) | copy-start | bytes 960004
  2.8 15.2 %copy-start.3 = (bf16[49,200]{1,0:T(8,128)(2,1)S(1)}, bf16[49,200]{1,0:T(8,128)(2,1)}, u32[]{:S(2)}) copy-start(bf16[49,200]{1,0:T(8,128)(2,1)} %taps_ref.2) | copy-start | bytes 58804
  2.8 15.2 %copy-start.4 = (f32[800]{0:T(1024)S(1)}, f32[800]{0:T(1024)}, u32[]{:S(2)}) copy-start(f32[800]{0:T(1024)} %bias_ref) | copy-start | bytes 9604
  2.8 15.2 %copy-start.5 = (f32[200]{0:T(256)S(1)}, f32[200]{0:T(256)}, u32[]{:S(2)}) copy-start(f32[200]{0:T(256)} %gain_ref) | copy-start | bytes 2404
  2.9 4.6 %collective-permute-start = (bf16[3,200,128]{2,1,0:T(8,128)(2,1)S(1)}, bf16[3,200,128]{2,1,0:T(8,128)(2,1)S(1)}, u32[]{:S(2)}, u32[]{:S(2)}) collective-permute-start(bf16[3,200,128]{2,1,0:T(8,128)(2,1)S(1)} %get-tuple-element.38), channel_id=1, source_target_pairs={{0,1},{1,0},{2,3},{3,2},{4,5},{5,4},{6,7},{7,6},{8,9},{9,8},{10,11... | collective-permute-start | bytes 460808 | tf_op jit(solution)/shard_map/ppermute | solution.py:440
  6.2 4.9 %collective-permute-start.1 = (bf16[3,200,128]{2,1,0:T(8,128)(2,1)S(1)}, bf16[3,200,128]{2,1,0:T(8,128)(2,1)S(1)}, u32[]{:S(2)}, u32[]{:S(2)}) collective-permute-start(bf16[3,200,128]{2,1,0:T(8,128)(2,1)S(1)} %get-tuple-element.39), channel_id=1, source_target_pairs={{0,15},{1,2},{2,1},{3,4},{4,3},{5,6},{6,5},{7,8},{8,7},{9,10},{10,... | collective-permute-start | bytes 460808 | tf_op jit(solution)/shard_map/ppermute | solution.py:440
  11.4 9.8 %copy-start = (s32[8,128]{1,0:T(8,128)S(1)}, s32[8,128]{1,0:T(8,128)}, u32[]{:S(2)}) copy-start(s32[8,128]{1,0:T(8,128)} %mask_ref.3) | copy-start | bytes 12292
  11.4 8.6 %collective-permute-start.3 = (bf16[200,128]{1,0:T(8,128)(2,1)S(1)}, bf16[200,128]{1,0:T(8,128)(2,1)S(1)}, u32[]{:S(2)}, u32[]{:S(2)}) collective-permute-start(bf16[200,128]{1,0:T(8,128)(2,1)S(1)} %shard_map.136), channel_id=1, source_target_pairs={{0,240},{16,32},{32,16},{48,64},{64,48},{80,96},{96,80},{112,128},... | collective-permute-start | bytes 153608 | tf_op jit(solution)/shard_map/ppermute | solution.py:432
  18.0 3.3 %collective-permute-start.2 = (bf16[200,128]{1,0:T(8,128)(2,1)S(1)}, bf16[200,128]{1,0:T(8,128)(2,1)S(1)}, u32[]{:S(2)}, u32[]{:S(2)}) collective-permute-start(bf16[200,128]{1,0:T(8,128)(2,1)S(1)} %shard_map.136), channel_id=1, source_target_pairs={{0,16},{16,0},{32,48},{48,32},{64,80},{80,64},{96,112},{112,96},{1... | collective-permute-start | bytes 153608 | tf_op jit(solution)/shard_map/ppermute | solution.py:433
  32.4 9.1 %collective-permute-start.4 = (bf16[800,208]{1,0:T(8,128)(2,1)S(1)}, bf16[800,208]{1,0:T(8,128)(2,1)S(1)}, u32[]{:S(2)}, u32[]{:S(2)}) collective-permute-start(bf16[800,208]{1,0:T(8,128)(2,1)S(1)} %get-tuple-element.53), channel_id=1, source_target_pairs={{0,1},{1,0},{2,3},{3,2},{4,5},{5,4},{6,7},{7,6},{8,9},{9,8},{10,11... | collective-permute-start | bytes 998408 | tf_op jit(solution)/shard_map/ppermute | solution.py:529
  40.2 1.3 %collective-permute-start.5 = (bf16[64,256]{1,0:T(8,128)(2,1)S(1)}, bf16[64,256]{1,0:T(8,128)(2,1)S(1)}, u32[]{:S(2)}, u32[]{:S(2)}) collective-permute-start(bf16[64,256]{1,0:T(8,128)(2,1)S(1)} %get-tuple-element.57), channel_id=1, source_target_pairs={{0,1},{1,0},{2,3},{3,2},{4,5},{5,4},{6,7},{7,6},{8,9},{9,8},{10,11... | collective-permute-start | bytes 98312 | tf_op jit(solution)/shard_map/ppermute | solution.py:538
  42.5 20.0 %all-to-all-start = ((bf16[16,64,256]{2,1,0:T(8,128)(2,1)}), bf16[16,64,256]{2,1,0:T(8,128)(2,1)S(1)}, u32[]{:S(2)}, u32[]{:S(2)}) async-start(bf16[16,64,256]{2,1,0:T(8,128)(2,1)} %shard_map.141), calls=%async_computation | async-start | bytes 1048576 | tf_op jit(solution)/shard_map/all_to_all | solution.py:553
  47.3 1.5 %collective-permute-start.6 = (bf16[3,200,128]{2,1,0:T(8,128)(2,1)S(1)}, bf16[3,200,128]{2,1,0:T(8,128)(2,1)S(1)}, u32[]{:S(2)}, u32[]{:S(2)}) collective-permute-start(bf16[3,200,128]{2,1,0:T(8,128)(2,1)S(1)} %get-tuple-element.58), channel_id=1, source_target_pairs={{0,1},{1,0},{2,3},{3,2},{4,5},{5,4},{6,7},{7,6},{8,9},{9,8},{10,11... | collective-permute-start | bytes 460808 | tf_op jit(solution)/shard_map/ppermute | solution.py:440
  47.8 4.9 %collective-permute-start.7 = (bf16[3,200,128]{2,1,0:T(8,128)(2,1)S(1)}, bf16[3,200,128]{2,1,0:T(8,128)(2,1)S(1)}, u32[]{:S(2)}, u32[]{:S(2)}) collective-permute-start(bf16[3,200,128]{2,1,0:T(8,128)(2,1)S(1)} %get-tuple-element.59), channel_id=1, source_target_pairs={{0,15},{1,2},{2,1},{3,4},{4,3},{5,6},{6,5},{7,8},{8,7},{9,10},{10,... | collective-permute-start | bytes 460808 | tf_op jit(solution)/shard_map/ppermute | solution.py:440
  53.0 17.1 %collective-permute-start.9 = (bf16[200,128]{1,0:T(8,128)(2,1)S(1)}, bf16[200,128]{1,0:T(8,128)(2,1)S(1)}, u32[]{:S(2)}, u32[]{:S(2)}) collective-permute-start(bf16[200,128]{1,0:T(8,128)(2,1)S(1)} %shard_map.143), channel_id=1, source_target_pairs={{0,240},{16,32},{32,16},{48,64},{64,48},{80,96},{96,80},{112,128},... | collective-permute-start | bytes 153608 | tf_op jit(solution)/shard_map/ppermute | solution.py:432
  58.5 11.6 %collective-permute-start.8 = (bf16[200,128]{1,0:T(8,128)(2,1)S(1)}, bf16[200,128]{1,0:T(8,128)(2,1)S(1)}, u32[]{:S(2)}, u32[]{:S(2)}) collective-permute-start(bf16[200,128]{1,0:T(8,128)(2,1)S(1)} %shard_map.143), channel_id=1, source_target_pairs={{0,16},{16,0},{32,48},{48,32},{64,80},{80,64},{96,112},{112,96},{1... | collective-permute-start | bytes 153608 | tf_op jit(solution)/shard_map/ppermute | solution.py:433
  63.4 16.5 %all-to-all-start.1 = ((bf16[16,64,256]{2,1,0:T(8,128)(2,1)}), bf16[16,64,256]{2,1,0:T(8,128)(2,1)S(1)}, u32[]{:S(2)}, u32[]{:S(2)}) async-start(bf16[16,64,256]{2,1,0:T(8,128)(2,1)} %shard_map.142), calls=%async_computation.1 | async-start | bytes 1048576 | tf_op jit(solution)/shard_map/all_to_all | solution.py:555

commit v4 on v3

--- a/solution.py
+++ b/solution.py
@@ -53,11 +53,14 @@
     return [flat[pl.ds(row, channels, stride=rows), :] for row in range(rows)]
 
 
-def state_body(x_ref, place_ref, m_ref, near_ref, far_ref, flat):
+def state_body(mask_ref, x_ref, place_ref, m_ref, near_ref, far_ref, pack_ref, flat):
+    rows = mask_ref.shape[0]
     masked = by_rows(x_ref, flat)
-    for row, value in enumerate(masked):
-        m_ref[row] = value.astype(BF)
+    masked = [value * mask_ref[r : r + 1, :].astype(F32) for r, value in enumerate(masked)]
+    pack_ref[...] = packed_edges(masked, HALO).astype(BF)
     send_edges(place_ref, masked, near_ref, far_ref)
+    for row in range(rows):
+        m_ref[row] = masked[row].astype(BF)
 
 
 def send_edges(place_ref, values, near_ref, far_ref):
@@ -68,9 +71,9 @@
         far_ref[r] = jnp.where(first, top, bottom).astype(BF)
 
 
-def gated_body(cot_ref, g_ref, flat):
+def gated_body(mask_ref, cot_ref, g_ref, flat):
     for row, value in enumerate(by_rows(cot_ref, flat)):
-        g_ref[row] = value.astype(BF)
+        g_ref[row] = (value * mask_ref[row : row + 1, :].astype(F32)).astype(BF)
 
 
 def spread_body(taps_ref, spread_ref):
@@ -127,36 +130,64 @@
         yield jnp.where(has_down, jnp.where(first, near[r], far[r]), 0.0)
 
 
-def pack_body(place_ref, mid_ref, near_ref, far_ref, out_ref):
-    channels, lanes = out_ref.shape
-    lane = lax.broadcasted_iota(jnp.int32, (channels, lanes), 1)
-    packed = jnp.zeros((channels, lanes), F32)
-    for r, value in enumerate(extended_rows(place_ref, mid_ref, near_ref, far_ref)):
+def packed_edges(values, first_row):
+    shape = values[0].shape
+    lanes = shape[1]
+    lane = lax.broadcasted_iota(jnp.int32, shape, 1)
+    packed = jnp.zeros(shape, F32)
+    for r, value in enumerate(values, first_row):
         if r:
             value = pltpu.roll(value, 8 * r, 1)
         packed = jnp.where(((lane + (HALO - 8 * r)) & (lanes - 1)) < 2 * HALO, value, packed)
-    out_ref[...] = packed.astype(BF)
-
-
-def fill_extended(ext, edge, place_ref, mid_ref, near_ref, far_ref, lon_near_ref, lon_far_ref):
-    for r, value in enumerate(extended_rows(place_ref, mid_ref, near_ref, far_ref)):
-        ext[r] = value
-    shape = edge.shape
+    return packed
+
+
+def pack_body(place_ref, mid_ref, near_ref, far_ref, out_ref):
+    rows = extended_rows(place_ref, mid_ref, near_ref, far_ref)
+    out_ref[...] = packed_edges(list(rows), 0).astype(BF)
+
+
+def lon_edges(place_ref, lon_near_ref, lon_far_ref):
+    shape = lon_near_ref.shape
     lane = lax.broadcasted_iota(jnp.int32, shape, 1)
     side = jnp.where((lane & 7) >= 4, 1.0, 0.0)
     near_is_right = jnp.broadcast_to(place_ref[3:4, : shape[1]], shape)
     near = lon_near_ref[...].astype(F32)
-    edge[...] = jnp.where(side != near_is_right, near, lon_far_ref[...].astype(F32))
-
-
-def joined(ext, edge, start):
-    n_rows, _, lanes = ext.shape
-    mid = ext[:, pl.ds(start, 8), :]
+    return jnp.where(side != near_is_right, near, lon_far_ref[...].astype(F32))
+
+
+def edges_body(place_ref, lon_near_ref, lon_far_ref, out_ref):
+    out_ref[...] = lon_edges(place_ref, lon_near_ref, lon_far_ref).astype(BF)
+
+
+def all_edges(place_ref, own_ref, near_ref, far_ref):
+    shape = own_ref.shape
+    first = is_first(place_ref, shape)
+    near, far = near_ref[...].astype(F32), far_ref[...].astype(F32)
+    up = jnp.where(flag(place_ref, 1, shape), jnp.where(first, far, near), 0.0)
+    down = jnp.where(flag(place_ref, 2, shape), jnp.where(first, near, far), 0.0)
+    lane = lax.broadcasted_iota(jnp.int32, shape, 1)
+    row = ((lane + HALO) >> 3) & 15
+    others = pltpu.roll(jnp.where(row < 8, down, up), 64, 1)
+    return jnp.where((row >= HALO) & (row < HALO + 8), own_ref[...].astype(F32), others)
+
+
+def fill_extended(ext, place_ref, mid_ref, near_ref, far_ref):
+    for r, value in enumerate(extended_rows(place_ref, mid_ref, near_ref, far_ref)):
+        ext[r] = value
+
+
+def line_up(edge, start, n_rows):
     ends = edge[pl.ds(start, 8), :]
-    wings = jnp.stack(
+    lanes = ends.shape[1]
+    return jnp.stack(
         [ends] + [pltpu.roll(ends, lanes - 8 * r, 1) for r in range(1, n_rows)], axis=0
     )
-    lane = lax.broadcasted_iota(jnp.int32, (8, lanes), 1)
+
+
+def joined(mid, wings):
+    lanes = mid.shape[2]
+    lane = lax.broadcasted_iota(jnp.int32, mid.shape[1:], 1)
     for shift in range(-HALO, HALO + 1):
         if shift == 0:
             yield shift, mid
@@ -165,10 +196,11 @@
         yield shift, jnp.where(outside[None], wings, mid)
 
 
-def convolve(ext, edge, spread_ref, start, rows, flipped):
+def convolve(ext, wings, spread_ref, start, rows, flipped):
     lanes = ext.shape[2]
+    mid = ext[:, pl.ds(start, 8), :]
     total = jnp.zeros((rows, 8, lanes), F32)
-    for b, (shift, value) in enumerate(joined(ext, edge, start)):
+    for b, (shift, value) in enumerate(joined(mid, wings)):
         window = pltpu.roll(value, -shift % lanes, 2) if shift else value
         for a in range(TAPS):
             tap = a * TAPS + b
@@ -183,8 +215,9 @@
     m_ref,
     near_ref,
     far_ref,
-    lon_near_ref,
-    lon_far_ref,
+    edge_own_ref,
+    edge_near_ref,
+    edge_far_ref,
     mask_ref,
     g_ref,
     spread_ref,
@@ -201,22 +234,24 @@
     gain_ref,
     own_ref,
     other_ref,
+    wings_ref,
     ext,
     edge,
     mixed,
     units,
     sides,
-    flat,
 ):
     rows, channels, lanes = m_ref.shape
     hidden, deep = own_ref.shape
-    chunk = hidden // 5
     pair = 2 * lanes
-    fill_extended(ext, edge, place_ref, m_ref, near_ref, far_ref, lon_near_ref, lon_far_ref)
+    fill_extended(ext, place_ref, m_ref, near_ref, far_ref)
+    edge[...] = all_edges(place_ref, edge_own_ref, edge_near_ref, edge_far_ref)
 
     def conv_step(block, carry):
         start = pl.multiple_of(block * 8, 8)
-        mixed[:, pl.ds(start, 8), :] = convolve(ext, edge, spread_ref, start, rows, False)
+        wings = line_up(edge, start, ext.shape[0])
+        wings_ref[:, pl.ds(start, 8), :] = wings
+        mixed[:, pl.ds(start, 8), :] = convolve(ext, wings, spread_ref, start, rows, False)
         return carry
 
     lax.fori_loop(0, channels // 8, conv_step, 0, unroll=5)
@@ -241,15 +276,12 @@
         sides[0, :, cells] = jnp.concatenate([normed, ones_rows], axis=0).astype(BF)
         normed = normed.astype(BF)
         gated = jnp.concatenate([g_ref[2 * p], g_ref[2 * p + 1]], axis=1)
-        for c in range(hidden // chunk):
-            part = pl.ds(c * chunk, chunk)
-            bias = biases_ref[part, :]
-            inner = dot(we_ref[part, :], normed) + jnp.concatenate([bias, bias], axis=1)
-            back_act = dot(wp_ref[part, :], gated)
-            normal_cdf = 0.5 * (1.0 + lax.erf(inner * 0.7071067811865476))
-            density = jnp.exp(-0.5 * inner * inner) * 0.3989422804014327
-            units[1, part, cells] = (inner * normal_cdf).astype(BF)
-            units[0, part, cells] = (back_act * (normal_cdf + inner * density)).astype(BF)
+        inner = dot(we_ref[...], normed) + jnp.concatenate([biases_ref[...]] * 2, axis=1)
+        back_act = dot(wp_ref[...], gated)
+        normal_cdf = 0.5 * (1.0 + lax.erf(inner * 0.7071067811865476))
+        density = jnp.exp(-0.5 * inner * inner) * 0.3989422804014327
+        units[1, :, cells] = (inner * normal_cdf).astype(BF)
+        units[0, :, cells] = (back_act * (normal_cdf + inner * density)).astype(BF)
         branch = dot(wp_t_ref[...], units[1, :, cells])
         back_norm = dot(we_t_ref[...], units[0, :, cells])
         gain_term = back_norm * whitened
@@ -262,18 +294,15 @@
             r = 2 * p + k
             mask = mask_ref[pl.ds(r, 1), :].astype(F32)
             here = slice(k * lanes, (k + 1) * lanes)
-            flat[pl.ds(r, channels, stride=rows), :] = ext[r + HALO] + mask * branch[:, here]
+            next_ref[r] = ext[r + HALO] + mask * branch[:, here]
             bm_ref[r] = back_mixed[:, here]
         return carry
 
-    lax.fori_loop(0, rows // 2, pair_step, 0)
-    next_ref[...] = flat[...].reshape(channels, rows, lanes).astype(BF)
+    lax.fori_loop(0, rows // 2, pair_step, 0, unroll=True)
     send_edges(place_ref, [bm_ref[r].astype(F32) for r in range(rows)], bnear_ref, bfar_ref)
     core = lax.axis_index("lat") % 2
     for out, which in ((own_ref, core), (other_ref, 1 - core)):
-        for c in range(hidden // chunk):
-            part = slice(c * chunk, (c + 1) * chunk)
-            out[part, :] = nt_dot(units[which, part, :], sides[which]).astype(out.dtype)
+        out[...] = nt_dot(units[which], sides[which]).astype(out.dtype)
 
 
 def taps_body(
@@ -281,20 +310,18 @@
     m_ref,
     near_ref,
     far_ref,
-    lon_near_ref,
-    lon_far_ref,
+    wings_ref,
     bm_ref,
     gain_ref,
     own_ref,
     other_ref,
     ext,
-    edge,
     upstream,
     sums,
     moved,
 ):
     rows, channels, lanes = m_ref.shape
-    fill_extended(ext, edge, place_ref, m_ref, near_ref, far_ref, lon_near_ref, lon_far_ref)
+    fill_extended(ext, place_ref, m_ref, near_ref, far_ref)
     for r in range(rows):
         upstream[r] = bm_ref[r].astype(F32)
     lane = lax.broadcasted_iota(jnp.int32, (8, lanes), 1)
@@ -303,8 +330,9 @@
     def step(block, carry):
         start = pl.multiple_of(block * 8, 8)
         back = upstream[:, pl.ds(start, 8), :]
+        mid, wings = ext[:, pl.ds(start, 8), :], wings_ref[:, pl.ds(start, 8), :]
         result = jnp.zeros((8, lanes), F32)
-        for b, (shift, value) in enumerate(joined(ext, edge, start)):
+        for b, (shift, value) in enumerate(joined(mid, wings)):
             turned = pltpu.roll(back, shift % lanes, 2) if shift else back
             terms = [jnp.sum(turned * value[a : a + rows], axis=0) for a in range(TAPS)]
             terms.append(gain_ref[pl.ds(start, 8), :])
@@ -315,7 +343,7 @@
         sums[pl.ds(start, 8), :] = result
         return carry
 
-    lax.fori_loop(0, channels // 8, step, 0, unroll=5)
+    lax.fori_loop(0, channels // 8, step, 0, unroll=True)
     block, wide = own_ref.shape
     row = lax.broadcasted_iota(jnp.int32, (2 * block, lanes), 0)
     col = lax.broadcasted_iota(jnp.int32, (2 * block, lanes), 1)
@@ -339,16 +367,20 @@
     other_ref[...] = jnp.where(first, turned[block:], turned[:block]).astype(BF)
 
 
-def message_body(own_ref, got_ref, taps_ref, taps_got_ref, out_ref, total, taps, piece):
+def message_body(own_ref, got_ref, out_ref, total, piece):
     hidden, deep = own_ref.shape
     share = hidden // out_ref.shape[0]
     total[...] = own_ref[...] + got_ref[...].astype(F32)
-    taps[...] = taps_ref[...] + taps_got_ref[...].astype(F32)
-    piece[...] = taps[...]
+    piece[...] = jnp.zeros_like(piece)
     for k in range(out_ref.shape[0]):
-        rows = total[k * share : (k + 1) * share, :]
-        piece[:share, :deep] = rows + taps[:share, :deep]
+        piece[:share, :deep] = total[k * share : (k + 1) * share, :]
         out_ref[k] = piece[...].astype(BF)
+
+
+def add_taps_body(rows_ref, taps_ref, taps_got_ref, out_ref):
+    taps = taps_ref[...] + taps_got_ref[...].astype(F32)
+    for k in range(out_ref.shape[0]):
+        out_ref[k] = (rows_ref[k].astype(F32) + taps).astype(BF)
 
 
 def sum_body(parts_ref, out_ref):
@@ -392,6 +424,13 @@
     gb_ref[...] = (nt_dot(pick, high) + nt_dot(pick, low))[:1, :share]
 
 
+def next_body(rows_ref, out_ref, flat):
+    channels, rows, lanes = out_ref.shape
+    for r in range(rows):
+        flat[pl.ds(r, channels, stride=rows), :] = rows_ref[r]
+    out_ref[...] = flat[...].reshape(channels, rows, lanes).astype(BF)
+
+
 def backward_body(
     place_ref,
     bm_ref,
@@ -411,11 +450,13 @@
 ):
     rows, channels, lanes = bm_ref.shape
     spread_body(taps_ref, spread)
-    fill_extended(ext, edge, place_ref, bm_ref, near_ref, far_ref, lon_near_ref, lon_far_ref)
+    fill_extended(ext, place_ref, bm_ref, near_ref, far_ref)
+    edge[...] = lon_edges(place_ref, lon_near_ref, lon_far_ref)
 
     def step(block, carry):
         start = pl.multiple_of(block * 8, 8)
-        back[:, pl.ds(start, 8), :] = convolve(ext, edge, spread, start, rows, True)
+        wings = line_up(edge, start, ext.shape[0])
+        back[:, pl.ds(start, 8), :] = convolve(ext, wings, spread, start, rows, True)
         return carry
 
     lax.fori_loop(0, channels // 8, step, 0, unroll=5)
@@ -463,18 +504,16 @@
     value = jnp.where(kind == 3, 1 - lax.axis_index("lon") % 2, value)
     place = jnp.where(kind == 4, 1 - lat // 2 % 2, value).astype(F32)
     swap = [(i, i ^ 1) for i in range(n_lat)]
-    zero = jnp.zeros((), BF)
-    masked, near, far = kernel_call(
-        state_body, [(full, BF), (edges, BF), (edges, BF)], [flat], n_in=2
-    )(jnp.where(land_sea[None] != 0, ocean_state, zero), place)
+    masked, near, far, pack = kernel_call(
+        state_body, [(full, BF), (edges, BF), (edges, BF), (tile, BF)], [flat], n_in=3
+    )(land_sea, ocean_state, place)
+    lon_near, lon_far = swap_lon(pack)
     near, far = swap_lat(far, near)
-    (gated,) = kernel_call(gated_body, [(full, BF)], [flat], n_in=1)(
-        jnp.where(land_sea[None] > 0, cotangent, zero)
-    )
-    (pack,) = kernel_call(pack_body, [(tile, BF)], n_in=4)(place, masked, near, far)
+    (own_edges,) = kernel_call(edges_body, [(tile, BF)], n_in=3)(place, lon_near, lon_far)
+    (gated,) = kernel_call(gated_body, [(full, BF)], [flat], n_in=2)(land_sea, cotangent)
     later = (depth_kernel, norm_gain, b_expand, w_expand.T, w_project.T)
-    pack, later = lax.optimization_barrier((pack, later))
-    lon_near, lon_far = swap_lon(pack)
+    own_edges, later = lax.optimization_barrier((own_edges, later))
+    edge_near, edge_far = swap_lat(own_edges, own_edges)
     spread, gains, biases, we, wp = kernel_call(
         weights_body,
         [
@@ -488,16 +527,17 @@
         micros=3,
     )(*later)
     we_t, wp_t = later[3:]
-    next_state, back_mixed, bnear, bfar, gain, own, other = kernel_call(
+    next_rows, back_mixed, bnear, bfar, gain, own, other, wings = kernel_call(
         main_body,
         [
-            ((channels, rows, lanes), BF),
+            (full, F32),
             (full, BF),
             (edges, BF),
             (edges, BF),
             (tile, F32),
             ((hidden, deep), F32),
             ((hidden, deep), BF),
+            ((rows + 2 * HALO, channels, lanes), F32),
         ],
         [
             ext_s,
@@ -505,17 +545,17 @@
             pltpu.VMEM(full, F32),
             pltpu.VMEM((2, hidden, cells), BF),
             pltpu.VMEM((2, deep, cells), BF),
-            flat,
         ],
-        n_in=15,
+        n_in=16,
         micros=12,
     )(
         place,
         masked,
         near,
         far,
-        lon_near,
-        lon_far,
+        own_edges,
+        edge_near,
+        edge_far,
         land_sea,
         gated,
         spread,
@@ -531,25 +571,29 @@
     taps_own, taps_other = kernel_call(
         taps_body,
         [((depth, wide), F32), ((depth, wide), BF)],
-        [ext_s, edge_s, pltpu.VMEM(full, F32), edge_s, pltpu.VMEM((wide, lanes), F32)],
-        n_in=8,
+        [ext_s, pltpu.VMEM(full, F32), edge_s, pltpu.VMEM((wide, lanes), F32)],
+        n_in=7,
         micros=6,
-    )(place, masked, near, far, lon_near, lon_far, back_mixed, gain)
+    )(place, masked, near, far, wings, back_mixed, gain)
+    got, taps_other = lax.optimization_barrier((got, taps_other))
     taps_got = lax.ppermute(taps_other, "lat", swap)
     (message,) = kernel_call(
         message_body,
         [((n_lon, depth, wide), BF)],
-        [
-            pltpu.VMEM((hidden, deep), F32),
-            pltpu.VMEM((depth, wide), F32),
-            pltpu.VMEM((depth, wide), F32),
-        ],
-        n_in=4,
-    )(own, got, taps_own, taps_got)
+        [pltpu.VMEM((hidden, deep), F32), pltpu.VMEM((depth, wide), F32)],
+        n_in=2,
+    )(own, got)
+    (message,) = kernel_call(add_taps_body, [((n_lon, depth, wide), BF)], n_in=3)(
+        message, taps_own, taps_got
+    )
     (back_pack,) = kernel_call(pack_body, [(tile, BF)], n_in=4)(
         place, back_mixed, bnear, bfar
     )
+    back_pack, next_rows = lax.optimization_barrier((back_pack, next_rows))
     blon_near, blon_far = swap_lon(back_pack)
+    (next_state,) = kernel_call(next_body, [((channels, rows, lanes), BF)], [flat], n_in=1)(
+        next_rows
+    )
     parts = lax.all_to_all(message, "lon", 0, 0)
     (copies,) = kernel_call(sum_body, [((n_lat, depth, wide), BF)], n_in=1)(parts)
     parts = lax.all_to_all(copies, "lat", 0, 0)

time: 81.2 us -> 77.2 us (0.951)
  waiting for transfers between devices: 17.8 us -> 12 us
  starting transfers between devices: 30.4 us -> 34.6 us
  other arithmetic: 2.85 us -> 0.09 us
  local copies, waits for them, and re-layouts: 0.04 us -> 2.72 us
  Pallas kernels: 28.8 us -> 26.6 us
    ppermute x4 -> x6, waiting for transfers between devices: 8.61 us -> 4.94 us  [swap_lat(): return (lax.ppermute(second, 'lat', near), lax.ppermute(first, 'lat', far))]
    unnamed x12 -> x18, local copies, waits for them, and re-layouts: 0.04 us -> 2.72 us
    ppermute x2, starting transfers between devices: 12 us -> 14.4 us  [swap_lon(): from_far = lax.ppermute(pack, 'lon', far)]
    select_n x2 -> x0, other arithmetic: 2.07 us -> none  [the longest x1 1.03 us: shards(): jnp.where(land_sea[None] != 0, ocean_state, zero)]
    ppermute x4 -> x6, starting transfers between devices: 3.86 us -> 5.52 us  [swap_lat(): return (lax.ppermute(second, 'lat', near), lax.ppermute(first, 'lat', far))]
    ppermute x2, waiting for transfers between devices: 1.22 us -> 0.01 us  [swap_lon(): return (lax.ppermute(pack, 'lon', near), from_far)]
    pallas_call x1, Pallas kernels: 4.71 us -> 3.83 us  [shards(): kernel_call(taps_body, [((depth, wide), F32), ((depth, wide), BF)], [ext_...]
    pallas_call x1, Pallas kernels: 1.06 us -> 0.21 us  [shards(): kernel_call(message_body, [((n_lon, depth, wide), BF)], [pltpu.VMEM((hidd...]
  transfers between devices with their start and end apart: 12 -> 14, of which waited for: 7 -> 5; matrix products, arithmetic and copies ran while one was open for 1% -> 0% of each run, Pallas kernels for 19% -> 20%
where the time goes in v4:
time: 77.2 us; the launch traced here: 76.8 us
  starting transfers between devices  34.6 us (45%)
  Pallas kernels  26.6 us (34%)
  waiting for transfers between devices  12 us (16%)
  local copies, waits for them, and re-layouts  2.72 us (4%)
  between operations  0.9 us (1%)
    ppermute x2, starting transfers between devices, swap_lon(): from_far = lax.ppermute(pack, 'lon', far)  14.4 us
    pallas_call x1, Pallas kernels, shards(): kernel_call(main_body, [(full, F32), (full, BF), (edges, BF), (edges, BF)...  8.91 us
    pallas_call x1, Pallas kernels, shards(): kernel_call(backward_body, [((channels, rows, lanes), BF)], [ext_s, edge_...  7.14 us
    all_to_all x1, starting transfers between devices, shards(): parts = lax.all_to_all(copies, 'lat', 0, 0)  6.54 us
    ppermute x6, starting transfers between devices, swap_lat(): return (lax.ppermute(second, 'lat', near), lax.ppermute(first, 'lat', far))  5.52 us
    all_to_all x1, starting transfers between devices, shards(): parts = lax.all_to_all(message, 'lon', 0, 0)  5.12 us
    ppermute x6, waiting for transfers between devices, swap_lat(): return (lax.ppermute(second, 'lat', near), lax.ppermute(first, 'lat', far))  4.94 us
    pallas_call x1, Pallas kernels, shards(): kernel_call(taps_body, [((depth, wide), F32), ((depth, wide), BF)], [ext_...  3.83 us
  transfers between devices with their start and end apart: 14, of which 5 were waited for; matrix products, arithmetic and copies ran while one was open for 0% of the time, Pallas kernels for 20%

profile of v4, /device:TPU:1, one launch (start us, length us, event | category | flops | bytes accessed | tf_op | source)
XLA Modules:
  0.0 76.8 jit_solution(18384395062078566884)
XLA Ops:
  0.7 0.1 select_convert_fusion.place_ref
  0.8 1.0 %copy-done = bf16[200,8,128]{2,1,0:T(8,128)(2,1)S(1)} copy-done((bf16[200,8,128]{2,1,0:T(8,128)(2,1)S(1)}, bf16[200,8,128]{2,1,0:T(8,128)(2,1)}, u32[]{:S(2)}) %copy-start) | copy-done | bytes 409624
  1.8 0.7 copy-done.6
  2.5 0.3 shard_map.135
  2.9 9.1 %collective-permute-start.3 = (bf16[200,128]{1,0:T(8,128)(2,1)S(1)}, bf16[200,128]{1,0:T(8,128)(2,1)S(1)}, u32[]{:S(2)}, u32[]{:S(2)}) collective-permute-start(bf16[200,128]{1,0:T(8,128)(2,1)S(1)} %get-tuple-element.46), channel_id=1, source_target_pairs={{0,240},{16,32},{32,16},{48,64},{64,48},{80,96},{96,80},{112,128},... | collective-permute-start | bytes 153608 | tf_op jit(solution)/shard_map/ppermute | solution.py:473
  12.0 1.0 %collective-permute-start = (bf16[3,200,128]{2,1,0:T(8,128)(2,1)S(1)}, bf16[3,200,128]{2,1,0:T(8,128)(2,1)S(1)}, u32[]{:S(2)}, u32[]{:S(2)}) collective-permute-start(bf16[3,200,128]{2,1,0:T(8,128)(2,1)S(1)} %get-tuple-element.44), channel_id=1, source_target_pairs={{0,1},{1,0},{2,3},{3,2},{4,5},{5,4},{6,7},{7,6},{8,9},{9,8},{10,11... | collective-permute-start | bytes 460808 | tf_op jit(solution)/shard_map/ppermute | solution.py:481
  12.9 1.1 %collective-permute-start.1 = (bf16[3,200,128]{2,1,0:T(8,128)(2,1)S(1)}, bf16[3,200,128]{2,1,0:T(8,128)(2,1)S(1)}, u32[]{:S(2)}, u32[]{:S(2)}) collective-permute-start(bf16[3,200,128]{2,1,0:T(8,128)(2,1)S(1)} %get-tuple-element.45), channel_id=1, source_target_pairs={{0,15},{1,2},{2,1},{3,4},{4,3},{5,6},{6,5},{7,8},{8,7},{9,10},{10,... | collective-permute-start | bytes 460808 | tf_op jit(solution)/shard_map/ppermute | solution.py:481
  14.0 1.0 %copy-done.1 = bf16[200,8,128]{2,1,0:T(8,128)(2,1)S(1)} copy-done((bf16[200,8,128]{2,1,0:T(8,128)(2,1)S(1)}, bf16[200,8,128]{2,1,0:T(8,128)(2,1)}, u32[]{:S(2)}) %copy-start.1) | copy-done | bytes 409624
  15.0 0.2 shard_map.137.g_ref
  15.3 2.9 %collective-permute-start.5 = (bf16[200,128]{1,0:T(8,128)(2,1)S(1)}, bf16[200,128]{1,0:T(8,128)(2,1)S(1)}, u32[]{:S(2)}, u32[]{:S(2)}) collective-permute-start(bf16[200,128]{1,0:T(8,128)(2,1)S(1)} %shard_map.136.edge_own_ref), channel_id=1, source_target_pairs={{0,15},{1,2},{2,1},{3,4},{4,3},{5,6},{6,5},{7,8},{8,7},{9,10},{10,... | collective-permute-start | bytes 153608 | tf_op jit(solution)/shard_map/ppermute | solution.py:481
  18.3 2.0 %shard_map.138 = (f32[49,200,128]{2,1,0:T(8,128)S(1)}, f32[200,128]{1,0:T(8,128)S(1)}, f32[800,128]{1,0:T(8,128)S(1)}, bf16[800,200]{1,0:T(8,128)(2,1)S(1)}, bf16[800,200]{1,0:T(8,128)(2,1)S(1)}) custom-call(bf16[49,200]{1,0:T(8,128)(2,1)S(1)} %copy-done.4, f32[200]{0:T(256)S(1)} %copy-done.8, f32[800]{0:T(1024)S(1)} %copy-done.5, ...), custom_call_target="tpu_custom_call" | custom-call | flops 3000000000 | bytes 9000000 | tf_op jit(solution)/shard_map/pallas_call | solution.py:517
  20.3 8.9 %shard_map.139 = (f32[8,200,128]{2,1,0:T(8,128)S(1)}, bf16[8,200,128]{2,1,0:T(8,128)(2,1)S(1)}, bf16[3,200,128]{2,1,0:T(8,128)(2,1)S(1)}, bf16[3,200,128]{2,1,0:...) custom-call(f32[8,256]{1,0:T(8,128)S(1)} %select_convert_fusion.plac, ...), custom_call_target="tpu_custom_call" | custom-call | flops 12000000000 | bytes 36000000 | tf_op jit(solution)/shard_map/pallas_call | solution.py:530
  29.2 2.9 %collective-permute-start.8 = (bf16[800,208]{1,0:T(8,128)(2,1)S(1)}, bf16[800,208]{1,0:T(8,128)(2,1)S(1)}, u32[]{:S(2)}, u32[]{:S(2)}) collective-permute-start(bf16[800,208]{1,0:T(8,128)(2,1)S(1)} %get-tuple-element.64), channel_id=1, source_target_pairs={{0,1},{1,0},{2,3},{3,2},{4,5},{5,4},{6,7},{7,6},{8,9},{9,8},{10,11... | collective-permute-start | bytes 998408 | tf_op jit(solution)/shard_map/ppermute | solution.py:569
  32.1 3.8 %shard_map.142 = (f32[64,256]{1,0:T(8,128)S(1)}, bf16[64,256]{1,0:T(8,128)(2,1)S(1)}) custom-call(f32[8,256]{1,0:T(8,128)S(1)} %select_convert_fusion.place_ref, bf16[8,200,128]{2,1,0:T(8,128)(2,1)S(1)} %get-tuple-element.43.m_ref, bf16[3,200,128]{2,1,0:T(8,128)(2,1)S(1)} %collective-permute-done.near_ref, ...), custom_call_target="tpu_custom_call" | custom-call | flops 6000000000 | bytes 18000000 | tf_op jit(solution)/shard_map/pallas_call | solution.py:571
  36.0 0.1 collective-permute-start.9
  36.1 0.2 shard_map.143.rows_ref
  36.3 1.0 %collective-permute-done.9.taps_got_ref = bf16[64,256]{1,0:T(8,128)(2,1)S(1)} collective-permute-done((bf16[64,256]{1,0:T(8,128)(2,1)S(1)}, bf16[64,256]{1,0:T(8,128)(2,1)S(1)}, u32[]{:S(2)}, u32[]{:S(2)}) %collective-permute-start.9) | collective-permute-done | bytes 32800 | tf_op jit(solution)/shard_map/ppermute | solution.py:579
  37.3 0.9 %shard_map.144 = bf16[16,64,256]{2,1,0:T(8,128)(2,1)} custom-call(bf16[16,64,256]{2,1,0:T(8,128)(2,1)S(1)} %shard_map.143.rows_ref, f32[64,256]{1,0:T(8,128)S(1)} %get-tuple-element.69.taps_ref, bf16[64,256]{1,0:T(8,128)(2,1)S(1)} %collective-permute-done.9.taps_got_ref), custom_call_target="tpu_custom_call" | custom-call | flops 1000000000 | bytes 3000000 | tf_op jit(solution)/shard_map/pallas_call | solution.py:586
  38.2 5.1 %all-to-all-start = ((bf16[16,64,256]{2,1,0:T(8,128)(2,1)}), bf16[16,64,256]{2,1,0:T(8,128)(2,1)S(1)}, u32[]{:S(2)}, u32[]{:S(2)}) async-start(bf16[16,64,256]{2,1,0:T(8,128)(2,1)} %shard_map.144), calls=%async_computation | async-start | bytes 1048576 | tf_op jit(solution)/shard_map/all_to_all | solution.py:597
  43.3 0.5 collective-permute-start.6
  43.8 1.0 %collective-permute-done.6.near_ref = bf16[3,200,128]{2,1,0:T(8,128)(2,1)S(1)} collective-permute-done((bf16[3,200,128]{2,1,0:T(8,128)(2,1)S(1)}, bf16[3,200,128]{2,1,0:T(8,128)(2,1)S(1)}, u32[]{:S(2)}, u32[]{:S(2)}) %collective-permute-start.6) | collective-permute-done | bytes 153632 | tf_op jit(solution)/shard_map/ppermute | solution.py:481
  44.9 3.9 %collective-permute-done.7.far_ref = bf16[3,200,128]{2,1,0:T(8,128)(2,1)S(1)} collective-permute-done((bf16[3,200,128]{2,1,0:T(8,128)(2,1)S(1)}, bf16[3,200,128]{2,1,0:T(8,128)(2,1)S(1)}, u32[]{:S(2)}, u32[]{:S(2)}) %collective-permute-start.7) | collective-permute-done | bytes 153632 | tf_op jit(solution)/shard_map/ppermute | solution.py:481
  48.8 0.3 shard_map.140
  49.1 0.0 copy-start.7
  49.1 5.3 %collective-permute-start.11 = (bf16[200,128]{1,0:T(8,128)(2,1)S(1)}, bf16[200,128]{1,0:T(8,128)(2,1)S(1)}, u32[]{:S(2)}, u32[]{:S(2)}) collective-permute-start(bf16[200,128]{1,0:T(8,128)(2,1)S(1)} %shard_map.140), channel_id=1, source_target_pairs={{0,240},{16,32},{32,16},{48,64},{64,48},{80,96},{96,80},{112,128},... | collective-permute-start | bytes 153608 | tf_op jit(solution)/shard_map/ppermute | solution.py:473
  54.3 1.0 %shard_map.141 = bf16[200,8,128]{2,1,0:T(8,128)(2,1)} custom-call(f32[8,200,128]{2,1,0:T(8,128)S(1)} %get-tuple-element.62.rows_ref), custom_call_target="tpu_custom_call" | custom-call | flops 1000000000 | bytes 3000000 | tf_op jit(solution)/shard_map/pallas_call | solution.py:594
  55.4 3.2 %all-to-all-done.parts_ref = bf16[16,64,256]{2,1,0:T(8,128)(2,1)S(1)} async-done(((bf16[16,64,256]{2,1,0:T(8,128)(2,1)}), bf16[16,64,256]{2,1,0:T(8,128)(2,1)S(1)}, u32[]{:S(2)}, u32[]{:S(2)}) %all-to-all-start) | async-done | bytes 524320 | tf_op jit(solution)/shard_map/all_to_all | solution.py:597
  58.6 0.9 %shard_map.145 = bf16[16,64,256]{2,1,0:T(8,128)(2,1)} custom-call(bf16[16,64,256]{2,1,0:T(8,128)(2,1)S(1)} %all-to-all-done.parts_ref), custom_call_target="tpu_custom_call" | custom-call | flops 1000000000 | bytes 3000000 | tf_op jit(solution)/shard_map/pallas_call | solution.py:598
  59.5 6.5 %all-to-all-start.1 = ((bf16[16,64,256]{2,1,0:T(8,128)(2,1)}), bf16[16,64,256]{2,1,0:T(8,128)(2,1)S(1)}, u32[]{:S(2)}, u32[]{:S(2)}) async-start(bf16[16,64,256]{2,1,0:T(8,128)(2,1)} %shard_map.145), calls=%async_computation.1 | async-start | bytes 1048576 | tf_op jit(solution)/shard_map/all_to_all | solution.py:599
  66.1 7.1 %shard_map.146 = bf16[200,8,128]{2,1,0:T(8,128)(2,1)} custom-call(f32[8,256]{1,0:T(8,128)S(1)} %select_convert_fusion.place_ref, bf16[8,200,128]{2,1,0:T(8,128)(2,1)S(1)} %get-tuple-element.58.mid_ref.bm_ref, bf16[3,200,128]{2,1,0:T(8,128)(2,1)S(1)} %collective-permute-done.6.near_ref, bf16[3,200,128]{2,1,0:T(8,128)(2,1)S(1)} %collective-permute-done.7.far_ref, ...), custom_call_target="tpu_custom_call" | custom-call | flops 8000000000 | bytes 24000000 | tf_op jit(solution)/shard_map/pallas_call | solution.py:600
  73.2 2.8 %all-to-all-done.1.parts_ref = bf16[16,64,256]{2,1,0:T(8,128)(2,1)S(1)} async-done(((bf16[16,64,256]{2,1,0:T(8,128)(2,1)}), bf16[16,64,256]{2,1,0:T(8,128)(2,1)S(1)}, u32[]{:S(2)}, u32[]{:S(2)}) %all-to-all-start.1) | async-done | bytes 524320 | tf_op jit(solution)/shard_map/all_to_all | solution.py:599
  76.0 0.8 %shard_map.147 = (f32[50,200]{1,0:T(8,128)}, f32[50,200]{1,0:T(8,128)}, f32[49,200]{1,0:T(8,128)}, f32[1,200]{1,0:T(1,128)}, f32[1,50]{1,0:T(1,128)}) custom-call(bf16[16,64,256]{2,1,0:T(8,128)(2,1)S(1)} %all-to-all-done.1.parts_ref), custom_call_target="tpu_custom_call" | custom-call | flops 1000000000 | bytes 3000000 | tf_op jit(solution)/shard_map/pallas_call | solution.py:611
  (31 shorter events, 0.1 us)
Async XLA Ops:
  0.8 1.0 %copy-start = (bf16[200,8,128]{2,1,0:T(8,128)(2,1)S(1)}, bf16[200,8,128]{2,1,0:T(8,128)(2,1)}, u32[]{:S(2)}) copy-start(bf16[200,8,128]{2,1,0:T(8,128)(2,1)} %x_ref.1) | copy-start | bytes 1228804
  1.8 0.7 copy-start.6
  2.5 15.8 %copy-start.2 = (bf16[800,200]{0,1:T(8,128)(2,1)S(1)}, bf16[800,200]{0,1:T(8,128)(2,1)}, u32[]{:S(2)}) copy-start(bf16[800,200]{0,1:T(8,128)(2,1)} %param.12) | copy-start | bytes 960004
  2.5 15.8 %copy-start.3 = (bf16[800,200]{0,1:T(8,128)(2,1)S(1)}, bf16[800,200]{0,1:T(8,128)(2,1)}, u32[]{:S(2)}) copy-start(bf16[800,200]{0,1:T(8,128)(2,1)} %param.14) | copy-start | bytes 960004
  2.5 15.8 %copy-start.4 = (bf16[49,200]{1,0:T(8,128)(2,1)S(1)}, bf16[49,200]{1,0:T(8,128)(2,1)}, u32[]{:S(2)}) copy-start(bf16[49,200]{1,0:T(8,128)(2,1)} %taps_ref.2) | copy-start | bytes 58804
  2.5 15.8 %copy-start.5 = (f32[800]{0:T(1024)S(1)}, f32[800]{0:T(1024)}, u32[]{:S(2)}) copy-start(f32[800]{0:T(1024)} %bias_ref) | copy-start | bytes 9604
  2.5 15.8 %copy-start.8 = (f32[200]{0:T(256)S(1)}, f32[200]{0:T(256)}, u32[]{:S(2)}) copy-start(f32[200]{0:T(256)} %gain_ref) | copy-start | bytes 2404
  2.9 12.4 %collective-permute-start.3 = (bf16[200,128]{1,0:T(8,128)(2,1)S(1)}, bf16[200,128]{1,0:T(8,128)(2,1)S(1)}, u32[]{:S(2)}, u32[]{:S(2)}) collective-permute-start(bf16[200,128]{1,0:T(8,128)(2,1)S(1)} %get-tuple-element.46), channel_id=1, source_target_pairs={{0,240},{16,32},{32,16},{48,64},{64,48},{80,96},{96,80},{112,128},... | collective-permute-start | bytes 153608 | tf_op jit(solution)/shard_map/ppermute | solution.py:473
  12.0 3.3 %collective-permute-start.2 = (bf16[200,128]{1,0:T(8,128)(2,1)S(1)}, bf16[200,128]{1,0:T(8,128)(2,1)S(1)}, u32[]{:S(2)}, u32[]{:S(2)}) collective-permute-start(bf16[200,128]{1,0:T(8,128)(2,1)S(1)} %get-tuple-element.46), channel_id=1, source_target_pairs={{0,16},{16,0},{32,48},{48,32},{64,80},{80,64},{96,112},{112,96},{1... | collective-permute-start | bytes 153608 | tf_op jit(solution)/shard_map/ppermute | solution.py:474
  12.0 8.3 %collective-permute-start = (bf16[3,200,128]{2,1,0:T(8,128)(2,1)S(1)}, bf16[3,200,128]{2,1,0:T(8,128)(2,1)S(1)}, u32[]{:S(2)}, u32[]{:S(2)}) collective-permute-start(bf16[3,200,128]{2,1,0:T(8,128)(2,1)S(1)} %get-tuple-element.44), channel_id=1, source_target_pairs={{0,1},{1,0},{2,3},{3,2},{4,5},{5,4},{6,7},{7,6},{8,9},{9,8},{10,11... | collective-permute-start | bytes 460808 | tf_op jit(solution)/shard_map/ppermute | solution.py:481
  12.9 7.4 %collective-permute-start.1 = (bf16[3,200,128]{2,1,0:T(8,128)(2,1)S(1)}, bf16[3,200,128]{2,1,0:T(8,128)(2,1)S(1)}, u32[]{:S(2)}, u32[]{:S(2)}) collective-permute-start(bf16[3,200,128]{2,1,0:T(8,128)(2,1)S(1)} %get-tuple-element.45), channel_id=1, source_target_pairs={{0,15},{1,2},{2,1},{3,4},{4,3},{5,6},{6,5},{7,8},{8,7},{9,10},{10,... | collective-permute-start | bytes 460808 | tf_op jit(solution)/shard_map/ppermute | solution.py:481
  14.0 1.0 %copy-start.1 = (bf16[200,8,128]{2,1,0:T(8,128)(2,1)S(1)}, bf16[200,8,128]{2,1,0:T(8,128)(2,1)}, u32[]{:S(2)}) copy-start(bf16[200,8,128]{2,1,0:T(8,128)(2,1)} %cot_ref.1) | copy-start | bytes 1228804
  15.3 5.0 %collective-permute-start.5 = (bf16[200,128]{1,0:T(8,128)(2,1)S(1)}, bf16[200,128]{1,0:T(8,128)(2,1)S(1)}, u32[]{:S(2)}, u32[]{:S(2)}) collective-permute-start(bf16[200,128]{1,0:T(8,128)(2,1)S(1)} %shard_map.136.edge_own_ref), channel_id=1, source_target_pairs={{0,15},{1,2},{2,1},{3,4},{4,3},{5,6},{6,5},{7,8},{8,7},{9,10},{10,... | collective-permute-start | bytes 153608 | tf_op jit(solution)/shard_map/ppermute | solution.py:481
  18.2 2.0 %collective-permute-start.4 = (bf16[200,128]{1,0:T(8,128)(2,1)S(1)}, bf16[200,128]{1,0:T(8,128)(2,1)S(1)}, u32[]{:S(2)}, u32[]{:S(2)}) collective-permute-start(bf16[200,128]{1,0:T(8,128)(2,1)S(1)} %shard_map.136.edge_own_ref), channel_id=1, source_target_pairs={{0,1},{1,0},{2,3},{3,2},{4,5},{5,4},{6,7},{7,6},{8,9},{9,8},{10,11... | collective-permute-start | bytes 153608 | tf_op jit(solution)/shard_map/ppermute | solution.py:481
  29.2 6.7 %collective-permute-start.8 = (bf16[800,208]{1,0:T(8,128)(2,1)S(1)}, bf16[800,208]{1,0:T(8,128)(2,1)S(1)}, u32[]{:S(2)}, u32[]{:S(2)}) collective-permute-start(bf16[800,208]{1,0:T(8,128)(2,1)S(1)} %get-tuple-element.64), channel_id=1, source_target_pairs={{0,1},{1,0},{2,3},{3,2},{4,5},{5,4},{6,7},{7,6},{8,9},{9,8},{10,11... | collective-permute-start | bytes 998408 | tf_op jit(solution)/shard_map/ppermute | solution.py:569
  36.0 1.3 %collective-permute-start.9 = (bf16[64,256]{1,0:T(8,128)(2,1)S(1)}, bf16[64,256]{1,0:T(8,128)(2,1)S(1)}, u32[]{:S(2)}, u32[]{:S(2)}) collective-permute-start(bf16[64,256]{1,0:T(8,128)(2,1)S(1)} %get-tuple-element.70), channel_id=1, source_target_pairs={{0,1},{1,0},{2,3},{3,2},{4,5},{5,4},{6,7},{7,6},{8,9},{9,8},{10,11... | collective-permute-start | bytes 98312 | tf_op jit(solution)/shard_map/ppermute | solution.py:579
  38.2 20.4 %all-to-all-start = ((bf16[16,64,256]{2,1,0:T(8,128)(2,1)}), bf16[16,64,256]{2,1,0:T(8,128)(2,1)S(1)}, u32[]{:S(2)}, u32[]{:S(2)}) async-start(bf16[16,64,256]{2,1,0:T(8,128)(2,1)} %shard_map.144), calls=%async_computation | async-start | bytes 1048576 | tf_op jit(solution)/shard_map/all_to_all | solution.py:597
  43.3 1.5 %collective-permute-start.6 = (bf16[3,200,128]{2,1,0:T(8,128)(2,1)S(1)}, bf16[3,200,128]{2,1,0:T(8,128)(2,1)S(1)}, u32[]{:S(2)}, u32[]{:S(2)}) collective-permute-start(bf16[3,200,128]{2,1,0:T(8,128)(2,1)S(1)} %get-tuple-element.59), channel_id=1, source_target_pairs={{0,1},{1,0},{2,3},{3,2},{4,5},{5,4},{6,7},{7,6},{8,9},{9,8},{10,11... | collective-permute-start | bytes 460808 | tf_op jit(solution)/shard_map/ppermute | solution.py:481
  43.8 4.9 %collective-permute-start.7 = (bf16[3,200,128]{2,1,0:T(8,128)(2,1)S(1)}, bf16[3,200,128]{2,1,0:T(8,128)(2,1)S(1)}, u32[]{:S(2)}, u32[]{:S(2)}) collective-permute-start(bf16[3,200,128]{2,1,0:T(8,128)(2,1)S(1)} %get-tuple-element.60), channel_id=1, source_target_pairs={{0,15},{1,2},{2,1},{3,4},{4,3},{5,6},{6,5},{7,8},{8,7},{9,10},{10,... | collective-permute-start | bytes 460808 | tf_op jit(solution)/shard_map/ppermute | solution.py:481
  49.1 17.0 %copy-start.7 = (s32[8,128]{1,0:T(8,128)S(1)}, s32[8,128]{1,0:T(8,128)}, u32[]{:S(2)}) copy-start(s32[8,128]{1,0:T(8,128)} %mask_ref.7) | copy-start | bytes 12292
  49.1 17.0 %collective-permute-start.11 = (bf16[200,128]{1,0:T(8,128)(2,1)S(1)}, bf16[200,128]{1,0:T(8,128)(2,1)S(1)}, u32[]{:S(2)}, u32[]{:S(2)}) collective-permute-start(bf16[200,128]{1,0:T(8,128)(2,1)S(1)} %shard_map.140), channel_id=1, source_target_pairs={{0,240},{16,32},{32,16},{48,64},{64,48},{80,96},{96,80},{112,128},... | collective-permute-start | bytes 153608 | tf_op jit(solution)/shard_map/ppermute | solution.py:473
  54.3 11.7 %collective-permute-start.10 = (bf16[200,128]{1,0:T(8,128)(2,1)S(1)}, bf16[200,128]{1,0:T(8,128)(2,1)S(1)}, u32[]{:S(2)}, u32[]{:S(2)}) collective-permute-start(bf16[200,128]{1,0:T(8,128)(2,1)S(1)} %shard_map.140), channel_id=1, source_target_pairs={{0,16},{16,0},{32,48},{48,32},{64,80},{80,64},{96,112},{112,96},{1... | collective-permute-start | bytes 153608 | tf_op jit(solution)/shard_map/ppermute | solution.py:474
  59.5 16.5 %all-to-all-start.1 = ((bf16[16,64,256]{2,1,0:T(8,128)(2,1)}), bf16[16,64,256]{2,1,0:T(8,128)(2,1)S(1)}, u32[]{:S(2)}, u32[]{:S(2)}) async-start(bf16[16,64,256]{2,1,0:T(8,128)(2,1)} %shard_map.145), calls=%async_computation.1 | async-start | bytes 1048576 | tf_op jit(solution)/shard_map/all_to_all | solution.py:599

commit v5 on v4

--- a/solution.py
+++ b/solution.py
@@ -49,7 +49,7 @@
 
 def by_rows(field_ref, flat):
     channels, rows, lanes = field_ref.shape
-    flat[...] = field_ref[...].astype(F32).reshape(channels * rows, lanes)
+    flat[: channels * rows, :] = field_ref[...].astype(F32).reshape(channels * rows, lanes)
     return [flat[pl.ds(row, channels, stride=rows), :] for row in range(rows)]
 
 
@@ -352,10 +352,10 @@
     def picked(first_row, first_tap, count):
         tap = inside - first_row + first_tap + second * HALF_TAPS
         pick = (col == tap) & (inside >= first_row) & (inside < first_row + count)
-        return nt_dot(jnp.where(pick, 1.0, 0.0).astype(BF), moved[...].astype(BF))
+        return nt_dot(jnp.where(pick, 1.0, 0.0).astype(BF), moved[:wide, :].astype(BF))
 
     moved[...] = jnp.zeros_like(moved)
-    moved[:channels, :] = sums[...]
+    moved[:channels, :] = sums[:channels, :]
     turned = picked(block - 1 - WHOLE_ROWS, 0, WHOLE_ROWS)
     moved[...] = jnp.zeros_like(moved)
     cut = channels // 4
@@ -370,7 +370,7 @@
 def message_body(own_ref, got_ref, out_ref, total, piece):
     hidden, deep = own_ref.shape
     share = hidden // out_ref.shape[0]
-    total[...] = own_ref[...] + got_ref[...].astype(F32)
+    total[:hidden, :] = own_ref[...] + got_ref[...].astype(F32)
     piece[...] = jnp.zeros_like(piece)
     for k in range(out_ref.shape[0]):
         piece[:share, :deep] = total[k * share : (k + 1) * share, :]
@@ -392,14 +392,14 @@
         out_ref[k] = total
 
 
-def final_body(parts_ref, ge_ref, gp_ref, gk_ref, gg_ref, gb_ref, halves):
+def final_body(parts_ref, ge_ref, gp_ref, gk_ref, gg_ref, gb_ref, halves, taps):
     share, channels = ge_ref.shape
     _, depth, wide = parts_ref.shape
     for k in range(2):
         total = parts_ref[k].astype(F32)
         for j in range(k + 2, parts_ref.shape[0], 2):
             total = total + parts_ref[j].astype(F32)
-        halves[k] = total
+        halves[k, :depth, :] = total
     ge_ref[...] = halves[0, :share, :channels]
     gp_ref[...] = halves[1, :share, :channels]
     cut = channels // 4
@@ -407,20 +407,21 @@
     for k in range(2):
         start = k * HALF_TAPS
         whole = depth - 1 - WHOLE_ROWS
-        gk_ref[start : start + WHOLE_ROWS, :] = halves[k, whole : depth - 1, :channels]
+        taps[start : start + WHOLE_ROWS, :] = halves[k, whole : depth - 1, :]
         rest = jnp.zeros((16, wide), F32)
         for q in range(4):
             value = halves[k, q * CUT_ROWS : q * CUT_ROWS + 16, :]
             value = pltpu.roll(value, (q * cut - SPARE_LANE) % wide, 1)
             rest = jnp.where((lane >= q * cut) & (lane < (q + 1) * cut), value, rest)
-        count = min(CUT_ROWS, TAPS * TAPS - start - WHOLE_ROWS)
         start = start + WHOLE_ROWS
-        gk_ref[start : start + count, :] = rest[:count, :channels]
+        taps[start : start + 16, :] = rest
+    gk_ref[...] = taps[: TAPS * TAPS, :channels]
     gg_ref[...] = rest[CUT_ROWS - 1 : CUT_ROWS, :channels]
     pick = lax.broadcasted_iota(jnp.int32, (8, wide), 1) == channels
     pick = jnp.where(pick, 1.0, 0.0).astype(BF)
-    high = halves[0].astype(BF)
-    low = (halves[0] - high.astype(F32)).astype(BF)
+    rows = halves[0, :depth, :]
+    high = rows.astype(BF)
+    low = (rows - high.astype(F32)).astype(BF)
     gb_ref[...] = (nt_dot(pick, high) + nt_dot(pick, low))[:1, :share]
 
 
@@ -428,7 +429,7 @@
     channels, rows, lanes = out_ref.shape
     for r in range(rows):
         flat[pl.ds(r, channels, stride=rows), :] = rows_ref[r]
-    out_ref[...] = flat[...].reshape(channels, rows, lanes).astype(BF)
+    out_ref[...] = flat[: channels * rows, :].reshape(channels, rows, lanes).astype(BF)
 
 
 def backward_body(
@@ -463,7 +464,7 @@
     for r in range(rows):
         mask = mask_ref[r : r + 1, :].astype(F32)
         flat[pl.ds(r, channels, stride=rows), :] = g_ref[r].astype(F32) + mask * back[r]
-    out_ref[...] = flat[...].reshape(channels, rows, lanes).astype(BF)
+    out_ref[...] = flat[: channels * rows, :].reshape(channels, rows, lanes).astype(BF)
 
 
 def swap_lon(pack):
@@ -495,7 +496,7 @@
     full = (rows, channels, lanes)
     edges = (HALO, channels, lanes)
     tile = (channels, lanes)
-    flat = pltpu.VMEM((channels * rows, lanes), F32)
+    flat = pltpu.VMEM(((channels + 1) * rows, lanes), F32)
     ext_s = pltpu.VMEM((rows + 2 * HALO, channels, lanes), F32)
     edge_s = pltpu.VMEM(tile, F32)
     lat = lax.axis_index("lat")
@@ -571,7 +572,12 @@
     taps_own, taps_other = kernel_call(
         taps_body,
         [((depth, wide), F32), ((depth, wide), BF)],
-        [ext_s, pltpu.VMEM(full, F32), edge_s, pltpu.VMEM((wide, lanes), F32)],
+        [
+            ext_s,
+            pltpu.VMEM(full, F32),
+            pltpu.VMEM((channels + 16, lanes), F32),
+            pltpu.VMEM((wide + 16, lanes), F32),
+        ],
         n_in=7,
         micros=6,
     )(place, masked, near, far, wings, back_mixed, gain)
@@ -580,7 +586,7 @@
     (message,) = kernel_call(
         message_body,
         [((n_lon, depth, wide), BF)],
-        [pltpu.VMEM((hidden, deep), F32), pltpu.VMEM((depth, wide), F32)],
+        [pltpu.VMEM((hidden + 16, deep), F32), pltpu.VMEM((depth, wide), F32)],
         n_in=2,
     )(own, got)
     (message,) = kernel_call(add_taps_body, [((n_lon, depth, wide), BF)], n_in=3)(
@@ -617,7 +623,7 @@
             ((1, channels), F32),
             ((1, share), F32),
         ],
-        [pltpu.VMEM((2, depth, wide), F32)],
+        [pltpu.VMEM((2, depth + 16, wide), F32), pltpu.VMEM((depth + 16, wide), F32)],
         n_in=1,
     )(parts)
     return (

time: 77.2 us -> 77.2 us (level)
  no operation moved by 1% of the time
where the time goes in v5:
time: 77.2 us; the launch traced here: 76.8 us
  starting transfers between devices  34.6 us (45%)
  Pallas kernels  26.6 us (34%)
  waiting for transfers between devices  12 us (16%)
  local copies, waits for them, and re-layouts  2.72 us (4%)
  between operations  0.91 us (1%)
    ppermute x2, starting transfers between devices, swap_lon(): from_far = lax.ppermute(pack, 'lon', far)  14.4 us
    pallas_call x1, Pallas kernels, shards(): kernel_call(main_body, [(full, F32), (full, BF), (edges, BF), (edges, BF)...  8.91 us
    pallas_call x1, Pallas kernels, shards(): kernel_call(backward_body, [((channels, rows, lanes), BF)], [ext_s, edge_...  7.14 us
    all_to_all x1, starting transfers between devices, shards(): parts = lax.all_to_all(copies, 'lat', 0, 0)  6.54 us
    ppermute x6, starting transfers between devices, swap_lat(): return (lax.ppermute(second, 'lat', near), lax.ppermute(first, 'lat', far))  5.52 us
    all_to_all x1, starting transfers between devices, shards(): parts = lax.all_to_all(message, 'lon', 0, 0)  5.13 us
    ppermute x6, waiting for transfers between devices, swap_lat(): return (lax.ppermute(second, 'lat', near), lax.ppermute(first, 'lat', far))  4.94 us
    pallas_call x1, Pallas kernels, shards(): kernel_call(taps_body, [((depth, wide), F32), ((depth, wide), BF)], [ext_...  3.83 us
  transfers between devices with their start and end apart: 14, of which 5 were waited for; matrix products, arithmetic and copies ran while one was open for 0% of the time, Pallas kernels for 20%

profile of v5, /device:TPU:1, one launch (start us, length us, event | category | flops | bytes accessed | tf_op | source)
XLA Modules:
  0.0 76.8 jit_solution(7429787704677613346)
XLA Ops:
  0.7 0.1 select_convert_fusion.place_ref
  0.8 1.0 %copy-done = bf16[200,8,128]{2,1,0:T(8,128)(2,1)S(1)} copy-done((bf16[200,8,128]{2,1,0:T(8,128)(2,1)S(1)}, bf16[200,8,128]{2,1,0:T(8,128)(2,1)}, u32[]{:S(2)}) %copy-start) | copy-done | bytes 409624
  1.8 0.7 copy-done.6
  2.5 0.3 shard_map.135
  2.9 9.1 %collective-permute-start.3 = (bf16[200,128]{1,0:T(8,128)(2,1)S(1)}, bf16[200,128]{1,0:T(8,128)(2,1)S(1)}, u32[]{:S(2)}, u32[]{:S(2)}) collective-permute-start(bf16[200,128]{1,0:T(8,128)(2,1)S(1)} %get-tuple-element.46), channel_id=1, source_target_pairs={{0,240},{16,32},{32,16},{48,64},{64,48},{80,96},{96,80},{112,128},... | collective-permute-start | bytes 153608 | tf_op jit(solution)/shard_map/ppermute | solution.py:474
  12.0 1.0 %collective-permute-start = (bf16[3,200,128]{2,1,0:T(8,128)(2,1)S(1)}, bf16[3,200,128]{2,1,0:T(8,128)(2,1)S(1)}, u32[]{:S(2)}, u32[]{:S(2)}) collective-permute-start(bf16[3,200,128]{2,1,0:T(8,128)(2,1)S(1)} %get-tuple-element.44), channel_id=1, source_target_pairs={{0,1},{1,0},{2,3},{3,2},{4,5},{5,4},{6,7},{7,6},{8,9},{9,8},{10,11... | collective-permute-start | bytes 460808 | tf_op jit(solution)/shard_map/ppermute | solution.py:482
  12.9 1.1 %collective-permute-start.1 = (bf16[3,200,128]{2,1,0:T(8,128)(2,1)S(1)}, bf16[3,200,128]{2,1,0:T(8,128)(2,1)S(1)}, u32[]{:S(2)}, u32[]{:S(2)}) collective-permute-start(bf16[3,200,128]{2,1,0:T(8,128)(2,1)S(1)} %get-tuple-element.45), channel_id=1, source_target_pairs={{0,15},{1,2},{2,1},{3,4},{4,3},{5,6},{6,5},{7,8},{8,7},{9,10},{10,... | collective-permute-start | bytes 460808 | tf_op jit(solution)/shard_map/ppermute | solution.py:482
  14.0 1.0 %copy-done.1 = bf16[200,8,128]{2,1,0:T(8,128)(2,1)S(1)} copy-done((bf16[200,8,128]{2,1,0:T(8,128)(2,1)S(1)}, bf16[200,8,128]{2,1,0:T(8,128)(2,1)}, u32[]{:S(2)}) %copy-start.1) | copy-done | bytes 409624
  15.0 0.2 shard_map.137.g_ref
  15.3 2.9 %collective-permute-start.5 = (bf16[200,128]{1,0:T(8,128)(2,1)S(1)}, bf16[200,128]{1,0:T(8,128)(2,1)S(1)}, u32[]{:S(2)}, u32[]{:S(2)}) collective-permute-start(bf16[200,128]{1,0:T(8,128)(2,1)S(1)} %shard_map.136.edge_own_ref), channel_id=1, source_target_pairs={{0,15},{1,2},{2,1},{3,4},{4,3},{5,6},{6,5},{7,8},{8,7},{9,10},{10,... | collective-permute-start | bytes 153608 | tf_op jit(solution)/shard_map/ppermute | solution.py:482
  18.3 2.0 %shard_map.138 = (f32[49,200,128]{2,1,0:T(8,128)S(1)}, f32[200,128]{1,0:T(8,128)S(1)}, f32[800,128]{1,0:T(8,128)S(1)}, bf16[800,200]{1,0:T(8,128)(2,1)S(1)}, bf16[800,200]{1,0:T(8,128)(2,1)S(1)}) custom-call(bf16[49,200]{1,0:T(8,128)(2,1)S(1)} %copy-done.4, f32[200]{0:T(256)S(1)} %copy-done.8, f32[800]{0:T(1024)S(1)} %copy-done.5, ...), custom_call_target="tpu_custom_call" | custom-call | flops 3000000000 | bytes 9000000 | tf_op jit(solution)/shard_map/pallas_call | solution.py:518
  20.3 8.9 %shard_map.139 = (f32[8,200,128]{2,1,0:T(8,128)S(1)}, bf16[8,200,128]{2,1,0:T(8,128)(2,1)S(1)}, bf16[3,200,128]{2,1,0:T(8,128)(2,1)S(1)}, bf16[3,200,128]{2,1,0:...) custom-call(f32[8,256]{1,0:T(8,128)S(1)} %select_convert_fusion.plac, ...), custom_call_target="tpu_custom_call" | custom-call | flops 12000000000 | bytes 36000000 | tf_op jit(solution)/shard_map/pallas_call | solution.py:531
  29.2 2.9 %collective-permute-start.8 = (bf16[800,208]{1,0:T(8,128)(2,1)S(1)}, bf16[800,208]{1,0:T(8,128)(2,1)S(1)}, u32[]{:S(2)}, u32[]{:S(2)}) collective-permute-start(bf16[800,208]{1,0:T(8,128)(2,1)S(1)} %get-tuple-element.64), channel_id=1, source_target_pairs={{0,1},{1,0},{2,3},{3,2},{4,5},{5,4},{6,7},{7,6},{8,9},{9,8},{10,11... | collective-permute-start | bytes 998408 | tf_op jit(solution)/shard_map/ppermute | solution.py:570
  32.1 3.8 %shard_map.142 = (f32[64,256]{1,0:T(8,128)S(1)}, bf16[64,256]{1,0:T(8,128)(2,1)S(1)}) custom-call(f32[8,256]{1,0:T(8,128)S(1)} %select_convert_fusion.place_ref, bf16[8,200,128]{2,1,0:T(8,128)(2,1)S(1)} %get-tuple-element.43.m_ref, bf16[3,200,128]{2,1,0:T(8,128)(2,1)S(1)} %collective-permute-done.near_ref, ...), custom_call_target="tpu_custom_call" | custom-call | flops 6000000000 | bytes 18000000 | tf_op jit(solution)/shard_map/pallas_call | solution.py:572
  36.0 0.1 collective-permute-start.9
  36.1 0.2 shard_map.143.rows_ref
  36.3 1.0 %collective-permute-done.9.taps_got_ref = bf16[64,256]{1,0:T(8,128)(2,1)S(1)} collective-permute-done((bf16[64,256]{1,0:T(8,128)(2,1)S(1)}, bf16[64,256]{1,0:T(8,128)(2,1)S(1)}, u32[]{:S(2)}, u32[]{:S(2)}) %collective-permute-start.9) | collective-permute-done | bytes 32800 | tf_op jit(solution)/shard_map/ppermute | solution.py:585
  37.3 0.9 %shard_map.144 = bf16[16,64,256]{2,1,0:T(8,128)(2,1)} custom-call(bf16[16,64,256]{2,1,0:T(8,128)(2,1)S(1)} %shard_map.143.rows_ref, f32[64,256]{1,0:T(8,128)S(1)} %get-tuple-element.69.taps_ref, bf16[64,256]{1,0:T(8,128)(2,1)S(1)} %collective-permute-done.9.taps_got_ref), custom_call_target="tpu_custom_call" | custom-call | flops 1000000000 | bytes 3000000 | tf_op jit(solution)/shard_map/pallas_call | solution.py:592
  38.2 5.1 %all-to-all-start = ((bf16[16,64,256]{2,1,0:T(8,128)(2,1)}), bf16[16,64,256]{2,1,0:T(8,128)(2,1)S(1)}, u32[]{:S(2)}, u32[]{:S(2)}) async-start(bf16[16,64,256]{2,1,0:T(8,128)(2,1)} %shard_map.144), calls=%async_computation | async-start | bytes 1048576 | tf_op jit(solution)/shard_map/all_to_all | solution.py:603
  43.3 0.5 collective-permute-start.6
  43.8 1.0 %collective-permute-done.6.near_ref = bf16[3,200,128]{2,1,0:T(8,128)(2,1)S(1)} collective-permute-done((bf16[3,200,128]{2,1,0:T(8,128)(2,1)S(1)}, bf16[3,200,128]{2,1,0:T(8,128)(2,1)S(1)}, u32[]{:S(2)}, u32[]{:S(2)}) %collective-permute-start.6) | collective-permute-done | bytes 153632 | tf_op jit(solution)/shard_map/ppermute | solution.py:482
  44.9 3.9 %collective-permute-done.7.far_ref = bf16[3,200,128]{2,1,0:T(8,128)(2,1)S(1)} collective-permute-done((bf16[3,200,128]{2,1,0:T(8,128)(2,1)S(1)}, bf16[3,200,128]{2,1,0:T(8,128)(2,1)S(1)}, u32[]{:S(2)}, u32[]{:S(2)}) %collective-permute-start.7) | collective-permute-done | bytes 153632 | tf_op jit(solution)/shard_map/ppermute | solution.py:482
  48.8 0.3 shard_map.140
  49.1 0.0 copy-start.7
  49.1 5.3 %collective-permute-start.11 = (bf16[200,128]{1,0:T(8,128)(2,1)S(1)}, bf16[200,128]{1,0:T(8,128)(2,1)S(1)}, u32[]{:S(2)}, u32[]{:S(2)}) collective-permute-start(bf16[200,128]{1,0:T(8,128)(2,1)S(1)} %shard_map.140), channel_id=1, source_target_pairs={{0,240},{16,32},{32,16},{48,64},{64,48},{80,96},{96,80},{112,128},... | collective-permute-start | bytes 153608 | tf_op jit(solution)/shard_map/ppermute | solution.py:474
  54.3 1.0 %shard_map.141 = bf16[200,8,128]{2,1,0:T(8,128)(2,1)} custom-call(f32[8,200,128]{2,1,0:T(8,128)S(1)} %get-tuple-element.62.rows_ref), custom_call_target="tpu_custom_call" | custom-call | flops 1000000000 | bytes 3000000 | tf_op jit(solution)/shard_map/pallas_call | solution.py:600
  55.4 3.2 %all-to-all-done.parts_ref = bf16[16,64,256]{2,1,0:T(8,128)(2,1)S(1)} async-done(((bf16[16,64,256]{2,1,0:T(8,128)(2,1)}), bf16[16,64,256]{2,1,0:T(8,128)(2,1)S(1)}, u32[]{:S(2)}, u32[]{:S(2)}) %all-to-all-start) | async-done | bytes 524320 | tf_op jit(solution)/shard_map/all_to_all | solution.py:603
  58.6 0.9 %shard_map.145 = bf16[16,64,256]{2,1,0:T(8,128)(2,1)} custom-call(bf16[16,64,256]{2,1,0:T(8,128)(2,1)S(1)} %all-to-all-done.parts_ref), custom_call_target="tpu_custom_call" | custom-call | flops 1000000000 | bytes 3000000 | tf_op jit(solution)/shard_map/pallas_call | solution.py:604
  59.5 6.5 %all-to-all-start.1 = ((bf16[16,64,256]{2,1,0:T(8,128)(2,1)}), bf16[16,64,256]{2,1,0:T(8,128)(2,1)S(1)}, u32[]{:S(2)}, u32[]{:S(2)}) async-start(bf16[16,64,256]{2,1,0:T(8,128)(2,1)} %shard_map.145), calls=%async_computation.1 | async-start | bytes 1048576 | tf_op jit(solution)/shard_map/all_to_all | solution.py:605
  66.1 7.1 %shard_map.146 = bf16[200,8,128]{2,1,0:T(8,128)(2,1)} custom-call(f32[8,256]{1,0:T(8,128)S(1)} %select_convert_fusion.place_ref, bf16[8,200,128]{2,1,0:T(8,128)(2,1)S(1)} %get-tuple-element.58.mid_ref.bm_ref, bf16[3,200,128]{2,1,0:T(8,128)(2,1)S(1)} %collective-permute-done.6.near_ref, bf16[3,200,128]{2,1,0:T(8,128)(2,1)S(1)} %collective-permute-done.7.far_ref, ...), custom_call_target="tpu_custom_call" | custom-call | flops 8000000000 | bytes 24000000 | tf_op jit(solution)/shard_map/pallas_call | solution.py:606
  73.2 2.8 %all-to-all-done.1.parts_ref = bf16[16,64,256]{2,1,0:T(8,128)(2,1)S(1)} async-done(((bf16[16,64,256]{2,1,0:T(8,128)(2,1)}), bf16[16,64,256]{2,1,0:T(8,128)(2,1)S(1)}, u32[]{:S(2)}, u32[]{:S(2)}) %all-to-all-start.1) | async-done | bytes 524320 | tf_op jit(solution)/shard_map/all_to_all | solution.py:605
  76.0 0.8 %shard_map.147 = (f32[50,200]{1,0:T(8,128)}, f32[50,200]{1,0:T(8,128)}, f32[49,200]{1,0:T(8,128)}, f32[1,200]{1,0:T(1,128)}, f32[1,50]{1,0:T(1,128)}) custom-call(bf16[16,64,256]{2,1,0:T(8,128)(2,1)S(1)} %all-to-all-done.1.parts_ref), custom_call_target="tpu_custom_call" | custom-call | flops 1000000000 | bytes 3000000 | tf_op jit(solution)/shard_map/pallas_call | solution.py:617
  (31 shorter events, 0.1 us)
Async XLA Ops:
  0.8 1.0 %copy-start = (bf16[200,8,128]{2,1,0:T(8,128)(2,1)S(1)}, bf16[200,8,128]{2,1,0:T(8,128)(2,1)}, u32[]{:S(2)}) copy-start(bf16[200,8,128]{2,1,0:T(8,128)(2,1)} %x_ref.1) | copy-start | bytes 1228804
  1.8 0.7 copy-start.6
  2.5 15.8 %copy-start.2 = (bf16[800,200]{0,1:T(8,128)(2,1)S(1)}, bf16[800,200]{0,1:T(8,128)(2,1)}, u32[]{:S(2)}) copy-start(bf16[800,200]{0,1:T(8,128)(2,1)} %param.12) | copy-start | bytes 960004
  2.5 15.8 %copy-start.3 = (bf16[800,200]{0,1:T(8,128)(2,1)S(1)}, bf16[800,200]{0,1:T(8,128)(2,1)}, u32[]{:S(2)}) copy-start(bf16[800,200]{0,1:T(8,128)(2,1)} %param.14) | copy-start | bytes 960004
  2.5 15.8 %copy-start.4 = (bf16[49,200]{1,0:T(8,128)(2,1)S(1)}, bf16[49,200]{1,0:T(8,128)(2,1)}, u32[]{:S(2)}) copy-start(bf16[49,200]{1,0:T(8,128)(2,1)} %taps_ref.2) | copy-start | bytes 58804
  2.5 15.8 %copy-start.5 = (f32[800]{0:T(1024)S(1)}, f32[800]{0:T(1024)}, u32[]{:S(2)}) copy-start(f32[800]{0:T(1024)} %bias_ref) | copy-start | bytes 9604
  2.5 15.8 %copy-start.8 = (f32[200]{0:T(256)S(1)}, f32[200]{0:T(256)}, u32[]{:S(2)}) copy-start(f32[200]{0:T(256)} %gain_ref) | copy-start | bytes 2404
  2.9 12.4 %collective-permute-start.3 = (bf16[200,128]{1,0:T(8,128)(2,1)S(1)}, bf16[200,128]{1,0:T(8,128)(2,1)S(1)}, u32[]{:S(2)}, u32[]{:S(2)}) collective-permute-start(bf16[200,128]{1,0:T(8,128)(2,1)S(1)} %get-tuple-element.46), channel_id=1, source_target_pairs={{0,240},{16,32},{32,16},{48,64},{64,48},{80,96},{96,80},{112,128},... | collective-permute-start | bytes 153608 | tf_op jit(solution)/shard_map/ppermute | solution.py:474
  12.0 3.3 %collective-permute-start.2 = (bf16[200,128]{1,0:T(8,128)(2,1)S(1)}, bf16[200,128]{1,0:T(8,128)(2,1)S(1)}, u32[]{:S(2)}, u32[]{:S(2)}) collective-permute-start(bf16[200,128]{1,0:T(8,128)(2,1)S(1)} %get-tuple-element.46), channel_id=1, source_target_pairs={{0,16},{16,0},{32,48},{48,32},{64,80},{80,64},{96,112},{112,96},{1... | collective-permute-start | bytes 153608 | tf_op jit(solution)/shard_map/ppermute | solution.py:475
  12.0 8.3 %collective-permute-start = (bf16[3,200,128]{2,1,0:T(8,128)(2,1)S(1)}, bf16[3,200,128]{2,1,0:T(8,128)(2,1)S(1)}, u32[]{:S(2)}, u32[]{:S(2)}) collective-permute-start(bf16[3,200,128]{2,1,0:T(8,128)(2,1)S(1)} %get-tuple-element.44), channel_id=1, source_target_pairs={{0,1},{1,0},{2,3},{3,2},{4,5},{5,4},{6,7},{7,6},{8,9},{9,8},{10,11... | collective-permute-start | bytes 460808 | tf_op jit(solution)/shard_map/ppermute | solution.py:482
  12.9 7.4 %collective-permute-start.1 = (bf16[3,200,128]{2,1,0:T(8,128)(2,1)S(1)}, bf16[3,200,128]{2,1,0:T(8,128)(2,1)S(1)}, u32[]{:S(2)}, u32[]{:S(2)}) collective-permute-start(bf16[3,200,128]{2,1,0:T(8,128)(2,1)S(1)} %get-tuple-element.45), channel_id=1, source_target_pairs={{0,15},{1,2},{2,1},{3,4},{4,3},{5,6},{6,5},{7,8},{8,7},{9,10},{10,... | collective-permute-start | bytes 460808 | tf_op jit(solution)/shard_map/ppermute | solution.py:482
  14.0 1.0 %copy-start.1 = (bf16[200,8,128]{2,1,0:T(8,128)(2,1)S(1)}, bf16[200,8,128]{2,1,0:T(8,128)(2,1)}, u32[]{:S(2)}) copy-start(bf16[200,8,128]{2,1,0:T(8,128)(2,1)} %cot_ref.1) | copy-start | bytes 1228804
  15.3 5.0 %collective-permute-start.5 = (bf16[200,128]{1,0:T(8,128)(2,1)S(1)}, bf16[200,128]{1,0:T(8,128)(2,1)S(1)}, u32[]{:S(2)}, u32[]{:S(2)}) collective-permute-start(bf16[200,128]{1,0:T(8,128)(2,1)S(1)} %shard_map.136.edge_own_ref), channel_id=1, source_target_pairs={{0,15},{1,2},{2,1},{3,4},{4,3},{5,6},{6,5},{7,8},{8,7},{9,10},{10,... | collective-permute-start | bytes 153608 | tf_op jit(solution)/shard_map/ppermute | solution.py:482
  18.2 2.0 %collective-permute-start.4 = (bf16[200,128]{1,0:T(8,128)(2,1)S(1)}, bf16[200,128]{1,0:T(8,128)(2,1)S(1)}, u32[]{:S(2)}, u32[]{:S(2)}) collective-permute-start(bf16[200,128]{1,0:T(8,128)(2,1)S(1)} %shard_map.136.edge_own_ref), channel_id=1, source_target_pairs={{0,1},{1,0},{2,3},{3,2},{4,5},{5,4},{6,7},{7,6},{8,9},{9,8},{10,11... | collective-permute-start | bytes 153608 | tf_op jit(solution)/shard_map/ppermute | solution.py:482
  29.2 6.7 %collective-permute-start.8 = (bf16[800,208]{1,0:T(8,128)(2,1)S(1)}, bf16[800,208]{1,0:T(8,128)(2,1)S(1)}, u32[]{:S(2)}, u32[]{:S(2)}) collective-permute-start(bf16[800,208]{1,0:T(8,128)(2,1)S(1)} %get-tuple-element.64), channel_id=1, source_target_pairs={{0,1},{1,0},{2,3},{3,2},{4,5},{5,4},{6,7},{7,6},{8,9},{9,8},{10,11... | collective-permute-start | bytes 998408 | tf_op jit(solution)/shard_map/ppermute | solution.py:570
  36.0 1.3 %collective-permute-start.9 = (bf16[64,256]{1,0:T(8,128)(2,1)S(1)}, bf16[64,256]{1,0:T(8,128)(2,1)S(1)}, u32[]{:S(2)}, u32[]{:S(2)}) collective-permute-start(bf16[64,256]{1,0:T(8,128)(2,1)S(1)} %get-tuple-element.70), channel_id=1, source_target_pairs={{0,1},{1,0},{2,3},{3,2},{4,5},{5,4},{6,7},{7,6},{8,9},{9,8},{10,11... | collective-permute-start | bytes 98312 | tf_op jit(solution)/shard_map/ppermute | solution.py:585
  38.2 20.4 %all-to-all-start = ((bf16[16,64,256]{2,1,0:T(8,128)(2,1)}), bf16[16,64,256]{2,1,0:T(8,128)(2,1)S(1)}, u32[]{:S(2)}, u32[]{:S(2)}) async-start(bf16[16,64,256]{2,1,0:T(8,128)(2,1)} %shard_map.144), calls=%async_computation | async-start | bytes 1048576 | tf_op jit(solution)/shard_map/all_to_all | solution.py:603
  43.3 1.5 %collective-permute-start.6 = (bf16[3,200,128]{2,1,0:T(8,128)(2,1)S(1)}, bf16[3,200,128]{2,1,0:T(8,128)(2,1)S(1)}, u32[]{:S(2)}, u32[]{:S(2)}) collective-permute-start(bf16[3,200,128]{2,1,0:T(8,128)(2,1)S(1)} %get-tuple-element.59), channel_id=1, source_target_pairs={{0,1},{1,0},{2,3},{3,2},{4,5},{5,4},{6,7},{7,6},{8,9},{9,8},{10,11... | collective-permute-start | bytes 460808 | tf_op jit(solution)/shard_map/ppermute | solution.py:482
  43.8 4.9 %collective-permute-start.7 = (bf16[3,200,128]{2,1,0:T(8,128)(2,1)S(1)}, bf16[3,200,128]{2,1,0:T(8,128)(2,1)S(1)}, u32[]{:S(2)}, u32[]{:S(2)}) collective-permute-start(bf16[3,200,128]{2,1,0:T(8,128)(2,1)S(1)} %get-tuple-element.60), channel_id=1, source_target_pairs={{0,15},{1,2},{2,1},{3,4},{4,3},{5,6},{6,5},{7,8},{8,7},{9,10},{10,... | collective-permute-start | bytes 460808 | tf_op jit(solution)/shard_map/ppermute | solution.py:482
  49.1 17.0 %copy-start.7 = (s32[8,128]{1,0:T(8,128)S(1)}, s32[8,128]{1,0:T(8,128)}, u32[]{:S(2)}) copy-start(s32[8,128]{1,0:T(8,128)} %mask_ref.7) | copy-start | bytes 12292
  49.1 17.0 %collective-permute-start.11 = (bf16[200,128]{1,0:T(8,128)(2,1)S(1)}, bf16[200,128]{1,0:T(8,128)(2,1)S(1)}, u32[]{:S(2)}, u32[]{:S(2)}) collective-permute-start(bf16[200,128]{1,0:T(8,128)(2,1)S(1)} %shard_map.140), channel_id=1, source_target_pairs={{0,240},{16,32},{32,16},{48,64},{64,48},{80,96},{96,80},{112,128},... | collective-permute-start | bytes 153608 | tf_op jit(solution)/shard_map/ppermute | solution.py:474
  54.3 11.7 %collective-permute-start.10 = (bf16[200,128]{1,0:T(8,128)(2,1)S(1)}, bf16[200,128]{1,0:T(8,128)(2,1)S(1)}, u32[]{:S(2)}, u32[]{:S(2)}) collective-permute-start(bf16[200,128]{1,0:T(8,128)(2,1)S(1)} %shard_map.140), channel_id=1, source_target_pairs={{0,16},{16,0},{32,48},{48,32},{64,80},{80,64},{96,112},{112,96},{1... | collective-permute-start | bytes 153608 | tf_op jit(solution)/shard_map/ppermute | solution.py:475
  59.5 16.5 %all-to-all-start.1 = ((bf16[16,64,256]{2,1,0:T(8,128)(2,1)}), bf16[16,64,256]{2,1,0:T(8,128)(2,1)S(1)}, u32[]{:S(2)}, u32[]{:S(2)}) async-start(bf16[16,64,256]{2,1,0:T(8,128)(2,1)} %shard_map.145), calls=%async_computation.1 | async-start | bytes 1048576 | tf_op jit(solution)/shard_map/all_to_all | solution.py:605

commit v6 on v5

--- a/solution.py
+++ b/solution.py
@@ -177,12 +177,13 @@
         ext[r] = value
 
 
-def line_up(edge, start, n_rows):
-    ends = edge[pl.ds(start, 8), :]
-    lanes = ends.shape[1]
-    return jnp.stack(
-        [ends] + [pltpu.roll(ends, lanes - 8 * r, 1) for r in range(1, n_rows)], axis=0
-    )
+def line_up(edge, wings):
+    channels, lanes = edge.shape
+    spare = jnp.zeros((-channels % 16, lanes), F32)
+    edge = jnp.concatenate([edge, spare], axis=0).astype(BF)
+    for r in range(wings.shape[0]):
+        turned = pltpu.roll(edge, lanes - 8 * r, 1) if r else edge
+        wings[r] = turned.astype(F32)[:channels]
 
 
 def joined(mid, wings):
@@ -236,7 +237,6 @@
     other_ref,
     wings_ref,
     ext,
-    edge,
     mixed,
     units,
     sides,
@@ -245,12 +245,11 @@
     hidden, deep = own_ref.shape
     pair = 2 * lanes
     fill_extended(ext, place_ref, m_ref, near_ref, far_ref)
-    edge[...] = all_edges(place_ref, edge_own_ref, edge_near_ref, edge_far_ref)
+    line_up(all_edges(place_ref, edge_own_ref, edge_near_ref, edge_far_ref), wings_ref)
 
     def conv_step(block, carry):
         start = pl.multiple_of(block * 8, 8)
-        wings = line_up(edge, start, ext.shape[0])
-        wings_ref[:, pl.ds(start, 8), :] = wings
+        wings = wings_ref[:, pl.ds(start, 8), :]
         mixed[:, pl.ds(start, 8), :] = convolve(ext, wings, spread_ref, start, rows, False)
         return carry
 
@@ -444,7 +443,7 @@
     taps_ref,
     out_ref,
     ext,
-    edge,
+    wings,
     back,
     flat,
     spread,
@@ -452,12 +451,12 @@
     rows, channels, lanes = bm_ref.shape
     spread_body(taps_ref, spread)
     fill_extended(ext, place_ref, bm_ref, near_ref, far_ref)
-    edge[...] = lon_edges(place_ref, lon_near_ref, lon_far_ref)
+    line_up(lon_edges(place_ref, lon_near_ref, lon_far_ref), wings)
 
     def step(block, carry):
         start = pl.multiple_of(block * 8, 8)
-        wings = line_up(edge, start, ext.shape[0])
-        back[:, pl.ds(start, 8), :] = convolve(ext, wings, spread, start, rows, True)
+        here = wings[:, pl.ds(start, 8), :]
+        back[:, pl.ds(start, 8), :] = convolve(ext, here, spread, start, rows, True)
         return carry
 
     lax.fori_loop(0, channels // 8, step, 0, unroll=5)
@@ -498,7 +497,6 @@
     tile = (channels, lanes)
     flat = pltpu.VMEM(((channels + 1) * rows, lanes), F32)
     ext_s = pltpu.VMEM((rows + 2 * HALO, channels, lanes), F32)
-    edge_s = pltpu.VMEM(tile, F32)
     lat = lax.axis_index("lat")
     kind = lax.broadcasted_iota(jnp.int32, (8, 256), 0)
     value = jnp.where(kind == 0, 1 - lat % 2, jnp.where(kind == 1, lat, n_lat - 1 - lat))
@@ -542,7 +540,6 @@
         ],
         [
             ext_s,
-            edge_s,
             pltpu.VMEM(full, F32),
             pltpu.VMEM((2, hidden, cells), BF),
             pltpu.VMEM((2, deep, cells), BF),
@@ -606,7 +603,7 @@
     (grad_state,) = kernel_call(
         backward_body,
         [((channels, rows, lanes), BF)],
-        [ext_s, edge_s, pltpu.VMEM(full, F32), flat, pltpu.VMEM((TAPS * TAPS, *tile), F32)],
+        [ext_s, ext_s, pltpu.VMEM(full, F32), flat, pltpu.VMEM((TAPS * TAPS, *tile), F32)],
         n_in=9,
         micros=8,
     )(

time: 77.2 us -> 76.4 us (0.990)
  Pallas kernels: 26.6 us -> 24.9 us
  waiting for transfers between devices: 12 us -> 12.8 us
    all_to_all x1, waiting for transfers between devices: 2.82 us -> 3.66 us  [shards(): parts = lax.all_to_all(copies, 'lat', 0, 0)]
    pallas_call x1, Pallas kernels: 7.14 us -> 6.3 us  [shards(): kernel_call(backward_body, [((channels, rows, lanes), BF)], [ext_s, ext_s...]
    pallas_call x1, Pallas kernels: 8.91 us -> 8.12 us  [shards(): kernel_call(main_body, [(full, F32), (full, BF), (edges, BF), (edges, BF)...]
  transfers between devices with their start and end apart: 14 -> 14, of which waited for: 5 -> 5; matrix products, arithmetic and copies ran while one was open for 0% -> 0% of each run, Pallas kernels for 20% -> 19%
where the time goes in v6:
time: 76.4 us; the launch traced here: 76 us
  starting transfers between devices  34.6 us (45%)
  Pallas kernels  24.9 us (33%)
  waiting for transfers between devices  12.8 us (17%)
  local copies, waits for them, and re-layouts  2.72 us (4%)
  between operations  0.91 us (1%)
    ppermute x2, starting transfers between devices, swap_lon(): from_far = lax.ppermute(pack, 'lon', far)  14.4 us
    pallas_call x1, Pallas kernels, shards(): kernel_call(main_body, [(full, F32), (full, BF), (edges, BF), (edges, BF)...  8.12 us
    all_to_all x1, starting transfers between devices, shards(): parts = lax.all_to_all(copies, 'lat', 0, 0)  6.54 us
    pallas_call x1, Pallas kernels, shards(): kernel_call(backward_body, [((channels, rows, lanes), BF)], [ext_s, ext_s...  6.3 us
    ppermute x6, starting transfers between devices, swap_lat(): return (lax.ppermute(second, 'lat', near), lax.ppermute(first, 'lat', far))  5.52 us
    all_to_all x1, starting transfers between devices, shards(): parts = lax.all_to_all(message, 'lon', 0, 0)  5.13 us
    ppermute x6, waiting for transfers between devices, swap_lat(): return (lax.ppermute(second, 'lat', near), lax.ppermute(first, 'lat', far))  4.94 us
    pallas_call x1, Pallas kernels, shards(): kernel_call(taps_body, [((depth, wide), F32), ((depth, wide), BF)], [ext_...  3.83 us
  transfers between devices with their start and end apart: 14, of which 5 were waited for; matrix products, arithmetic and copies ran while one was open for 0% of the time, Pallas kernels for 19%

profile of v6, /device:TPU:1, one launch (start us, length us, event | category | flops | bytes accessed | tf_op | source)
XLA Modules:
  0.0 76.0 jit_solution(3363835167133851901)
XLA Ops:
  0.7 0.1 select_convert_fusion.place_ref
  0.8 1.0 %copy-done = bf16[200,8,128]{2,1,0:T(8,128)(2,1)S(1)} copy-done((bf16[200,8,128]{2,1,0:T(8,128)(2,1)S(1)}, bf16[200,8,128]{2,1,0:T(8,128)(2,1)}, u32[]{:S(2)}) %copy-start) | copy-done | bytes 409624
  1.8 0.7 copy-done.6
  2.5 0.3 shard_map.135
  2.9 9.1 %collective-permute-start.3 = (bf16[200,128]{1,0:T(8,128)(2,1)S(1)}, bf16[200,128]{1,0:T(8,128)(2,1)S(1)}, u32[]{:S(2)}, u32[]{:S(2)}) collective-permute-start(bf16[200,128]{1,0:T(8,128)(2,1)S(1)} %get-tuple-element.46), channel_id=1, source_target_pairs={{0,240},{16,32},{32,16},{48,64},{64,48},{80,96},{96,80},{112,128},... | collective-permute-start | bytes 153608 | tf_op jit(solution)/shard_map/ppermute | solution.py:473
  12.0 1.0 %collective-permute-start = (bf16[3,200,128]{2,1,0:T(8,128)(2,1)S(1)}, bf16[3,200,128]{2,1,0:T(8,128)(2,1)S(1)}, u32[]{:S(2)}, u32[]{:S(2)}) collective-permute-start(bf16[3,200,128]{2,1,0:T(8,128)(2,1)S(1)} %get-tuple-element.44), channel_id=1, source_target_pairs={{0,1},{1,0},{2,3},{3,2},{4,5},{5,4},{6,7},{7,6},{8,9},{9,8},{10,11... | collective-permute-start | bytes 460808 | tf_op jit(solution)/shard_map/ppermute | solution.py:481
  12.9 1.1 %collective-permute-start.1 = (bf16[3,200,128]{2,1,0:T(8,128)(2,1)S(1)}, bf16[3,200,128]{2,1,0:T(8,128)(2,1)S(1)}, u32[]{:S(2)}, u32[]{:S(2)}) collective-permute-start(bf16[3,200,128]{2,1,0:T(8,128)(2,1)S(1)} %get-tuple-element.45), channel_id=1, source_target_pairs={{0,15},{1,2},{2,1},{3,4},{4,3},{5,6},{6,5},{7,8},{8,7},{9,10},{10,... | collective-permute-start | bytes 460808 | tf_op jit(solution)/shard_map/ppermute | solution.py:481
  14.0 1.0 %copy-done.1 = bf16[200,8,128]{2,1,0:T(8,128)(2,1)S(1)} copy-done((bf16[200,8,128]{2,1,0:T(8,128)(2,1)S(1)}, bf16[200,8,128]{2,1,0:T(8,128)(2,1)}, u32[]{:S(2)}) %copy-start.1) | copy-done | bytes 409624
  15.0 0.2 shard_map.137.g_ref
  15.3 2.9 %collective-permute-start.5 = (bf16[200,128]{1,0:T(8,128)(2,1)S(1)}, bf16[200,128]{1,0:T(8,128)(2,1)S(1)}, u32[]{:S(2)}, u32[]{:S(2)}) collective-permute-start(bf16[200,128]{1,0:T(8,128)(2,1)S(1)} %shard_map.136.edge_own_ref), channel_id=1, source_target_pairs={{0,15},{1,2},{2,1},{3,4},{4,3},{5,6},{6,5},{7,8},{8,7},{9,10},{10,... | collective-permute-start | bytes 153608 | tf_op jit(solution)/shard_map/ppermute | solution.py:481
  18.3 2.0 %shard_map.138 = (f32[49,200,128]{2,1,0:T(8,128)S(1)}, f32[200,128]{1,0:T(8,128)S(1)}, f32[800,128]{1,0:T(8,128)S(1)}, bf16[800,200]{1,0:T(8,128)(2,1)S(1)}, bf16[800,200]{1,0:T(8,128)(2,1)S(1)}) custom-call(bf16[49,200]{1,0:T(8,128)(2,1)S(1)} %copy-done.4, f32[200]{0:T(256)S(1)} %copy-done.8, f32[800]{0:T(1024)S(1)} %copy-done.5, ...), custom_call_target="tpu_custom_call" | custom-call | flops 3000000000 | bytes 9000000 | tf_op jit(solution)/shard_map/pallas_call | solution.py:516
  20.3 8.1 %shard_map.139 = (f32[8,200,128]{2,1,0:T(8,128)S(1)}, bf16[8,200,128]{2,1,0:T(8,128)(2,1)S(1)}, bf16[3,200,128]{2,1,0:T(8,128)(2,1)S(1)}, bf16[3,200,128]{2,1,0:...) custom-call(f32[8,256]{1,0:T(8,128)S(1)} %select_convert_fusion.plac, ...), custom_call_target="tpu_custom_call" | custom-call | flops 12000000000 | bytes 36000000 | tf_op jit(solution)/shard_map/pallas_call | solution.py:529
  28.4 2.9 %collective-permute-start.8 = (bf16[800,208]{1,0:T(8,128)(2,1)S(1)}, bf16[800,208]{1,0:T(8,128)(2,1)S(1)}, u32[]{:S(2)}, u32[]{:S(2)}) collective-permute-start(bf16[800,208]{1,0:T(8,128)(2,1)S(1)} %get-tuple-element.64), channel_id=1, source_target_pairs={{0,1},{1,0},{2,3},{3,2},{4,5},{5,4},{6,7},{7,6},{8,9},{9,8},{10,11... | collective-permute-start | bytes 998408 | tf_op jit(solution)/shard_map/ppermute | solution.py:567
  31.3 3.8 %shard_map.142 = (f32[64,256]{1,0:T(8,128)S(1)}, bf16[64,256]{1,0:T(8,128)(2,1)S(1)}) custom-call(f32[8,256]{1,0:T(8,128)S(1)} %select_convert_fusion.place_ref, bf16[8,200,128]{2,1,0:T(8,128)(2,1)S(1)} %get-tuple-element.43.m_ref, bf16[3,200,128]{2,1,0:T(8,128)(2,1)S(1)} %collective-permute-done.near_ref, ...), custom_call_target="tpu_custom_call" | custom-call | flops 6000000000 | bytes 18000000 | tf_op jit(solution)/shard_map/pallas_call | solution.py:569
  35.2 0.1 collective-permute-start.9
  35.3 0.2 shard_map.143.rows_ref
  35.5 1.0 %collective-permute-done.9.taps_got_ref = bf16[64,256]{1,0:T(8,128)(2,1)S(1)} collective-permute-done((bf16[64,256]{1,0:T(8,128)(2,1)S(1)}, bf16[64,256]{1,0:T(8,128)(2,1)S(1)}, u32[]{:S(2)}, u32[]{:S(2)}) %collective-permute-start.9) | collective-permute-done | bytes 32800 | tf_op jit(solution)/shard_map/ppermute | solution.py:582
  36.5 0.9 %shard_map.144 = bf16[16,64,256]{2,1,0:T(8,128)(2,1)} custom-call(bf16[16,64,256]{2,1,0:T(8,128)(2,1)S(1)} %shard_map.143.rows_ref, f32[64,256]{1,0:T(8,128)S(1)} %get-tuple-element.69.taps_ref, bf16[64,256]{1,0:T(8,128)(2,1)S(1)} %collective-permute-done.9.taps_got_ref), custom_call_target="tpu_custom_call" | custom-call | flops 1000000000 | bytes 3000000 | tf_op jit(solution)/shard_map/pallas_call | solution.py:589
  37.4 5.1 %all-to-all-start = ((bf16[16,64,256]{2,1,0:T(8,128)(2,1)}), bf16[16,64,256]{2,1,0:T(8,128)(2,1)S(1)}, u32[]{:S(2)}, u32[]{:S(2)}) async-start(bf16[16,64,256]{2,1,0:T(8,128)(2,1)} %shard_map.144), calls=%async_computation | async-start | bytes 1048576 | tf_op jit(solution)/shard_map/all_to_all | solution.py:600
  42.5 0.5 collective-permute-start.6
  43.1 1.0 %collective-permute-done.6.near_ref = bf16[3,200,128]{2,1,0:T(8,128)(2,1)S(1)} collective-permute-done((bf16[3,200,128]{2,1,0:T(8,128)(2,1)S(1)}, bf16[3,200,128]{2,1,0:T(8,128)(2,1)S(1)}, u32[]{:S(2)}, u32[]{:S(2)}) %collective-permute-start.6) | collective-permute-done | bytes 153632 | tf_op jit(solution)/shard_map/ppermute | solution.py:481
  44.1 3.9 %collective-permute-done.7.far_ref = bf16[3,200,128]{2,1,0:T(8,128)(2,1)S(1)} collective-permute-done((bf16[3,200,128]{2,1,0:T(8,128)(2,1)S(1)}, bf16[3,200,128]{2,1,0:T(8,128)(2,1)S(1)}, u32[]{:S(2)}, u32[]{:S(2)}) %collective-permute-start.7) | collective-permute-done | bytes 153632 | tf_op jit(solution)/shard_map/ppermute | solution.py:481
  48.0 0.3 shard_map.140
  48.3 0.0 copy-start.7
  48.3 5.3 %collective-permute-start.11 = (bf16[200,128]{1,0:T(8,128)(2,1)S(1)}, bf16[200,128]{1,0:T(8,128)(2,1)S(1)}, u32[]{:S(2)}, u32[]{:S(2)}) collective-permute-start(bf16[200,128]{1,0:T(8,128)(2,1)S(1)} %shard_map.140), channel_id=1, source_target_pairs={{0,240},{16,32},{32,16},{48,64},{64,48},{80,96},{96,80},{112,128},... | collective-permute-start | bytes 153608 | tf_op jit(solution)/shard_map/ppermute | solution.py:473
  53.6 1.0 %shard_map.141 = bf16[200,8,128]{2,1,0:T(8,128)(2,1)} custom-call(f32[8,200,128]{2,1,0:T(8,128)S(1)} %get-tuple-element.62.rows_ref), custom_call_target="tpu_custom_call" | custom-call | flops 1000000000 | bytes 3000000 | tf_op jit(solution)/shard_map/pallas_call | solution.py:597
  54.6 3.2 %all-to-all-done.parts_ref = bf16[16,64,256]{2,1,0:T(8,128)(2,1)S(1)} async-done(((bf16[16,64,256]{2,1,0:T(8,128)(2,1)}), bf16[16,64,256]{2,1,0:T(8,128)(2,1)S(1)}, u32[]{:S(2)}, u32[]{:S(2)}) %all-to-all-start) | async-done | bytes 524320 | tf_op jit(solution)/shard_map/all_to_all | solution.py:600
  57.8 0.9 %shard_map.145 = bf16[16,64,256]{2,1,0:T(8,128)(2,1)} custom-call(bf16[16,64,256]{2,1,0:T(8,128)(2,1)S(1)} %all-to-all-done.parts_ref), custom_call_target="tpu_custom_call" | custom-call | flops 1000000000 | bytes 3000000 | tf_op jit(solution)/shard_map/pallas_call | solution.py:601
  58.7 6.5 %all-to-all-start.1 = ((bf16[16,64,256]{2,1,0:T(8,128)(2,1)}), bf16[16,64,256]{2,1,0:T(8,128)(2,1)S(1)}, u32[]{:S(2)}, u32[]{:S(2)}) async-start(bf16[16,64,256]{2,1,0:T(8,128)(2,1)} %shard_map.145), calls=%async_computation.1 | async-start | bytes 1048576 | tf_op jit(solution)/shard_map/all_to_all | solution.py:602
  65.3 6.3 %shard_map.146 = bf16[200,8,128]{2,1,0:T(8,128)(2,1)} custom-call(f32[8,256]{1,0:T(8,128)S(1)} %select_convert_fusion.place_ref, bf16[8,200,128]{2,1,0:T(8,128)(2,1)S(1)} %get-tuple-element.58.mid_ref.bm_ref, bf16[3,200,128]{2,1,0:T(8,128)(2,1)S(1)} %collective-permute-done.6.near_ref, bf16[3,200,128]{2,1,0:T(8,128)(2,1)S(1)} %collective-permute-done.7.far_ref, ...), custom_call_target="tpu_custom_call" | custom-call | flops 8000000000 | bytes 24000000 | tf_op jit(solution)/shard_map/pallas_call | solution.py:603
  71.6 3.7 %all-to-all-done.1.parts_ref = bf16[16,64,256]{2,1,0:T(8,128)(2,1)S(1)} async-done(((bf16[16,64,256]{2,1,0:T(8,128)(2,1)}), bf16[16,64,256]{2,1,0:T(8,128)(2,1)S(1)}, u32[]{:S(2)}, u32[]{:S(2)}) %all-to-all-start.1) | async-done | bytes 524320 | tf_op jit(solution)/shard_map/all_to_all | solution.py:602
  75.2 0.8 %shard_map.147 = (f32[50,200]{1,0:T(8,128)}, f32[50,200]{1,0:T(8,128)}, f32[49,200]{1,0:T(8,128)}, f32[1,200]{1,0:T(1,128)}, f32[1,50]{1,0:T(1,128)}) custom-call(bf16[16,64,256]{2,1,0:T(8,128)(2,1)S(1)} %all-to-all-done.1.parts_ref), custom_call_target="tpu_custom_call" | custom-call | flops 1000000000 | bytes 3000000 | tf_op jit(solution)/shard_map/pallas_call | solution.py:614
  (31 shorter events, 0.1 us)
Async XLA Ops:
  0.8 1.0 %copy-start = (bf16[200,8,128]{2,1,0:T(8,128)(2,1)S(1)}, bf16[200,8,128]{2,1,0:T(8,128)(2,1)}, u32[]{:S(2)}) copy-start(bf16[200,8,128]{2,1,0:T(8,128)(2,1)} %x_ref.1) | copy-start | bytes 1228804
  1.8 0.7 copy-start.6
  2.5 15.8 %copy-start.2 = (bf16[800,200]{0,1:T(8,128)(2,1)S(1)}, bf16[800,200]{0,1:T(8,128)(2,1)}, u32[]{:S(2)}) copy-start(bf16[800,200]{0,1:T(8,128)(2,1)} %param.12) | copy-start | bytes 960004
  2.5 15.8 %copy-start.3 = (bf16[800,200]{0,1:T(8,128)(2,1)S(1)}, bf16[800,200]{0,1:T(8,128)(2,1)}, u32[]{:S(2)}) copy-start(bf16[800,200]{0,1:T(8,128)(2,1)} %param.14) | copy-start | bytes 960004
  2.5 15.8 %copy-start.4 = (bf16[49,200]{1,0:T(8,128)(2,1)S(1)}, bf16[49,200]{1,0:T(8,128)(2,1)}, u32[]{:S(2)}) copy-start(bf16[49,200]{1,0:T(8,128)(2,1)} %taps_ref.2) | copy-start | bytes 58804
  2.5 15.8 %copy-start.5 = (f32[800]{0:T(1024)S(1)}, f32[800]{0:T(1024)}, u32[]{:S(2)}) copy-start(f32[800]{0:T(1024)} %bias_ref) | copy-start | bytes 9604
  2.5 15.8 %copy-start.8 = (f32[200]{0:T(256)S(1)}, f32[200]{0:T(256)}, u32[]{:S(2)}) copy-start(f32[200]{0:T(256)} %gain_ref) | copy-start | bytes 2404
  2.9 12.4 %collective-permute-start.3 = (bf16[200,128]{1,0:T(8,128)(2,1)S(1)}, bf16[200,128]{1,0:T(8,128)(2,1)S(1)}, u32[]{:S(2)}, u32[]{:S(2)}) collective-permute-start(bf16[200,128]{1,0:T(8,128)(2,1)S(1)} %get-tuple-element.46), channel_id=1, source_target_pairs={{0,240},{16,32},{32,16},{48,64},{64,48},{80,96},{96,80},{112,128},... | collective-permute-start | bytes 153608 | tf_op jit(solution)/shard_map/ppermute | solution.py:473
  12.0 3.3 %collective-permute-start.2 = (bf16[200,128]{1,0:T(8,128)(2,1)S(1)}, bf16[200,128]{1,0:T(8,128)(2,1)S(1)}, u32[]{:S(2)}, u32[]{:S(2)}) collective-permute-start(bf16[200,128]{1,0:T(8,128)(2,1)S(1)} %get-tuple-element.46), channel_id=1, source_target_pairs={{0,16},{16,0},{32,48},{48,32},{64,80},{80,64},{96,112},{112,96},{1... | collective-permute-start | bytes 153608 | tf_op jit(solution)/shard_map/ppermute | solution.py:474
  12.0 8.3 %collective-permute-start = (bf16[3,200,128]{2,1,0:T(8,128)(2,1)S(1)}, bf16[3,200,128]{2,1,0:T(8,128)(2,1)S(1)}, u32[]{:S(2)}, u32[]{:S(2)}) collective-permute-start(bf16[3,200,128]{2,1,0:T(8,128)(2,1)S(1)} %get-tuple-element.44), channel_id=1, source_target_pairs={{0,1},{1,0},{2,3},{3,2},{4,5},{5,4},{6,7},{7,6},{8,9},{9,8},{10,11... | collective-permute-start | bytes 460808 | tf_op jit(solution)/shard_map/ppermute | solution.py:481
  12.9 7.4 %collective-permute-start.1 = (bf16[3,200,128]{2,1,0:T(8,128)(2,1)S(1)}, bf16[3,200,128]{2,1,0:T(8,128)(2,1)S(1)}, u32[]{:S(2)}, u32[]{:S(2)}) collective-permute-start(bf16[3,200,128]{2,1,0:T(8,128)(2,1)S(1)} %get-tuple-element.45), channel_id=1, source_target_pairs={{0,15},{1,2},{2,1},{3,4},{4,3},{5,6},{6,5},{7,8},{8,7},{9,10},{10,... | collective-permute-start | bytes 460808 | tf_op jit(solution)/shard_map/ppermute | solution.py:481
  14.0 1.0 %copy-start.1 = (bf16[200,8,128]{2,1,0:T(8,128)(2,1)S(1)}, bf16[200,8,128]{2,1,0:T(8,128)(2,1)}, u32[]{:S(2)}) copy-start(bf16[200,8,128]{2,1,0:T(8,128)(2,1)} %cot_ref.1) | copy-start | bytes 1228804
  15.3 5.0 %collective-permute-start.5 = (bf16[200,128]{1,0:T(8,128)(2,1)S(1)}, bf16[200,128]{1,0:T(8,128)(2,1)S(1)}, u32[]{:S(2)}, u32[]{:S(2)}) collective-permute-start(bf16[200,128]{1,0:T(8,128)(2,1)S(1)} %shard_map.136.edge_own_ref), channel_id=1, source_target_pairs={{0,15},{1,2},{2,1},{3,4},{4,3},{5,6},{6,5},{7,8},{8,7},{9,10},{10,... | collective-permute-start | bytes 153608 | tf_op jit(solution)/shard_map/ppermute | solution.py:481
  18.2 2.0 %collective-permute-start.4 = (bf16[200,128]{1,0:T(8,128)(2,1)S(1)}, bf16[200,128]{1,0:T(8,128)(2,1)S(1)}, u32[]{:S(2)}, u32[]{:S(2)}) collective-permute-start(bf16[200,128]{1,0:T(8,128)(2,1)S(1)} %shard_map.136.edge_own_ref), channel_id=1, source_target_pairs={{0,1},{1,0},{2,3},{3,2},{4,5},{5,4},{6,7},{7,6},{8,9},{9,8},{10,11... | collective-permute-start | bytes 153608 | tf_op jit(solution)/shard_map/ppermute | solution.py:481
  28.4 6.7 %collective-permute-start.8 = (bf16[800,208]{1,0:T(8,128)(2,1)S(1)}, bf16[800,208]{1,0:T(8,128)(2,1)S(1)}, u32[]{:S(2)}, u32[]{:S(2)}) collective-permute-start(bf16[800,208]{1,0:T(8,128)(2,1)S(1)} %get-tuple-element.64), channel_id=1, source_target_pairs={{0,1},{1,0},{2,3},{3,2},{4,5},{5,4},{6,7},{7,6},{8,9},{9,8},{10,11... | collective-permute-start | bytes 998408 | tf_op jit(solution)/shard_map/ppermute | solution.py:567
  35.2 1.3 %collective-permute-start.9 = (bf16[64,256]{1,0:T(8,128)(2,1)S(1)}, bf16[64,256]{1,0:T(8,128)(2,1)S(1)}, u32[]{:S(2)}, u32[]{:S(2)}) collective-permute-start(bf16[64,256]{1,0:T(8,128)(2,1)S(1)} %get-tuple-element.70), channel_id=1, source_target_pairs={{0,1},{1,0},{2,3},{3,2},{4,5},{5,4},{6,7},{7,6},{8,9},{9,8},{10,11... | collective-permute-start | bytes 98312 | tf_op jit(solution)/shard_map/ppermute | solution.py:582
  37.4 20.4 %all-to-all-start = ((bf16[16,64,256]{2,1,0:T(8,128)(2,1)}), bf16[16,64,256]{2,1,0:T(8,128)(2,1)S(1)}, u32[]{:S(2)}, u32[]{:S(2)}) async-start(bf16[16,64,256]{2,1,0:T(8,128)(2,1)} %shard_map.144), calls=%async_computation | async-start | bytes 1048576 | tf_op jit(solution)/shard_map/all_to_all | solution.py:600
  42.5 1.5 %collective-permute-start.6 = (bf16[3,200,128]{2,1,0:T(8,128)(2,1)S(1)}, bf16[3,200,128]{2,1,0:T(8,128)(2,1)S(1)}, u32[]{:S(2)}, u32[]{:S(2)}) collective-permute-start(bf16[3,200,128]{2,1,0:T(8,128)(2,1)S(1)} %get-tuple-element.59), channel_id=1, source_target_pairs={{0,1},{1,0},{2,3},{3,2},{4,5},{5,4},{6,7},{7,6},{8,9},{9,8},{10,11... | collective-permute-start | bytes 460808 | tf_op jit(solution)/shard_map/ppermute | solution.py:481
  43.1 4.9 %collective-permute-start.7 = (bf16[3,200,128]{2,1,0:T(8,128)(2,1)S(1)}, bf16[3,200,128]{2,1,0:T(8,128)(2,1)S(1)}, u32[]{:S(2)}, u32[]{:S(2)}) collective-permute-start(bf16[3,200,128]{2,1,0:T(8,128)(2,1)S(1)} %get-tuple-element.60), channel_id=1, source_target_pairs={{0,15},{1,2},{2,1},{3,4},{4,3},{5,6},{6,5},{7,8},{8,7},{9,10},{10,... | collective-permute-start | bytes 460808 | tf_op jit(solution)/shard_map/ppermute | solution.py:481
  48.3 17.0 %copy-start.7 = (s32[8,128]{1,0:T(8,128)S(1)}, s32[8,128]{1,0:T(8,128)}, u32[]{:S(2)}) copy-start(s32[8,128]{1,0:T(8,128)} %mask_ref.7) | copy-start | bytes 12292
  48.3 17.0 %collective-permute-start.11 = (bf16[200,128]{1,0:T(8,128)(2,1)S(1)}, bf16[200,128]{1,0:T(8,128)(2,1)S(1)}, u32[]{:S(2)}, u32[]{:S(2)}) collective-permute-start(bf16[200,128]{1,0:T(8,128)(2,1)S(1)} %shard_map.140), channel_id=1, source_target_pairs={{0,240},{16,32},{32,16},{48,64},{64,48},{80,96},{96,80},{112,128},... | collective-permute-start | bytes 153608 | tf_op jit(solution)/shard_map/ppermute | solution.py:473
  53.6 11.7 %collective-permute-start.10 = (bf16[200,128]{1,0:T(8,128)(2,1)S(1)}, bf16[200,128]{1,0:T(8,128)(2,1)S(1)}, u32[]{:S(2)}, u32[]{:S(2)}) collective-permute-start(bf16[200,128]{1,0:T(8,128)(2,1)S(1)} %shard_map.140), channel_id=1, source_target_pairs={{0,16},{16,0},{32,48},{48,32},{64,80},{80,64},{96,112},{112,96},{1... | collective-permute-start | bytes 153608 | tf_op jit(solution)/shard_map/ppermute | solution.py:474
  58.7 16.5 %all-to-all-start.1 = ((bf16[16,64,256]{2,1,0:T(8,128)(2,1)}), bf16[16,64,256]{2,1,0:T(8,128)(2,1)S(1)}, u32[]{:S(2)}, u32[]{:S(2)}) async-start(bf16[16,64,256]{2,1,0:T(8,128)(2,1)} %shard_map.145), calls=%async_computation.1 | async-start | bytes 1048576 | tf_op jit(solution)/shard_map/all_to_all | solution.py:602
